TPU v7x, 32 devices: a whole 2x2x4 slice. The times are simulated.
32 devices in a mesh: dp: 4 (over y, x), seq: 8 (over z, core).
Axes of the slice: x: 2, y: 2, z: 4, core: 2. Of those that a mesh axis runs over, the one named last changes fastest.
Arguments:
- frames_in: bfloat16 [8, 16, 144, 1152], P('dp', 'seq'), may hold values from -36 to 36
- modulation: float32 [8, 6, 1152], P('dp'), may hold values from -3 to 3
- spatial_qkv: bfloat16 [1152, 3456], replicated, may hold values from -0.8249579 to 0.8249579
- spatial_out: bfloat16 [1152, 1152], replicated, may hold values from -0.1875 to 0.1875
- temporal_qkv: bfloat16 [1152, 3456], replicated, may hold values from -0.8249579 to 0.8249579
- temporal_out: bfloat16 [1152, 1152], replicated, may hold values from -0.1875 to 0.1875
- cotangent: bfloat16 [8, 16, 144, 1152], P('dp', 'seq'), may hold values from -6 to 6
Outputs:
- block_out: bfloat16 [8, 16, 144, 1152], P('dp', 'seq')
- grad_input: bfloat16 [8, 16, 144, 1152], P('dp', 'seq')
- grad_spatial_qkv: bfloat16 [1152, 3456], P(('dp', 'seq'))
- grad_spatial_out: bfloat16 [1152, 1152], P(('dp', 'seq'))
- grad_temporal_qkv: bfloat16 [1152, 3456], P(('dp', 'seq'))
- grad_temporal_out: bfloat16 [1152, 1152], P(('dp', 'seq'))
All inputs are finite; a program needn't handle non-finite values.
Results may differ from a plain program's by a relative error of at most 0.02.
Values may be sent and summed in bfloat16 or wider, within the bound.
No kernel may reach another device: no remote copies, remote signals or barrier semaphores. Data moves between devices by JAX's collectives and lax.ppermute only.
A program may use at most 192 MiB of HBM per device.

v0:
```python
import functools

import jax
import jax.numpy as jnp
import numpy as np
from jax import lax
from jax.experimental import pallas as pl
from jax.experimental.pallas import tpu as pltpu
from jax.sharding import PartitionSpec as P

HEADS = 16
NORM_EPSILON = 1e-06
MASKED = -1e30
LOG2_E = 1.4426950408889634
MIB = 1024 * 1024
F32 = jnp.float32
BF16 = jnp.bfloat16

NN = (((1,), (0,)), ((), ()))
NT = (((1,), (1,)), ((), ()))
TN = (((0,), (0,)), ((), ()))


def dot(left, right, dims=NN):
    return lax.dot_general(left, right, dims, preferred_element_type=F32)


ROOM = {
    "split": 56, "space_forward": 56, "time": 56, "weights": 56, "space_backward": 56,
    "grad_input": 56, "stage": 16, "core_stage": 16, "assemble": 16, "join": 56,
}
SPACES = {"v": pltpu.VMEM, "s": pltpu.SMEM, "a": pl.ANY}


def call(name, us, body, ins, out_shape, outs, scratch=()):
    def run(*operands, deps=()):
        return pl.pallas_call(
            body,
            out_shape=out_shape,
            in_specs=[pl.BlockSpec(memory_space=SPACES[s]) for s in ins + "a" * len(deps)],
            out_specs=(
                tuple(pl.BlockSpec(memory_space=SPACES[s]) for s in outs)
                if isinstance(out_shape, tuple)
                else pl.BlockSpec(memory_space=SPACES[outs])
            ),
            scratch_shapes=list(scratch),
            compiler_params=pltpu.CompilerParams(vmem_limit_bytes=ROOM[name] * MIB),
            cost_estimate=pl.CostEstimate(
                flops=int(us * 1e9), transcendentals=0, bytes_accessed=int(us * 1e6)
            ),
            name=name,
        )(*operands, *deps)

    return run


def shaped(*shape, dtype=BF16):
    return jax.ShapeDtypeStruct(shape, dtype)


def norm_stats(values):
    mean = jnp.mean(values, -1, keepdims=True)
    centred = values - mean
    inverse = lax.rsqrt(jnp.mean(centred * centred, -1, keepdims=True) + NORM_EPSILON)
    return centred * inverse, inverse


def norm_backward(d_modded, normed, inverse, scale):
    e = d_modded * (1.0 + scale)
    return inverse * (
        e
        - jnp.mean(e, -1, keepdims=True)
        - normed * jnp.mean(e * normed, -1, keepdims=True)
    )


def pair_windows(width):
    size = 2 * width // HEADS
    found = []
    for pair in range(HEADS // 2):
        start = pair * size // 128 * 128
        offset = pair * size - start
        found.append((start, 128 * pl.cdiv(offset + size, 128), offset))
    return found


def pair_masks(rows, span, offset, size):
    lane = lax.broadcasted_iota(jnp.int32, (rows, span), 1)
    first = (lane >= offset) & (lane < offset + size)
    both = (lane >= offset) & (lane < offset + 2 * size)
    return first, both


def two_heads(values, first, both):
    zero = jnp.zeros_like(values)
    return jnp.concatenate(
        [jnp.where(first, values, zero), jnp.where(both & ~first, values, zero)], 0
    )


def per_query(by_key, other, first):
    out = dot(by_key, other, TN)
    rows = out.shape[0] // 2
    return jnp.where(first, out[:rows], out[rows:])


def probs_by_key(queries, key, factor, keep):
    scores = dot(key, queries, NT)
    if keep is not None:
        scores = jnp.where(keep, scores, MASKED)
    raised = jnp.exp2((scores - jnp.max(scores, 0, keepdims=True)) * (factor * LOG2_E))
    return raised * (1.0 / jnp.sum(raised, 0, keepdims=True))


def put(ref, rows, start, both, value):
    at = (pl.ds(rows, both.shape[0]), pl.ds(start, both.shape[1]))
    ref[at] = jnp.where(both, value.astype(BF16), ref[at])


def frame_rows(pieces):
    n, rows, width = pieces.shape
    return pieces.astype(F32).reshape(n * rows, width).astype(BF16)


def piece_rows(values, n):
    return values.reshape(n, values.shape[0] // n, values.shape[1]).astype(BF16)


def same_video(rows, frames):
    left = lax.broadcasted_iota(jnp.int32, (rows, 2 * rows), 0) // frames
    column = lax.broadcasted_iota(jnp.int32, (rows, 2 * rows), 1)
    right = jnp.where(column >= rows, column - rows, column) // frames
    return left == right


class Copies:
    def __init__(self, sems):
        self.sems, self.used = sems, 0

    def start(self, source, target):
        copy = pltpu.make_async_copy(source, target, self.sems.at[self.used])
        self.used += 1
        copy.start()
        return copy


def qkv_loads(copies, wqkv_ref, wqkv, width):
    parts = [pl.ds(part * width, width) for part in range(3)]
    return [copies.start(wqkv_ref.at[:, at], wqkv.at[:, at]) for at in parts]


def project_qkv(modded, wqkv, loads, packed, width):
    for part, load in enumerate(loads):
        load.wait()
        at = pl.ds(part * width, width)
        packed[:, at] = dot(modded, wqkv[:, at]).astype(BF16)


def split_kernel(n, x_ref, scatter_ref, out_ref):
    out_ref[...] = piece_rows(dot(scatter_ref[...], x_ref[0]), n)


def join_kernel(pieces_ref, gather_ref, *refs):
    out_ref = refs[-1]
    rows = dot(gather_ref[...], frame_rows(pieces_ref[...])).astype(BF16)
    out_ref[...] = rows.reshape(out_ref.shape)


def space_forward_kernel(
    n, block, video, x_ref, cot_ref, mod_ref, wqkv_ref, wout_ref, scatter_ref, scatter_cot_ref, *refs
):
    sent_ref, packed_out, modded_out, attended_out, weights_out = refs[-14:-9]
    x, cot, modded, packed, attended, weights, wqkv, wout, sems = refs[-9:]
    width = x.shape[1]
    size = width // HEADS
    factor = size ** (-0.5)
    copies = Copies(sems)
    load_x = copies.start(x_ref.at[video], x)
    load_qkv = qkv_loads(copies, wqkv_ref, wqkv, width)
    load_out = copies.start(wout_ref, wout)
    if video:
        load_cot = copies.start(cot_ref.at[video], cot)
    load_x.wait()
    normed, _ = norm_stats(x[...].astype(F32))
    modded[...] = (normed * (1.0 + mod_ref[video, 1:2, :]) + mod_ref[video, 0:1, :]).astype(BF16)
    stores = [copies.start(modded, modded_out)]
    project_qkv(modded[...], wqkv, load_qkv, packed, width)
    stores.append(copies.start(packed, packed_out))
    pairs = pair_windows(width)

    def one_block(g, carry):
        rows = pl.multiple_of(g * block, 16)
        for pair, (start, span, offset) in enumerate(pairs):
            first, both = pair_masks(block, span, offset, size)
            at = pl.ds(rows, block)
            query = packed[at, pl.ds(start, span)]
            key = packed[at, pl.ds(width + start, span)]
            value = packed[at, pl.ds(2 * width + start, span)]
            probs = probs_by_key(two_heads(query, first, both), key, factor, None).astype(BF16)
            weights[g * len(pairs) + pair] = probs
            put(attended, rows, start, both, per_query(probs, value, first))
        return carry

    lax.fori_loop(0, x.shape[0] // block, one_block, 0)
    stores.append(copies.start(attended, attended_out))
    stores.append(copies.start(weights, weights_out))
    load_out.wait()
    projected = dot(attended[...], wout[...])
    middle = (x[...].astype(F32) + mod_ref[video, 2:3, :] * projected).astype(BF16)
    pieces = dot(scatter_ref[...], middle)
    if video:
        load_cot.wait()
        pieces += dot(scatter_cot_ref[...], cot[...])
    sent_ref[...] = piece_rows(pieces, n)
    for store in stores:
        store.wait()


def unit_stores(copies, core, width, left, right, outs):
    *sent_outs, right_out = outs
    other = (1 - core) * (2 * width)
    sources = [left.at[:, pl.ds(unit * width, width)] for unit in range(2)]
    sources += [
        right.at[:, pl.ds(pl.multiple_of(other + unit * width, 128), width)] for unit in range(2)
    ]
    return [copies.start(source, out) for source, out in zip(sources, sent_outs)] + [
        copies.start(right, right_out)
    ]


def time_kernel(
    n, block, frames, video, core_ref, middle_ref, cot_ref, mod_ref, wqkv_ref, wout_ref,
    gather_ref, gather_cot_ref, scatter_ref, scatter_out_ref, others_ref, *refs
):
    (d_middle_ref, block_out_ref, *unit_outs), scratch = refs[-17:-10], refs[-10:]
    normed, x, up, left, packed, d_out, right, wqkv, wout, sems = scratch
    width = x.shape[1]
    size = width // HEADS
    factor = size ** (-0.5)
    copies = Copies(sems)
    load_qkv = qkv_loads(copies, wqkv_ref, wqkv, width)
    load_out = copies.start(wout_ref, wout)
    x[...] = dot(gather_ref[...], frame_rows(middle_ref[...])).astype(BF16)
    up[...] = dot(gather_cot_ref[...], frame_rows(cot_ref[...])).astype(BF16)
    normed_now, inverse = norm_stats(x[...].astype(F32))
    normed[...] = normed_now
    left[:, 0:width] = (
        normed_now * (1.0 + mod_ref[video, 4:5, :]) + mod_ref[video, 3:4, :]
    ).astype(BF16)
    right[:, 3 * width :] = (mod_ref[video, 5:6, :] * up[...].astype(F32)).astype(BF16)
    project_qkv(left[:, 0:width], wqkv, load_qkv, packed, width)
    load_out.wait()
    d_out[...] = dot(right[:, 3 * width :], wout[...], NT).astype(BF16)
    keep = same_video(block, frames)

    def one_block(g, carry):
        rows = pl.multiple_of(g * block, 16)
        for start, span, offset in pair_windows(width):
            first, both = pair_masks(block, span, offset, size)
            at = pl.ds(rows, block)
            query = two_heads(packed[at, pl.ds(start, span)], first, both)
            key = packed[at, pl.ds(width + start, span)]
            value = packed[at, pl.ds(2 * width + start, span)]
            d_rows = two_heads(d_out[at, pl.ds(start, span)], first, both)
            probs = probs_by_key(query, key, factor, keep)
            weights = probs.astype(BF16)
            put(left, rows, width + start, both, per_query(weights, value, first))
            d_probs = dot(value, d_rows, NT)
            total = jnp.sum(probs * d_probs, 0, keepdims=True)
            d_scores = (probs * (d_probs - total) * factor).astype(BF16)
            put(right, rows, start, both, per_query(d_scores, key, first))
            put(right, rows, width + start, both, dot(d_scores, query))
            put(right, rows, 2 * width + start, both, dot(weights, d_rows))
        return carry

    lax.fori_loop(0, x.shape[0] // block, one_block, 0)
    stores = unit_stores(copies, core_ref[1] & 1, width, left, right, unit_outs)
    d_modded = dot(right[:, 0 : 3 * width], wqkv[...], NT)
    d_middle = up[...].astype(F32) + norm_backward(
        d_modded, normed[...], inverse, mod_ref[video, 4:5, :]
    )
    d_middle_ref[...] = piece_rows(dot(scatter_ref[...], d_middle.astype(BF16)), n)
    projected = dot(left[:, width:], wout[...])
    out = (x[...].astype(F32) + mod_ref[video, 5:6, :] * projected).astype(BF16)
    pieces = dot(scatter_out_ref[...], out)
    if video:
        pieces += others_ref[...].astype(F32).reshape(pieces.shape)
    block_out_ref[...] = piece_rows(pieces, n)
    for store in stores:
        store.wait()


def space_backward_kernel(
    block, video, core_ref, up_ref, mod_ref, wout_ref, gather_ref, packed_ref, modded_ref,
    attended_ref, weights_ref, *refs
):
    d_middle_ref, *unit_outs = refs[-12:-6]
    d_out, left, right, packed, wout, sems = refs[-6:]
    width = wout.shape[0]
    size = width // HEADS
    factor = size ** (-0.5)
    copies = Copies(sems)
    load_out = copies.start(wout_ref, wout)
    load_packed = copies.start(packed_ref, packed)
    loads = [
        copies.start(modded_ref, left.at[:, pl.ds(0, width)]),
        copies.start(attended_ref, left.at[:, pl.ds(width, width)]),
    ]
    up = dot(gather_ref[...], frame_rows(up_ref[...]))
    d_middle_ref[...] = up.astype(BF16)
    right[:, 3 * width :] = (mod_ref[video, 2:3, :] * up).astype(BF16)
    load_out.wait()
    d_out[...] = dot(right[:, 3 * width :], wout[...], NT).astype(BF16)
    load_packed.wait()
    pairs = pair_windows(width)

    def one_block(g, carry):
        rows = pl.multiple_of(g * block, 16)
        for pair, (start, span, offset) in enumerate(pairs):
            first, both = pair_masks(block, span, offset, size)
            at = pl.ds(rows, block)
            query = two_heads(packed[at, pl.ds(start, span)], first, both)
            key = packed[at, pl.ds(width + start, span)]
            value = packed[at, pl.ds(2 * width + start, span)]
            d_rows = two_heads(d_out[at, pl.ds(start, span)], first, both)
            weights = weights_ref[g * len(pairs) + pair]
            probs = weights.astype(F32)
            d_probs = dot(value, d_rows, NT)
            total = jnp.sum(probs * d_probs, 0, keepdims=True) / jnp.sum(probs, 0, keepdims=True)
            d_scores = (probs * (d_probs - total) * factor).astype(BF16)
            put(right, rows, start, both, per_query(d_scores, key, first))
            put(right, rows, width + start, both, dot(d_scores, query))
            put(right, rows, 2 * width + start, both, dot(weights, d_rows))
        return carry

    lax.fori_loop(0, d_out.shape[0] // block, one_block, 0)
    for load in loads:
        load.wait()
    for store in unit_stores(copies, core_ref[1] & 1, width, left, right, unit_outs):
        store.wait()


def grad_input_kernel(video, right_ref, d_middle_ref, x_ref, mod_ref, wqkv_ref, *refs):
    out_ref, d_packed, wqkv, sems = refs[-4:]
    width = out_ref.shape[1]
    copies = Copies(sems)
    parts = [pl.ds(part * width, width) for part in range(3)]
    loads = [
        (copies.start(right_ref.at[:, at], d_packed.at[:, at]),
         copies.start(wqkv_ref.at[:, at], wqkv.at[:, at]))
        for at in parts
    ]
    normed, inverse = norm_stats(x_ref[video].astype(F32))
    d_modded = 0.0
    for at, load in zip(parts, loads):
        for one in load:
            one.wait()
        d_modded += dot(d_packed[:, at], wqkv[:, at], NT)
    d_tokens = norm_backward(d_modded, normed, inverse, mod_ref[video, 1:2, :])
    out_ref[...] = (d_middle_ref[...].astype(F32) + d_tokens).astype(BF16)


def bit_of(place_ref, axis, bit):
    return (place_ref[0 if axis == "dp" else 1] >> bit) & 1


def emit_halves(rows, inner, mine, kept_ref, sent_ref):
    for outer in range(kept_ref.shape[0]):
        low = rows[2 * outer * inner : (2 * outer + 1) * inner, :]
        high = rows[(2 * outer + 1) * inner : (2 * outer + 2) * inner, :]
        kept_ref[outer] = jnp.where(mine == 0, low, high).astype(BF16)
        sent_ref[outer] = jnp.where(mine == 0, high, low).astype(BF16)


def weight_kernel(videos, cuts, steps, grad_scale, place_ref, *refs):
    right, units = refs[:videos], refs[videos : 9 * videos]
    sent = [units[4 * v : 4 * v + 4] for v in range(videos)]
    got = [units[4 * v : 4 * v + 4] for v in range(videos, 2 * videos)]
    count = 2 * len(cuts)
    outs, scratch = refs[-4 - 2 * count : -4 - count], refs[-4 - count : -4]
    left_rows, right_rows, total, sems = refs[-4:]
    width = left_rows.shape[1] // 2
    tokens = right[0].shape[0]
    copies = Copies(sems)
    core = place_ref[1] & 1
    own = pl.multiple_of(core * (2 * width), 128)
    waits = []
    for unit in range(2):
        now = []
        for video in range(videos):
            for place, (left, mine) in enumerate(((sent[video], right[video]), (got[video], None))):
                rows = pl.ds((2 * video + place) * tokens, tokens)
                at = pl.ds(unit * width, width)
                now.append(copies.start(left[unit], left_rows.at[rows, at]))
                source = (
                    left[2 + unit]
                    if mine is None
                    else mine.at[:, pl.ds(pl.multiple_of(own + unit * width, 128), width)]
                )
                now.append(copies.start(source, right_rows.at[rows, at]))
        waits.append(now)
    done, stores = 0, []
    for part, ((low, high), (axis, bit, inner)) in enumerate(zip(cuts, steps)):
        for unit in range(2):
            start, stop = max(low, unit * width), min(high, (unit + 1) * width)
            if start >= stop:
                continue
            while done <= unit:
                for wait in waits[done]:
                    wait.wait()
                done += 1
            column = pl.multiple_of(core * width, 128) if unit else 0
            left = left_rows[:, pl.ds(column, width)]
            total[:, start - low : stop - low] = (
                dot(left, right_rows[:, start:stop], TN) * grad_scale
            )
        pair = slice(2 * part, 2 * part + 2)
        emit_halves(total, inner, bit_of(place_ref, axis, bit), *scratch[pair])
        stores += [copies.start(a, b) for a, b in zip(scratch[pair], outs[pair])]
    for store in stores:
        store.wait()


def stage_kernel(steps, place_ref, *refs):
    count = len(steps)
    total, outs = refs[-1], refs[-1 - 2 * count : -1]
    for part, (axis, bit, inner) in enumerate(steps):
        kept, got = refs[part], refs[count + part]
        each = kept.shape[1]
        for outer in range(kept.shape[0]):
            total[outer * each : (outer + 1) * each, :] = kept[outer].astype(F32) + got[
                outer
            ].astype(F32)
        emit_halves(
            total, inner, bit_of(place_ref, axis, bit), outs[2 * part], outs[2 * part + 1]
        )


def core_stage_kernel(count, place_ref, *refs):
    kept_out, sent_out = refs[-2:]
    rows, columns = refs[0].shape[1:]
    core = place_ref[1] & 1
    for part in range(count):
        total = refs[part][0].astype(F32) + refs[count + part][0].astype(F32)
        low, high = total[: rows // 2], total[rows // 2 :]
        at = slice(part * columns, (part + 1) * columns)
        kept_out[:, at] = jnp.where(core == 0, low, high).astype(BF16)
        sent_out[:, at] = jnp.where(core == 0, high, low).astype(BF16)


def assemble_kernel(place_ref, kept_ref, got_ref, qkv_ref, out_ref):
    width = out_ref.shape[1]
    core = place_ref[1] & 1
    kept, got = kept_ref[...].astype(F32), got_ref[...].astype(F32)
    low = jnp.where(core == 0, kept, got).astype(BF16)
    high = jnp.where(core == 0, got, kept).astype(BF16)
    qkv_ref[:, : 2 * width] = low
    qkv_ref[:, 2 * width :] = high[:, :width]
    out_ref[...] = high[:, width:]


def swap(x, axis, mask):
    size = lax.axis_size(axis)
    return lax.ppermute(x, axis, [(i, i ^ mask) for i in range(size)])


class Reduction:
    def __init__(self, place, width, late):
        dp_bits = [("dp", bit) for bit in range(lax.axis_size("dp").bit_length() - 1)]
        seq_bits = [("seq", bit) for bit in range(1, lax.axis_size("seq").bit_length() - 1)]
        if late:
            self.orders = (
                dp_bits + seq_bits,
                dp_bits[-1:] + seq_bits[:1] + dp_bits[:-1] + seq_bits[1:],
                seq_bits[:1] + dp_bits + seq_bits[1:],
            )
        else:
            self.orders = (dp_bits + seq_bits, dp_bits[::-1] + seq_bits)
        self.parts = len(self.orders)
        self.place, self.width, self.columns = place, width, 2 * width // self.parts
        self.cuts = tuple(
            (part * self.columns, (part + 1) * self.columns) for part in range(self.parts)
        )
        self.bits = dp_bits[::-1] + seq_bits[::-1]
        self.step = 0

    def next_steps(self):
        least = self.width >> len(self.bits)
        steps, shapes = [], []
        for order in self.orders:
            left = [bit for bit in self.bits if bit not in order[: self.step]]
            above = left.index(order[self.step])
            inner = least << (len(left) - above - 1)
            steps.append((*order[self.step], inner))
            shapes += 2 * [shaped(1 << above, inner, self.columns)]
        return tuple(steps), tuple(shapes)

    def send(self, halves):
        self.kept = halves[0::2]
        self.got = [
            swap(half, order[self.step][0], 1 << order[self.step][1])
            for half, order in zip(halves[1::2], self.orders)
        ]
        self.step += 1

    def stage(self, deps=()):
        steps, shapes = self.next_steps()
        halves = call(
            "stage", 2, functools.partial(stage_kernel, steps), "s" + "v" * len(shapes), shapes,
            "v" * len(shapes),
            [pltpu.VMEM((self.width >> self.step, self.columns), F32)],
        )(self.place, *self.kept, *self.got, deps=deps)
        self.send(halves)
        return halves[0]

    def core_stage(self, deps=()):
        while self.step < len(self.bits):
            self.stage()
        rows = self.width >> (len(self.bits) + 1)
        half = shaped(rows, 2 * self.width)
        self.mine, sent = call(
            "core_stage", 1, functools.partial(core_stage_kernel, self.parts),
            "s" + "v" * (2 * self.parts), (half, half), "vv",
        )(self.place, *self.kept, *self.got, deps=deps)
        self.other = swap(sent, "seq", 1)
        return self.mine

    def finish(self):
        rows = self.mine.shape[0]
        return call(
            "assemble", 1, assemble_kernel, "svv",
            (shaped(rows, 3 * self.width), shaped(rows, self.width)), "vv",
        )(self.place, self.mine, self.other)


def shards(frames_in, modulation, spatial_qkv, spatial_out, temporal_qkv, temporal_out, cotangent):
    n = lax.axis_size("seq")
    videos, frames, patches, width = frames_in.shape
    all_frames = frames * n
    tokens = frames * patches
    own_patches = patches // n
    rows = frames * own_patches
    padded = -(-rows // 8) * 8
    time_block = 6 * all_frames if own_patches % 6 == 0 else 3 * all_frames
    core = jnp.stack([lax.axis_index("dp"), lax.axis_index("seq")]).astype(jnp.int32)

    joint_padded = -(-videos * rows // 8) * 8
    to_pieces = np.zeros((n * padded, tokens), np.float32)
    to_joint = np.zeros((videos, n * joint_padded, tokens), np.float32)
    by_patch = np.zeros((tokens, n * padded), np.float32)
    joint_by_patch = np.zeros((videos, tokens, n * joint_padded), np.float32)
    for device in range(n):
        for f in range(frames):
            for p in range(own_patches):
                inside = f * own_patches + p
                before = f * patches + device * own_patches + p
                after = p * all_frames + device * frames + f
                to_pieces[device * padded + inside, before] = 1
                by_patch[after, device * padded + inside] = 1
                for v in range(videos):
                    place = device * joint_padded + v * rows + inside
                    to_joint[v, place, before] = 1
                    joint_by_patch[v, after, place] = 1
    from_joint = jnp.asarray(np.concatenate(list(to_joint), 1).T, BF16)
    to_pieces, from_pieces = jnp.asarray(to_pieces, BF16), jnp.asarray(to_pieces.T, BF16)
    to_joint = [jnp.asarray(m, BF16) for m in to_joint]
    by_patch, from_patch = jnp.asarray(by_patch, BF16), jnp.asarray(by_patch.T, BF16)
    joint_from_patch = [jnp.asarray(m.T, BF16) for m in joint_by_patch]
    joint_by_patch = [jnp.asarray(m, BF16) for m in joint_by_patch]

    def exchange(pieces):
        return lax.all_to_all(pieces, "seq", split_axis=0, concat_axis=0, tiled=True)

    piece = shaped(n, padded, width)
    joint_piece = shaped(n, joint_padded, width)
    row = shaped(tokens, width)
    three, four = shaped(tokens, 3 * width), shaped(tokens, 4 * width)
    all_rows = shaped(videos, tokens, width)
    weights_shape = (frames * (HEADS // 2), patches, 2 * patches)

    def vmem(*shape, dtype=BF16):
        return pltpu.VMEM(shape, dtype)

    def sems(count):
        return pltpu.SemaphoreType.DMA((count,))

    weight_refs = [vmem(width, 3 * width), vmem(width, width)]
    x = frames_in.reshape(videos, tokens, width)
    cot = cotangent.reshape(videos, tokens, width)

    cot_sent = call("split", 3, functools.partial(split_kernel, n), "vv", piece, "v")(
        cot, to_pieces
    )
    cot_pieces = exchange(cot_sent)
    deps = [cot_sent]
    saved, arrived = [], []
    for v in range(videos):
        sent, *keep = call(
            "space_forward", 14, functools.partial(space_forward_kernel, n, patches, v),
            "aavaavv",
            (joint_piece if v else piece, three, row, row, shaped(*weights_shape)),
            "vaaaa",
            [
                vmem(tokens, width), vmem(tokens, width), vmem(tokens, width),
                vmem(tokens, 3 * width), vmem(tokens, width), vmem(*weights_shape),
                *weight_refs, sems(10),
            ],
        )(
            x, cot, modulation, spatial_qkv, spatial_out, to_joint[0] if v else to_pieces,
            to_joint[1], deps=deps,
        )
        deps = [keep[0], cot_pieces]
        arrived.append(exchange(sent))
        saved.append(keep)

    def exchange_units(sent):
        return [swap(unit, "seq", 1) for unit in sent]

    returned, time_units, out_sent = [], [], core
    for v in range(videos):
        d_middle, out_sent, *sent, right = call(
            "time", 25, functools.partial(time_kernel, n, time_block, all_frames, v),
            "svvvaavvvv" + ("v" if v else "a"),
            (piece, joint_piece) + 4 * (row,) + (four,),
            "vvaaaaa",
            [
                vmem(tokens, width, dtype=F32), vmem(tokens, width), vmem(tokens, width),
                vmem(tokens, 2 * width), vmem(tokens, 3 * width), vmem(tokens, width),
                vmem(tokens, 4 * width), *weight_refs, sems(9),
            ],
        )(
            core, arrived[v], arrived[v] if v else cot_pieces, modulation, temporal_qkv,
            temporal_out, joint_by_patch[0] if v else by_patch,
            joint_by_patch[1] if v else by_patch, from_patch, joint_from_patch[v], out_sent,
            deps=deps,
        )
        deps = [right]
        returned.append(exchange(d_middle))
        time_units.append((sent, right, exchange_units(sent)))

    grad_scale = (videos * lax.axis_size("dp") * all_frames * patches) ** (-0.5)

    def weights(units, late, deps=()):
        reduction = Reduction(core, width, late)
        steps, shapes = reduction.next_steps()
        sent, right, got = zip(*units)
        halves = call(
            "weights", 10,
            functools.partial(weight_kernel, videos, reduction.cuts, steps, grad_scale),
            "s" + "a" * (9 * videos), shapes, "a" * len(shapes),
            [vmem(*half.shape) for half in shapes] + [
                vmem(2 * videos * tokens, 2 * width), vmem(2 * videos * tokens, 2 * width),
                vmem(width, reduction.columns, dtype=F32), sems(8 * videos + len(shapes)),
            ],
        )(core, *right, *sum(sent, []), *sum(got, []), deps=deps)
        reduction.send(halves)
        return reduction, halves[0]

    def grad_of(video, units, d_middle, deps=()):
        return call(
            "grad_input", 8, functools.partial(grad_input_kernel, video), "avvva", row, "v",
            [vmem(tokens, 3 * width), vmem(width, 3 * width), sems(6)],
        )(units[1], d_middle, x, modulation, spatial_qkv, deps=deps)

    d_middles, space_units, grad_input = [], [], []
    for v in range(videos):
        d_middle, *sent, right = call(
            "space_backward", 15, functools.partial(space_backward_kernel, patches, v),
            "svvavaaav",
            (row,) + 4 * (row,) + (four,),
            "vaaaaa",
            [
                vmem(tokens, width), vmem(tokens, 2 * width), vmem(tokens, 4 * width),
                vmem(tokens, 3 * width), vmem(width, width), sems(9),
            ],
        )(
            core, returned[v], modulation, spatial_out, from_pieces, *saved[v], deps=deps
        )
        if v == 0:
            time_sum, began = weights(time_units, False, deps=[right])
            deps = [began]
            out_back = exchange(out_sent)
        d_middles.append(d_middle)
        space_units.append((sent, right, exchange_units(sent)))
    grad_input.append(grad_of(0, space_units[0], d_middles[0], deps=[right]))
    began = time_sum.stage(deps=grad_input)
    space_sum, began = weights(space_units, True, deps=[began])
    began = time_sum.stage(deps=[began, out_back])
    for v in range(1, videos):
        grad_input.append(grad_of(v, space_units[v], d_middles[v], deps=[began]))
    began = time_sum.stage(deps=[grad_input[-1]])
    began = space_sum.stage(deps=[began])
    block_out = call("join", 4, join_kernel, "vv", all_rows, "v")(
        out_back, from_joint, deps=[began]
    )
    space_sum.stage(deps=[block_out, time_sum.core_stage(deps=[began])])
    space_sum.core_stage()
    grad_input = jnp.stack(grad_input)
    grad_time, grad_space = time_sum.finish(), space_sum.finish()
    return (
        block_out.reshape(frames_in.shape), grad_input.reshape(frames_in.shape),
        *grad_space, *grad_time,
    )


def solution(mesh):
    return jax.shard_map(
        shards,
        mesh=mesh,
        in_specs=(
            P("dp", "seq", None, None),
            P("dp", None, None),
            P(),
            P(),
            P(),
            P(),
            P("dp", "seq", None, None),
        ),
        out_specs=(
            P("dp", "seq", None, None),
            P("dp", "seq", None, None),
            P(("dp", "seq"), None),
            P(("dp", "seq"), None),
            P(("dp", "seq"), None),
            P(("dp", "seq"), None),
        ),
        check_vma=False,
    )
```

profile of v0, /device:TPU:0, one launch (start us, length us, event | category | flops | bytes accessed | tf_op | source)
XLA Modules:
  0.0 316.6 jit_solution(237540748184746675)
XLA Ops:
  0.6 2.8 split.1.refs_0_
  3.4 6.5 %all-to-all-start = ((bf16[8,40,1152]{2,1,0:T(8,128)(2,1)}), bf16[8,40,1152]{2,1,0:T(8,128)(2,1)S(1)}, u32[]{:S(2)}, u32[]{:S(2)}) async-start(bf16[8,40,1152]{2,1,0:T(8,128)(2,1)} %split.1.refs_0_), calls=%async_computation | async-start | bytes 1474560 | tf_op jit(solution)/shard_map/all_to_all | solution.py:572
  11.1 14.4 %space_forward.2 = (bf16[8,40,1152]{2,1,0:T(8,128)(2,1)}, bf16[288,3456]{1,0:T(8,128)(2,1)}, bf16[288,1152]{1,0:T(8,128)(2,1)}, bf16[288,1152]{1,0:T(8,128)(2,1)}, bf16[16,144,288]{2,1,0:T(8,128)(2,1)}) custom-call(bf16[2,288,1152]{2,1,0:T(8,128)(2,1)} %bitcast.13, bf16[2,288,1152]{2,1,0:T(8,128)(2,1)} %bitcast.11, f32[2,6,1152]{2,1,0:T(8,128)} %copy.25.mod_ref, ...), custom_call_target="tpu_custom_call" | custom-call | flops 14000000000 | bytes 14000000 | tf_op jit(solution)/shard_map/space_forward/pallas_call | solution.py:37
  25.5 4.2 %all-to-all-done.refs_1_.cot_ref = bf16[8,40,1152]{2,1,0:T(8,128)(2,1)S(1)} async-done(((bf16[8,40,1152]{2,1,0:T(8,128)(2,1)}), bf16[8,40,1152]{2,1,0:T(8,128)(2,1)S(1)}, u32[]{:S(2)}, u32[]{:S(2)}) %all-to-all-start) | async-done | bytes 737312 | tf_op jit(solution)/shard_map/all_to_all | solution.py:572
  29.8 3.8 %all-to-all-start.2 = ((bf16[8,40,1152]{2,1,0:T(8,128)(2,1)}), bf16[8,40,1152]{2,1,0:T(8,128)(2,1)S(1)}, u32[]{:S(2)}, u32[]{:S(2)}) async-start(bf16[8,40,1152]{2,1,0:T(8,128)(2,1)} %get-tuple-element.92), calls=%async_computation.2 | async-start | bytes 1474560 | tf_op jit(solution)/shard_map/all_to_all | solution.py:572
  33.6 16.2 %space_forward.3 = (bf16[8,72,1152]{2,1,0:T(8,128)(2,1)}, bf16[288,3456]{1,0:T(8,128)(2,1)}, bf16[288,1152]{1,0:T(8,128)(2,1)}, bf16[288,1152]{1,0:T(8,128)(2,1)}, bf16[16,144,288]{2,1,0:T(8,128)(2,1)}) custom-call(bf16[2,288,1152]{2,1,0:T(8,128)(2,1)} %bitcast.14, bf16[2,288,1152]{2,1,0:T(8,128)(2,1)} %bitcast.12, f32[2,6,1152]{2,1,0:T(8,128)} %copy.25.mod_ref, ...), custom_call_target="tpu_custom_call" | custom-call | flops 14000000000 | bytes 14000000 | tf_op jit(solution)/shard_map/space_forward/pallas_call | solution.py:37
  49.8 3.6 %all-to-all-done.2.middle_ref = bf16[8,40,1152]{2,1,0:T(8,128)(2,1)S(1)} async-done(((bf16[8,40,1152]{2,1,0:T(8,128)(2,1)}), bf16[8,40,1152]{2,1,0:T(8,128)(2,1)S(1)}, u32[]{:S(2)}, u32[]{:S(2)}) %all-to-all-start.2) | async-done | bytes 737312 | tf_op jit(solution)/shard_map/all_to_all | solution.py:572
  54.3 4.1 %all-to-all-start.1 = ((bf16[8,72,1152]{2,1,0:T(8,128)(2,1)}), bf16[8,72,1152]{2,1,0:T(8,128)(2,1)S(1)}, u32[]{:S(2)}, u32[]{:S(2)}) async-start(bf16[8,72,1152]{2,1,0:T(8,128)(2,1)} %get-tuple-element.91), calls=%async_computation.1 | async-start | bytes 2654208 | tf_op jit(solution)/shard_map/all_to_all | solution.py:572
  58.4 25.6 %time.2 = (bf16[8,40,1152]{2,1,0:T(8,128)(2,1)}, bf16[8,72,1152]{2,1,0:T(8,128)(2,1)}, bf16[288,1152]{1,0:T(8,128)(2,1)}, bf16[288,1152]{1,0:T(8,128)(2,1)}, bf1...) custom-call(s32[2]{0:T(128)} %pad_add_fusion.core_ref.others_ref.place_ref, ...), custom_call_target="tpu_custom_call" | custom-call | flops 24999999488 | bytes 25000000 | tf_op jit(solution)/shard_map/time/pallas_call | solution.py:37
  85.1 5.8 %all-to-all-done.1.middle_ref.cot_ref = bf16[8,72,1152]{2,1,0:T(8,128)(2,1)S(1)} async-done(((bf16[8,72,1152]{2,1,0:T(8,128)(2,1)}), bf16[8,72,1152]{2,1,0:T(8,128)(2,1)S(1)}, u32[]{:S(2)}, u32[]{:S(2)}) %all-to-all-start.1) | async-done | bytes 1327136 | tf_op jit(solution)/shard_map/all_to_all | solution.py:572
  90.9 3.7 %all-to-all-start.4 = ((bf16[8,40,1152]{2,1,0:T(8,128)(2,1)}), bf16[8,40,1152]{2,1,0:T(8,128)(2,1)S(1)}, u32[]{:S(2)}, u32[]{:S(2)}) async-start(bf16[8,40,1152]{2,1,0:T(8,128)(2,1)} %get-tuple-element.97), calls=%async_computation.4 | async-start | bytes 1474560 | tf_op jit(solution)/shard_map/all_to_all | solution.py:572
  94.7 26.4 %time.3 = (bf16[8,40,1152]{2,1,0:T(8,128)(2,1)}, bf16[8,72,1152]{2,1,0:T(8,128)(2,1)}, bf16[288,1152]{1,0:T(8,128)(2,1)}, bf16[288,1152]{1,0:T(8,128)(2,1)}, bf1...) custom-call(s32[2]{0:T(128)} %pad_add_fusion.core_ref.others_ref.place_ref, ...), custom_call_target="tpu_custom_call" | custom-call | flops 24999999488 | bytes 25000000 | tf_op jit(solution)/shard_map/time/pallas_call | solution.py:37
  121.6 5.2 %all-to-all-start.5 = ((bf16[8,40,1152]{2,1,0:T(8,128)(2,1)}), bf16[8,40,1152]{2,1,0:T(8,128)(2,1)S(1)}, u32[]{:S(2)}, u32[]{:S(2)}) async-start(bf16[8,40,1152]{2,1,0:T(8,128)(2,1)} %get-tuple-element.103), calls=%async_computation.5 | async-start | bytes 1474560 | tf_op jit(solution)/shard_map/all_to_all | solution.py:572
  128.0 14.1 %space_backward.2 = (bf16[288,1152]{1,0:T(8,128)(2,1)}, bf16[288,1152]{1,0:T(8,128)(2,1)}, bf16[288,1152]{1,0:T(8,128)(2,1)}, bf16[288,1152]{1,0:T(8,128)(2,1)},...) custom-call(s32[2]{0:T(128)} %pad_add_fusion.core_ref.others_ref.place_ref, bf16[8,40,1152]{2,1,0:T(8,128)(2,1)} %copy-done.24, ...), custom_call_target="tpu_custom_call" | custom-call | flops 15000000512 | bytes 15000000 | tf_op jit(solution)/shard_map/space_backward/pallas_call | solution.py:37
  144.0 14.3 %weights.2 = (bf16[2,288,1152]{2,1,0:T(8,128)(2,1)}, bf16[2,288,1152]{2,1,0:T(8,128)(2,1)}, bf16[1,576,1152]{2,1,0:T(8,128)(2,1)}, bf16[1,576,1152]{2,1,0:T(8,128)(2,1)}) custom-call(s32[2]{0:T(128)} %pad_add_fusion.core_ref.others_ref.place_ref, bf16[288,4608]{1,0:T(8,128)(2,1)} %get-tuple-element.95.refs_0_, ...), custom_call_target="tpu_custom_call" | custom-call | flops 10000000000 | bytes 10000000 | tf_op jit(solution)/shard_map/weights/pallas_call | solution.py:37
  158.2 1.6 collective-permute-start.16
  159.8 1.5 collective-permute-start.17
  162.2 4.9 %all-to-all-start.3 = ((bf16[8,72,1152]{2,1,0:T(8,128)(2,1)}), bf16[8,72,1152]{2,1,0:T(8,128)(2,1)S(1)}, u32[]{:S(2)}, u32[]{:S(2)}) async-start(bf16[8,72,1152]{2,1,0:T(8,128)(2,1)} %get-tuple-element.96), calls=%async_computation.3 | async-start | bytes 2654208 | tf_op jit(solution)/shard_map/all_to_all | solution.py:572
  167.2 14.3 %space_backward.3 = (bf16[288,1152]{1,0:T(8,128)(2,1)}, bf16[288,1152]{1,0:T(8,128)(2,1)}, bf16[288,1152]{1,0:T(8,128)(2,1)}, bf16[288,1152]{1,0:T(8,128)(2,1)},...) custom-call(s32[2]{0:T(128)} %pad_add_fusion.core_ref.others_ref.place_ref, bf16[8,40,1152]{2,1,0:T(8,128)(2,1)} %copy-done.23, ...), custom_call_target="tpu_custom_call" | custom-call | flops 15000000512 | bytes 15000000 | tf_op jit(solution)/shard_map/space_backward/pallas_call | solution.py:37
  182.6 7.3 %collective-permute-done.16.refs_2_ = bf16[2,288,1152]{2,1,0:T(8,128)(2,1)S(1)} collective-permute-done((bf16[2,288,1152]{2,1,0:T(8,128)(2,1)}, bf16[2,288,1152]{2,1,0:T(8,128)(2,1)S(1)}, u32[]{:S(2)}, u32[]{:S(2)}) %collective-permute-start.16) | collective-permute-done | bytes 1327136 | tf_op jit(solution)/shard_map/ppermute | solution.py:464
  191.2 9.3 %grad_input.2.refs_4_ = bf16[288,1152]{1,0:T(8,128)(2,1)} custom-call(bf16[288,4608]{1,0:T(8,128)(2,1)} %get-tuple-element.102.refs_18_.right_ref.refs_0_, bf16[288,1152]{1,0:T(8,128)(2,1)} %get-tuple-element.128.d_middle_ref, bf16[2,288,1152]{2,1,0:T(8,128)(2,1)} %bitcast.15, f32[2,6,1152]{2,1,0:T(8,128)} %copy.25.mod_ref, bf16[1152,3456]{1,0:T(8,128)(2,1)} %wqkv_ref.11, ...), custom_call_target="tpu_custom_call" | custom-call | flops 8000000000 | bytes 8000000 | tf_op jit(solution)/shard_map/grad_input/pallas_call | solution.py:37
  201.7 3.1 stage.6
  206.4 1.5 collective-permute-start.21
  208.7 15.5 %weights.3 = (bf16[2,288,768]{2,1,0:T(8,128)(2,1)}, bf16[2,288,768]{2,1,0:T(8,128)(2,1)}, bf16[1,576,768]{2,1,0:T(8,128)(2,1)}, bf16[1,576,768]{2,1,0:T(8,128)(2...) custom-call(s32[2]{0:T(128)} %pad_add_fusion.core_ref.others_ref.place_ref, ...), custom_call_target="tpu_custom_call" | custom-call | flops 10000000000 | bytes 10000000 | tf_op jit(solution)/shard_map/weights/pallas_call | solution.py:37
  224.2 1.4 collective-permute-start.18
  226.1 1.7 collective-permute-start.20
  227.9 1.6 copy-done.11
  231.7 1.8 stage.7
  234.5 1.7 collective-permute-start.24
  236.2 9.2 %grad_input.3.refs_4_ = bf16[288,1152]{1,0:T(8,128)(2,1)} custom-call(bf16[288,4608]{1,0:T(8,128)(2,1)} %get-tuple-element.116.refs_0_.refs_1_.right_ref, bf16[288,1152]{1,0:T(8,128)(2,1)} %get-tuple-element.143.d_middle_ref, bf16[2,288,1152]{2,1,0:T(8,128)(2,1)} %bitcast.16, f32[2,6,1152]{2,1,0:T(8,128)} %copy.25.mod_ref, bf16[1152,3456]{1,0:T(8,128)(2,1)} %wqkv_ref.11, ...), custom_call_target="tpu_custom_call" | custom-call | flops 8000000000 | bytes 8000000 | tf_op jit(solution)/shard_map/grad_input/pallas_call | solution.py:37
  245.5 10.5 %collective-permute-done.23.refs_2_ = bf16[2,72,1152]{2,1,0:T(8,128)(2,1)S(1)} collective-permute-done((bf16[2,72,1152]{2,1,0:T(8,128)(2,1)S(1)}, bf16[2,72,1152]{2,1,0:T(8,128)(2,1)S(1)}, u32[]{:S(2)}, u32[]{:S(2)}) %collective-permute-start.23) | collective-permute-done | bytes 331808 | tf_op jit(solution)/shard_map/ppermute | solution.py:464
  256.0 5.5 %collective-permute-done.24.refs_3_ = bf16[2,72,1152]{2,1,0:T(8,128)(2,1)S(1)} collective-permute-done((bf16[2,72,1152]{2,1,0:T(8,128)(2,1)S(1)}, bf16[2,72,1152]{2,1,0:T(8,128)(2,1)S(1)}, u32[]{:S(2)}, u32[]{:S(2)}) %collective-permute-start.24) | collective-permute-done | bytes 331808 | tf_op jit(solution)/shard_map/ppermute | solution.py:464
  264.3 2.0 stage.9
  267.1 1.5 collective-permute-start.25
  268.6 1.7 collective-permute-start.26
  270.9 2.4 collective-permute-start.28
  273.8 3.9 %join.1.refs_6_ = bf16[2,288,1152]{2,1,0:T(8,128)(2,1)} custom-call(bf16[8,72,1152]{2,1,0:T(8,128)(2,1)} %copy-done, bf16[576,576]{1,0:T(8,128)(2,1)} %constant.30.clone.gather_ref, bf16[1,288,768]{2,1,0:T(8,128)(2,1)} %copy-done.18), custom_call_target="tpu_custom_call" | custom-call | flops 4000000000 | bytes 4000000 | tf_op jit(solution)/shard_map/join/pallas_call | solution.py:37
  277.7 5.8 %collective-permute-done.28.refs_2_ = bf16[1,72,1152]{2,1,0:T(8,128)(2,1)S(1)} collective-permute-done((bf16[1,72,1152]{2,1,0:T(8,128)(2,1)S(1)}, bf16[1,72,1152]{2,1,0:T(8,128)(2,1)S(1)}, u32[]{:S(2)}, u32[]{:S(2)}) %collective-permute-start.28) | collective-permute-done | bytes 165920 | tf_op jit(solution)/shard_map/ppermute | solution.py:464
  283.5 1.8 collective-permute-done.29.refs_3_
  287.5 3.4 %collective-permute-start.30 = (bf16[2,72,768]{2,1,0:T(8,128)(2,1)S(1)}, bf16[2,72,768]{2,1,0:T(8,128)(2,1)S(1)}, u32[]{:S(2)}, u32[]{:S(2)}) collective-permute-start(bf16[2,72,768]{2,1,0:T(8,128)(2,1)S(1)} %get-tuple-element.158), channel_id=1, source_target_pairs={{0,2},{1,3},{2,0},{3,1},{4,6},{5,7},{6,4},{7,5},{8,10},{9,11},{10,... | collective-permute-start | bytes 663560 | tf_op jit(solution)/shard_map/ppermute | solution.py:464
  291.9 3.0 collective-permute-done.30.refs_3_
  294.9 2.0 collective-permute-done.31.refs_4_
  298.0 1.8 collective-permute-start.33
  301.0 1.7 collective-permute-start.35
  302.7 5.4 %collective-permute-done.33.refs_3_ = bf16[1,72,768]{2,1,0:T(8,128)(2,1)S(1)} collective-permute-done((bf16[1,72,768]{2,1,0:T(8,128)(2,1)S(1)}, bf16[1,72,768]{2,1,0:T(8,128)(2,1)S(1)}, u32[]{:S(2)}, u32[]{:S(2)}) %collective-permute-start.33) | collective-permute-done | bytes 110624 | tf_op jit(solution)/shard_map/ppermute | solution.py:464
  308.2 1.8 collective-permute-done.34.refs_4_
  313.6 1.3 assemble.3
  315.0 1.3 assemble.2
  (131 shorter events, 31.1 us)
Async XLA Ops:
  3.4 26.4 %all-to-all-start = ((bf16[8,40,1152]{2,1,0:T(8,128)(2,1)}), bf16[8,40,1152]{2,1,0:T(8,128)(2,1)S(1)}, u32[]{:S(2)}, u32[]{:S(2)}) async-start(bf16[8,40,1152]{2,1,0:T(8,128)(2,1)} %split.1.refs_0_), calls=%async_computation | async-start | bytes 1474560 | tf_op jit(solution)/shard_map/all_to_all | solution.py:572
  29.8 23.7 %all-to-all-start.2 = ((bf16[8,40,1152]{2,1,0:T(8,128)(2,1)}), bf16[8,40,1152]{2,1,0:T(8,128)(2,1)S(1)}, u32[]{:S(2)}, u32[]{:S(2)}) async-start(bf16[8,40,1152]{2,1,0:T(8,128)(2,1)} %get-tuple-element.92), calls=%async_computation.2 | async-start | bytes 1474560 | tf_op jit(solution)/shard_map/all_to_all | solution.py:572
  54.3 36.6 %all-to-all-start.1 = ((bf16[8,72,1152]{2,1,0:T(8,128)(2,1)}), bf16[8,72,1152]{2,1,0:T(8,128)(2,1)S(1)}, u32[]{:S(2)}, u32[]{:S(2)}) async-start(bf16[8,72,1152]{2,1,0:T(8,128)(2,1)} %get-tuple-element.91), calls=%async_computation.1 | async-start | bytes 2654208 | tf_op jit(solution)/shard_map/all_to_all | solution.py:572
  84.0 42.8 %collective-permute-start = (bf16[288,1152]{1,0:T(8,128)(2,1)}, bf16[288,1152]{1,0:T(8,128)(2,1)S(1)}, u32[]{:S(2)}, u32[]{:S(2)}) collective-permute-start(bf16[288,1152]{1,0:T(8,128)(2,1)} %get-tuple-element.107.refs_2_), channel_id=1, source_target_pairs={{0,1},{1,0},{2,3},{3,2},{4,5},{5,4},{6,7},{7,6},{8,9},{9,8},{10,11... | collective-permute-start | bytes 1990664 | tf_op jit(solution)/shard_map/ppermute | solution.py:464
  84.5 42.9 %collective-permute-start.1 = (bf16[288,1152]{1,0:T(8,128)(2,1)}, bf16[288,1152]{1,0:T(8,128)(2,1)S(1)}, u32[]{:S(2)}, u32[]{:S(2)}) collective-permute-start(bf16[288,1152]{1,0:T(8,128)(2,1)} %get-tuple-element.108.refs_3_), channel_id=1, source_target_pairs={{0,1},{1,0},{2,3},{3,2},{4,5},{5,4},{6,7},{7,6},{8,9},{9,8},{10,11... | collective-permute-start | bytes 1990664 | tf_op jit(solution)/shard_map/ppermute | solution.py:464
  84.6 42.9 %collective-permute-start.2 = (bf16[288,1152]{1,0:T(8,128)(2,1)}, bf16[288,1152]{1,0:T(8,128)(2,1)}, u32[]{:S(2)}, u32[]{:S(2)}) collective-permute-start(bf16[288,1152]{1,0:T(8,128)(2,1)} %get-tuple-element.109.refs_4_), channel_id=1, source_target_pairs={{0,1},{1,0},{2,3},{3,2},{4,5},{5,4},{6,7},{7,6},{8,9},{9,8},{10,11... | collective-permute-start | bytes 1990664 | tf_op jit(solution)/shard_map/ppermute | solution.py:464
  85.0 57.0 %collective-permute-start.3 = (bf16[288,1152]{1,0:T(8,128)(2,1)}, bf16[288,1152]{1,0:T(8,128)(2,1)}, u32[]{:S(2)}, u32[]{:S(2)}) collective-permute-start(bf16[288,1152]{1,0:T(8,128)(2,1)} %get-tuple-element.110.refs_5_), channel_id=1, source_target_pairs={{0,1},{1,0},{2,3},{3,2},{4,5},{5,4},{6,7},{7,6},{8,9},{9,8},{10,11... | collective-permute-start | bytes 1990664 | tf_op jit(solution)/shard_map/ppermute | solution.py:464
  90.9 30.7 %all-to-all-start.4 = ((bf16[8,40,1152]{2,1,0:T(8,128)(2,1)}), bf16[8,40,1152]{2,1,0:T(8,128)(2,1)S(1)}, u32[]{:S(2)}, u32[]{:S(2)}) async-start(bf16[8,40,1152]{2,1,0:T(8,128)(2,1)} %get-tuple-element.97), calls=%async_computation.4 | async-start | bytes 1474560 | tf_op jit(solution)/shard_map/all_to_all | solution.py:572
  121.1 21.2 %collective-permute-start.4 = (bf16[288,1152]{1,0:T(8,128)(2,1)}, bf16[288,1152]{1,0:T(8,128)(2,1)}, u32[]{:S(2)}, u32[]{:S(2)}) collective-permute-start(bf16[288,1152]{1,0:T(8,128)(2,1)} %get-tuple-element.111.refs_6_), channel_id=1, source_target_pairs={{0,1},{1,0},{2,3},{3,2},{4,5},{5,4},{6,7},{7,6},{8,9},{9,8},{10,11... | collective-permute-start | bytes 1990664 | tf_op jit(solution)/shard_map/ppermute | solution.py:464
  121.6 39.7 %all-to-all-start.5 = ((bf16[8,40,1152]{2,1,0:T(8,128)(2,1)}), bf16[8,40,1152]{2,1,0:T(8,128)(2,1)S(1)}, u32[]{:S(2)}, u32[]{:S(2)}) async-start(bf16[8,40,1152]{2,1,0:T(8,128)(2,1)} %get-tuple-element.103), calls=%async_computation.5 | async-start | bytes 1474560 | tf_op jit(solution)/shard_map/all_to_all | solution.py:572
  126.9 15.2 %copy-start.28 = (bf16[288,1152]{1,0:T(8,128)(2,1)}, bf16[288,1152]{1,0:T(8,128)(2,1)S(1)}, u32[]{:S(2)}) copy-start(bf16[288,1152]{1,0:T(8,128)(2,1)S(1)} %collective-permute-done.refs_10_) | copy-start | bytes 1990660
  126.9 15.8 %collective-permute-start.5 = (bf16[288,1152]{1,0:T(8,128)(2,1)}, bf16[288,1152]{1,0:T(8,128)(2,1)S(1)}, u32[]{:S(2)}, u32[]{:S(2)}) collective-permute-start(bf16[288,1152]{1,0:T(8,128)(2,1)} %get-tuple-element.112.refs_7_), channel_id=1, source_target_pairs={{0,1},{1,0},{2,3},{3,2},{4,5},{5,4},{6,7},{7,6},{8,9},{9,8},{10,11... | collective-permute-start | bytes 1990664 | tf_op jit(solution)/shard_map/ppermute | solution.py:464
  127.4 14.6 %copy-start.29 = (bf16[288,1152]{1,0:T(8,128)(2,1)}, bf16[288,1152]{1,0:T(8,128)(2,1)S(1)}, u32[]{:S(2)}) copy-start(bf16[288,1152]{1,0:T(8,128)(2,1)S(1)} %collective-permute-done.1.refs_11_) | copy-start | bytes 1990660
  127.4 15.3 %collective-permute-start.6 = (bf16[288,1152]{1,0:T(8,128)(2,1)}, bf16[288,1152]{1,0:T(8,128)(2,1)S(1)}, u32[]{:S(2)}, u32[]{:S(2)}) collective-permute-start(bf16[288,1152]{1,0:T(8,128)(2,1)} %get-tuple-element.113.refs_8_), channel_id=1, source_target_pairs={{0,1},{1,0},{2,3},{3,2},{4,5},{5,4},{6,7},{7,6},{8,9},{9,8},{10,11... | collective-permute-start | bytes 1990664 | tf_op jit(solution)/shard_map/ppermute | solution.py:464
  127.5 15.2 %collective-permute-start.7 = (bf16[288,1152]{1,0:T(8,128)(2,1)}, bf16[288,1152]{1,0:T(8,128)(2,1)S(1)}, u32[]{:S(2)}, u32[]{:S(2)}) collective-permute-start(bf16[288,1152]{1,0:T(8,128)(2,1)} %get-tuple-element.114.refs_9_), channel_id=1, source_target_pairs={{0,1},{1,0},{2,3},{3,2},{4,5},{5,4},{6,7},{7,6},{8,9},{9,8},{10,11... | collective-permute-start | bytes 1990664 | tf_op jit(solution)/shard_map/ppermute | solution.py:464
  142.1 39.4 %collective-permute-start.8 = (bf16[288,1152]{1,0:T(8,128)(2,1)}, bf16[288,1152]{1,0:T(8,128)(2,1)}, u32[]{:S(2)}, u32[]{:S(2)}) collective-permute-start(bf16[288,1152]{1,0:T(8,128)(2,1)} %get-tuple-element.117.refs_2_), channel_id=1, source_target_pairs={{0,1},{1,0},{2,3},{3,2},{4,5},{5,4},{6,7},{7,6},{8,9},{9,8},{10,11... | collective-permute-start | bytes 1990664 | tf_op jit(solution)/shard_map/ppermute | solution.py:464
  142.3 39.8 %collective-permute-start.9 = (bf16[288,1152]{1,0:T(8,128)(2,1)}, bf16[288,1152]{1,0:T(8,128)(2,1)}, u32[]{:S(2)}, u32[]{:S(2)}) collective-permute-start(bf16[288,1152]{1,0:T(8,128)(2,1)} %get-tuple-element.118.refs_3_), channel_id=1, source_target_pairs={{0,1},{1,0},{2,3},{3,2},{4,5},{5,4},{6,7},{7,6},{8,9},{9,8},{10,11... | collective-permute-start | bytes 1990664 | tf_op jit(solution)/shard_map/ppermute | solution.py:464
  142.7 39.5 %collective-permute-start.10 = (bf16[288,1152]{1,0:T(8,128)(2,1)}, bf16[288,1152]{1,0:T(8,128)(2,1)}, u32[]{:S(2)}, u32[]{:S(2)}) collective-permute-start(bf16[288,1152]{1,0:T(8,128)(2,1)} %get-tuple-element.119.refs_4_), channel_id=1, source_target_pairs={{0,1},{1,0},{2,3},{3,2},{4,5},{5,4},{6,7},{7,6},{8,9},{9,8},{10,11... | collective-permute-start | bytes 1990664 | tf_op jit(solution)/shard_map/ppermute | solution.py:464
  158.2 31.6 %collective-permute-start.16 = (bf16[2,288,1152]{2,1,0:T(8,128)(2,1)}, bf16[2,288,1152]{2,1,0:T(8,128)(2,1)S(1)}, u32[]{:S(2)}, u32[]{:S(2)}) collective-permute-start(bf16[2,288,1152]{2,1,0:T(8,128)(2,1)} %get-tuple-element.126), channel_id=1, source_target_pairs={{0,8},{8,0},{16,24},{24,16},{1,9},{9,1},{17,25},{25,17},{2,10},{10... | collective-permute-start | bytes 3981320 | tf_op jit(solution)/shard_map/ppermute | solution.py:464
  159.8 31.4 %collective-permute-start.17 = (bf16[1,576,1152]{2,1,0:T(8,128)(2,1)}, bf16[1,576,1152]{2,1,0:T(8,128)(2,1)}, u32[]{:S(2)}, u32[]{:S(2)}) collective-permute-start(bf16[1,576,1152]{2,1,0:T(8,128)(2,1)} %get-tuple-element.127), channel_id=1, source_target_pairs={{0,16},{8,24},{16,0},{24,8},{1,17},{9,25},{17,1},{25,9},{2,18},{10... | collective-permute-start | bytes 3981320 | tf_op jit(solution)/shard_map/ppermute | solution.py:464
  162.2 65.6 %all-to-all-start.3 = ((bf16[8,72,1152]{2,1,0:T(8,128)(2,1)}), bf16[8,72,1152]{2,1,0:T(8,128)(2,1)S(1)}, u32[]{:S(2)}, u32[]{:S(2)}) async-start(bf16[8,72,1152]{2,1,0:T(8,128)(2,1)} %get-tuple-element.96), calls=%async_computation.3 | async-start | bytes 2654208 | tf_op jit(solution)/shard_map/all_to_all | solution.py:572
  181.5 25.0 %collective-permute-start.11 = (bf16[288,1152]{1,0:T(8,128)(2,1)}, bf16[288,1152]{1,0:T(8,128)(2,1)}, u32[]{:S(2)}, u32[]{:S(2)}) collective-permute-start(bf16[288,1152]{1,0:T(8,128)(2,1)} %get-tuple-element.120.refs_5_), channel_id=1, source_target_pairs={{0,1},{1,0},{2,3},{3,2},{4,5},{5,4},{6,7},{7,6},{8,9},{9,8},{10,11... | collective-permute-start | bytes 1990664 | tf_op jit(solution)/shard_map/ppermute | solution.py:464
  182.1 25.9 %collective-permute-start.12 = (bf16[288,1152]{1,0:T(8,128)(2,1)}, bf16[288,1152]{1,0:T(8,128)(2,1)}, u32[]{:S(2)}, u32[]{:S(2)}) collective-permute-start(bf16[288,1152]{1,0:T(8,128)(2,1)} %get-tuple-element.121.refs_6_), channel_id=1, source_target_pairs={{0,1},{1,0},{2,3},{3,2},{4,5},{5,4},{6,7},{7,6},{8,9},{9,8},{10,11... | collective-permute-start | bytes 1990664 | tf_op jit(solution)/shard_map/ppermute | solution.py:464
  182.2 26.5 %collective-permute-start.13 = (bf16[288,1152]{1,0:T(8,128)(2,1)}, bf16[288,1152]{1,0:T(8,128)(2,1)}, u32[]{:S(2)}, u32[]{:S(2)}) collective-permute-start(bf16[288,1152]{1,0:T(8,128)(2,1)} %get-tuple-element.122.refs_7_), channel_id=1, source_target_pairs={{0,1},{1,0},{2,3},{3,2},{4,5},{5,4},{6,7},{7,6},{8,9},{9,8},{10,11... | collective-permute-start | bytes 1990664 | tf_op jit(solution)/shard_map/ppermute | solution.py:464
  189.9 18.8 %collective-permute-start.14 = (bf16[288,1152]{1,0:T(8,128)(2,1)}, bf16[288,1152]{1,0:T(8,128)(2,1)}, u32[]{:S(2)}, u32[]{:S(2)}) collective-permute-start(bf16[288,1152]{1,0:T(8,128)(2,1)} %get-tuple-element.123.refs_8_), channel_id=1, source_target_pairs={{0,1},{1,0},{2,3},{3,2},{4,5},{5,4},{6,7},{7,6},{8,9},{9,8},{10,11... | collective-permute-start | bytes 1990664 | tf_op jit(solution)/shard_map/ppermute | solution.py:464
  191.2 17.5 %collective-permute-start.15 = (bf16[288,1152]{1,0:T(8,128)(2,1)}, bf16[288,1152]{1,0:T(8,128)(2,1)}, u32[]{:S(2)}, u32[]{:S(2)}) collective-permute-start(bf16[288,1152]{1,0:T(8,128)(2,1)} %get-tuple-element.124.refs_9_), channel_id=1, source_target_pairs={{0,1},{1,0},{2,3},{3,2},{4,5},{5,4},{6,7},{7,6},{8,9},{9,8},{10,11... | collective-permute-start | bytes 1990664 | tf_op jit(solution)/shard_map/ppermute | solution.py:464
  206.4 21.4 %collective-permute-start.21 = (bf16[1,288,1152]{2,1,0:T(8,128)(2,1)}, bf16[1,288,1152]{2,1,0:T(8,128)(2,1)}, u32[]{:S(2)}, u32[]{:S(2)}) collective-permute-start(bf16[1,288,1152]{2,1,0:T(8,128)(2,1)} %get-tuple-element.137), channel_id=1, source_target_pairs={{0,16},{8,24},{16,0},{24,8},{1,17},{9,25},{17,1},{25,9},{2,18},{10... | collective-permute-start | bytes 1990664 | tf_op jit(solution)/shard_map/ppermute | solution.py:464
  208.0 19.9 %collective-permute-start.22 = (bf16[1,288,1152]{2,1,0:T(8,128)(2,1)}, bf16[1,288,1152]{2,1,0:T(8,128)(2,1)}, u32[]{:S(2)}, u32[]{:S(2)}) collective-permute-start(bf16[1,288,1152]{2,1,0:T(8,128)(2,1)} %get-tuple-element.138), channel_id=1, source_target_pairs={{0,8},{8,0},{16,24},{24,16},{1,9},{9,1},{17,25},{25,17},{2,10},{10... | collective-permute-start | bytes 1990664 | tf_op jit(solution)/shard_map/ppermute | solution.py:464
  208.7 19.2 %copy-start.7 = (s32[2]{0:T(128)S(1)}, s32[2]{0:T(128)}, u32[]{:S(2)}) copy-start(s32[2]{0:T(128)} %pad_add_fusion.core_ref.others_ref.place_ref) | copy-start | bytes 28
  224.2 39.2 %collective-permute-start.18 = (bf16[2,288,768]{2,1,0:T(8,128)(2,1)}, bf16[2,288,768]{2,1,0:T(8,128)(2,1)S(1)}, u32[]{:S(2)}, u32[]{:S(2)}) collective-permute-start(bf16[2,288,768]{2,1,0:T(8,128)(2,1)} %get-tuple-element.133), channel_id=1, source_target_pairs={{0,8},{8,0},{16,24},{24,16},{1,9},{9,1},{17,25},{25,17},{2,10},{10... | collective-permute-start | bytes 2654216 | tf_op jit(solution)/shard_map/ppermute | solution.py:464
  225.6 37.8 %collective-permute-start.19 = (bf16[1,576,768]{2,1,0:T(8,128)(2,1)}, bf16[1,576,768]{2,1,0:T(8,128)(2,1)S(1)}, u32[]{:S(2)}, u32[]{:S(2)}) collective-permute-start(bf16[1,576,768]{2,1,0:T(8,128)(2,1)} %get-tuple-element.134), channel_id=1, source_target_pairs={{0,16},{8,24},{16,0},{24,8},{1,17},{9,25},{17,1},{25,9},{2,18},{10... | collective-permute-start | bytes 2654216 | tf_op jit(solution)/shard_map/ppermute | solution.py:464
  226.1 37.3 %collective-permute-start.20 = (bf16[8,72,768]{2,1,0:T(8,128)(2,1)}, bf16[8,72,768]{2,1,0:T(8,128)(2,1)}, u32[]{:S(2)}, u32[]{:S(2)}) collective-permute-start(bf16[8,72,768]{2,1,0:T(8,128)(2,1)} %get-tuple-element.135), channel_id=1, source_target_pairs={{0,2},{1,3},{2,0},{3,1},{4,6},{5,7},{6,4},{7,5},{8,10},{9,11},{10,... | collective-permute-start | bytes 2654216 | tf_op jit(solution)/shard_map/ppermute | solution.py:464
  234.2 21.8 %collective-permute-start.23 = (bf16[2,72,1152]{2,1,0:T(8,128)(2,1)S(1)}, bf16[2,72,1152]{2,1,0:T(8,128)(2,1)S(1)}, u32[]{:S(2)}, u32[]{:S(2)}) collective-permute-start(bf16[2,72,1152]{2,1,0:T(8,128)(2,1)S(1)} %get-tuple-element.141), channel_id=1, source_target_pairs={{0,2},{1,3},{2,0},{3,1},{4,6},{5,7},{6,4},{7,5},{8,10},{9,11},{10,... | collective-permute-start | bytes 995336 | tf_op jit(solution)/shard_map/ppermute | solution.py:464
  234.5 27.0 %collective-permute-start.24 = (bf16[2,72,1152]{2,1,0:T(8,128)(2,1)S(1)}, bf16[2,72,1152]{2,1,0:T(8,128)(2,1)S(1)}, u32[]{:S(2)}, u32[]{:S(2)}) collective-permute-start(bf16[2,72,1152]{2,1,0:T(8,128)(2,1)S(1)} %get-tuple-element.142), channel_id=1, source_target_pairs={{0,2},{1,3},{2,0},{3,1},{4,6},{5,7},{6,4},{7,5},{8,10},{9,11},{10,... | collective-permute-start | bytes 995336 | tf_op jit(solution)/shard_map/ppermute | solution.py:464
  236.2 25.3 %copy-start.21 = (bf16[2,72,1152]{2,1,0:T(8,128)(2,1)S(1)}, bf16[2,72,1152]{2,1,0:T(8,128)(2,1)}, u32[]{:S(2)}) copy-start(bf16[2,72,1152]{2,1,0:T(8,128)(2,1)} %copy-done.20) | copy-start | bytes 995332
  267.1 18.9 %collective-permute-start.25 = (bf16[1,288,768]{2,1,0:T(8,128)(2,1)S(1)}, bf16[1,288,768]{2,1,0:T(8,128)(2,1)S(1)}, u32[]{:S(2)}, u32[]{:S(2)}) collective-permute-start(bf16[1,288,768]{2,1,0:T(8,128)(2,1)S(1)} %get-tuple-element.148), channel_id=1, source_target_pairs={{0,16},{8,24},{16,0},{24,8},{1,17},{9,25},{17,1},{25,9},{2,18},{10... | collective-permute-start | bytes 1327112 | tf_op jit(solution)/shard_map/ppermute | solution.py:464
  268.6 17.4 %collective-permute-start.26 = (bf16[4,72,768]{2,1,0:T(8,128)(2,1)S(1)}, bf16[4,72,768]{2,1,0:T(8,128)(2,1)S(1)}, u32[]{:S(2)}, u32[]{:S(2)}) collective-permute-start(bf16[4,72,768]{2,1,0:T(8,128)(2,1)S(1)} %get-tuple-element.149), channel_id=1, source_target_pairs={{0,2},{1,3},{2,0},{3,1},{4,6},{5,7},{6,4},{7,5},{8,10},{9,11},{10,... | collective-permute-start | bytes 1327112 | tf_op jit(solution)/shard_map/ppermute | solution.py:464
  270.3 15.7 %collective-permute-start.27 = (bf16[2,144,768]{2,1,0:T(8,128)(2,1)S(1)}, bf16[2,144,768]{2,1,0:T(8,128)(2,1)S(1)}, u32[]{:S(2)}, u32[]{:S(2)}) collective-permute-start(bf16[2,144,768]{2,1,0:T(8,128)(2,1)S(1)} %get-tuple-element.150), channel_id=1, source_target_pairs={{0,8},{8,0},{16,24},{24,16},{1,9},{9,1},{17,25},{25,17},{2,10},{10... | collective-permute-start | bytes 1327112 | tf_op jit(solution)/shard_map/ppermute | solution.py:464
  270.9 12.6 %collective-permute-start.28 = (bf16[1,72,1152]{2,1,0:T(8,128)(2,1)S(1)}, bf16[1,72,1152]{2,1,0:T(8,128)(2,1)S(1)}, u32[]{:S(2)}, u32[]{:S(2)}) collective-permute-start(bf16[1,72,1152]{2,1,0:T(8,128)(2,1)S(1)} %get-tuple-element.152), channel_id=1, source_target_pairs={{0,4},{1,5},{2,6},{3,7},{4,0},{5,1},{6,2},{7,3},{8,12},{9,13},{10,... | collective-permute-start | bytes 497672 | tf_op jit(solution)/shard_map/ppermute | solution.py:464
  273.2 12.0 %collective-permute-start.29 = (bf16[1,72,1152]{2,1,0:T(8,128)(2,1)S(1)}, bf16[1,72,1152]{2,1,0:T(8,128)(2,1)S(1)}, u32[]{:S(2)}, u32[]{:S(2)}) collective-permute-start(bf16[1,72,1152]{2,1,0:T(8,128)(2,1)S(1)} %get-tuple-element.153), channel_id=1, source_target_pairs={{0,4},{1,5},{2,6},{3,7},{4,0},{5,1},{6,2},{7,3},{8,12},{9,13},{10,... | collective-permute-start | bytes 497672 | tf_op jit(solution)/shard_map/ppermute | solution.py:464
  287.5 7.4 %collective-permute-start.30 = (bf16[2,72,768]{2,1,0:T(8,128)(2,1)S(1)}, bf16[2,72,768]{2,1,0:T(8,128)(2,1)S(1)}, u32[]{:S(2)}, u32[]{:S(2)}) collective-permute-start(bf16[2,72,768]{2,1,0:T(8,128)(2,1)S(1)} %get-tuple-element.158), channel_id=1, source_target_pairs={{0,2},{1,3},{2,0},{3,1},{4,6},{5,7},{6,4},{7,5},{8,10},{9,11},{10,... | collective-permute-start | bytes 663560 | tf_op jit(solution)/shard_map/ppermute | solution.py:464
  291.0 5.9 %collective-permute-start.31 = (bf16[1,144,768]{2,1,0:T(8,128)(2,1)S(1)}, bf16[1,144,768]{2,1,0:T(8,128)(2,1)S(1)}, u32[]{:S(2)}, u32[]{:S(2)}) collective-permute-start(bf16[1,144,768]{2,1,0:T(8,128)(2,1)S(1)} %get-tuple-element.159), channel_id=1, source_target_pairs={{0,8},{8,0},{16,24},{24,16},{1,9},{9,1},{17,25},{25,17},{2,10},{10... | collective-permute-start | bytes 663560 | tf_op jit(solution)/shard_map/ppermute | solution.py:464
  291.4 5.9 %collective-permute-start.32 = (bf16[1,144,768]{2,1,0:T(8,128)(2,1)S(1)}, bf16[1,144,768]{2,1,0:T(8,128)(2,1)S(1)}, u32[]{:S(2)}, u32[]{:S(2)}) collective-permute-start(bf16[1,144,768]{2,1,0:T(8,128)(2,1)S(1)} %get-tuple-element.160), channel_id=1, source_target_pairs={{0,16},{8,24},{16,0},{24,8},{1,17},{9,25},{17,1},{25,9},{2,18},{10... | collective-permute-start | bytes 663560 | tf_op jit(solution)/shard_map/ppermute | solution.py:464
  298.0 10.1 %collective-permute-start.33 = (bf16[1,72,768]{2,1,0:T(8,128)(2,1)S(1)}, bf16[1,72,768]{2,1,0:T(8,128)(2,1)S(1)}, u32[]{:S(2)}, u32[]{:S(2)}) collective-permute-start(bf16[1,72,768]{2,1,0:T(8,128)(2,1)S(1)} %get-tuple-element.164), channel_id=1, source_target_pairs={{0,4},{1,5},{2,6},{3,7},{4,0},{5,1},{6,2},{7,3},{8,12},{9,13},{10,... | collective-permute-start | bytes 331784 | tf_op jit(solution)/shard_map/ppermute | solution.py:464
  299.8 10.2 %collective-permute-start.34 = (bf16[1,72,768]{2,1,0:T(8,128)(2,1)S(1)}, bf16[1,72,768]{2,1,0:T(8,128)(2,1)S(1)}, u32[]{:S(2)}, u32[]{:S(2)}) collective-permute-start(bf16[1,72,768]{2,1,0:T(8,128)(2,1)S(1)} %get-tuple-element.165), channel_id=1, source_target_pairs={{0,4},{1,5},{2,6},{3,7},{4,0},{5,1},{6,2},{7,3},{8,12},{9,13},{10,... | collective-permute-start | bytes 331784 | tf_op jit(solution)/shard_map/ppermute | solution.py:464
  301.0 10.1 %collective-permute-start.35 = (bf16[1,72,768]{2,1,0:T(8,128)(2,1)S(1)}, bf16[1,72,768]{2,1,0:T(8,128)(2,1)S(1)}, u32[]{:S(2)}, u32[]{:S(2)}) collective-permute-start(bf16[1,72,768]{2,1,0:T(8,128)(2,1)S(1)} %get-tuple-element.166), channel_id=1, source_target_pairs={{0,4},{1,5},{2,6},{3,7},{4,0},{5,1},{6,2},{7,3},{8,12},{9,13},{10,... | collective-permute-start | bytes 331784 | tf_op jit(solution)/shard_map/ppermute | solution.py:464
  302.7 10.9 %collective-permute-start.37 = (bf16[36,2304]{1,0:T(8,128)(2,1)S(1)}, bf16[36,2304]{1,0:T(8,128)(2,1)S(1)}, u32[]{:S(2)}, u32[]{:S(2)}) collective-permute-start(bf16[36,2304]{1,0:T(8,128)(2,1)S(1)} %get-tuple-element.171), channel_id=1, source_target_pairs={{0,1},{1,0},{2,3},{3,2},{4,5},{5,4},{6,7},{7,6},{8,9},{9,8},{10,11... | collective-permute-start | bytes 497672 | tf_op jit(solution)/shard_map/ppermute | solution.py:464
  311.9 3.1 collective-permute-start.36
  (29 other events, 87.6 us)
where the time goes:
time: 323 us; the launch traced here: 317 us
  Pallas kernels  180 us (56%)
  waiting for transfers between devices  59.8 us (19%)
  starting transfers between devices  59.4 us (18%)
  local copies, waits for them, and re-layouts  14.8 us (5%)
    pallas_call x22, Pallas kernels, run(): pl.pallas_call(body, out_shape=out_shape, in_specs=[pl.BlockSpec(memory_s...  180 us
    ppermute x38, waiting for transfers between devices, swap(): return lax.ppermute(x, axis, [(i, i ^ mask) for i in range(size)])  46.1 us
    ppermute x38, starting transfers between devices, swap(): return lax.ppermute(x, axis, [(i, i ^ mask) for i in range(size)])  31.2 us
    all_to_all x6, starting transfers between devices, exchange(): lax.all_to_all(pieces, 'seq', split_axis=0, concat_axis=0, tiled=True)  28.2 us
    unnamed x67, local copies, waits for them, and re-layouts  14.8 us
    all_to_all x6, waiting for transfers between devices, exchange(): lax.all_to_all(pieces, 'seq', split_axis=0, concat_axis=0, tiled=True)  13.7 us
  transfers between devices with their start and end apart: 44, of which 15 were waited for; matrix products, arithmetic and copies ran while one was open for 1% of the time, Pallas kernels for 54%

commit v1 on v0

--- a/solution.py
+++ b/solution.py
@@ -104,8 +104,7 @@
     return jnp.where(first, out[:rows], out[rows:])
 
 
-def probs_by_key(queries, key, factor, keep):
-    scores = dot(key, queries, NT)
+def softmax_by_key(scores, factor, keep):
     if keep is not None:
         scores = jnp.where(keep, scores, MASKED)
     raised = jnp.exp2((scores - jnp.max(scores, 0, keepdims=True)) * (factor * LOG2_E))
@@ -169,8 +168,8 @@
 def space_forward_kernel(
     n, block, video, x_ref, cot_ref, mod_ref, wqkv_ref, wout_ref, scatter_ref, scatter_cot_ref, *refs
 ):
-    sent_ref, packed_out, modded_out, attended_out, weights_out = refs[-14:-9]
-    x, cot, modded, packed, attended, weights, wqkv, wout, sems = refs[-9:]
+    sent_ref, packed_out, left_out, weights_out = refs[-13:-9]
+    x, cot, left, packed, weights, wqkv, wout, scores_ref, sems = refs[-9:]
     width = x.shape[1]
     size = width // HEADS
     factor = size ** (-0.5)
@@ -182,30 +181,35 @@
         load_cot = copies.start(cot_ref.at[video], cot)
     load_x.wait()
     normed, _ = norm_stats(x[...].astype(F32))
-    modded[...] = (normed * (1.0 + mod_ref[video, 1:2, :]) + mod_ref[video, 0:1, :]).astype(BF16)
-    stores = [copies.start(modded, modded_out)]
-    project_qkv(modded[...], wqkv, load_qkv, packed, width)
-    stores.append(copies.start(packed, packed_out))
+    left[:, 0:width] = (
+        normed * (1.0 + mod_ref[video, 1:2, :]) + mod_ref[video, 0:1, :]
+    ).astype(BF16)
+    project_qkv(left[:, 0:width], wqkv, load_qkv, packed, width)
+    stores = [copies.start(packed, packed_out)]
     pairs = pair_windows(width)
 
     def one_block(g, carry):
         rows = pl.multiple_of(g * block, 16)
+        at = pl.ds(rows, block)
         for pair, (start, span, offset) in enumerate(pairs):
             first, both = pair_masks(block, span, offset, size)
-            at = pl.ds(rows, block)
-            query = packed[at, pl.ds(start, span)]
-            key = packed[at, pl.ds(width + start, span)]
+            query = two_heads(packed[at, pl.ds(start, span)], first, both)
+            scores_ref[pair] = dot(packed[at, pl.ds(width + start, span)], query, NT)
+        for pair in range(len(pairs)):
+            probs = softmax_by_key(scores_ref[pair], factor, None)
+            weights[g * len(pairs) + pair] = probs.astype(BF16)
+        for pair, (start, span, offset) in enumerate(pairs):
+            first, both = pair_masks(block, span, offset, size)
             value = packed[at, pl.ds(2 * width + start, span)]
-            probs = probs_by_key(two_heads(query, first, both), key, factor, None).astype(BF16)
-            weights[g * len(pairs) + pair] = probs
-            put(attended, rows, start, both, per_query(probs, value, first))
+            attended = per_query(weights[g * len(pairs) + pair], value, first)
+            put(left, rows, width + start, both, attended)
         return carry
 
     lax.fori_loop(0, x.shape[0] // block, one_block, 0)
-    stores.append(copies.start(attended, attended_out))
+    stores.append(copies.start(left, left_out))
     stores.append(copies.start(weights, weights_out))
     load_out.wait()
-    projected = dot(attended[...], wout[...])
+    projected = dot(left[:, width:], wout[...])
     middle = (x[...].astype(F32) + mod_ref[video, 2:3, :] * projected).astype(BF16)
     pieces = dot(scatter_ref[...], middle)
     if video:
@@ -216,15 +220,11 @@
         store.wait()
 
 
-def unit_stores(copies, core, width, left, right, outs):
-    *sent_outs, right_out = outs
-    other = (1 - core) * (2 * width)
-    sources = [left.at[:, pl.ds(unit * width, width)] for unit in range(2)]
-    sources += [
-        right.at[:, pl.ds(pl.multiple_of(other + unit * width, 128), width)] for unit in range(2)
-    ]
-    return [copies.start(source, out) for source, out in zip(sources, sent_outs)] + [
-        copies.start(right, right_out)
+def unit_stores(copies, core, width, right, outs):
+    sent_out, right_out = outs
+    other = pl.multiple_of((1 - core) * (2 * width), 128)
+    return [
+        copies.start(right.at[:, pl.ds(other, 2 * width)], sent_out), copies.start(right, right_out)
     ]
 
 
@@ -232,8 +232,9 @@
     n, block, frames, video, core_ref, middle_ref, cot_ref, mod_ref, wqkv_ref, wout_ref,
     gather_ref, gather_cot_ref, scatter_ref, scatter_out_ref, others_ref, *refs
 ):
-    (d_middle_ref, block_out_ref, *unit_outs), scratch = refs[-17:-10], refs[-10:]
-    normed, x, up, left, packed, d_out, right, wqkv, wout, sems = scratch
+    (d_middle_ref, block_out_ref, left_out, *unit_outs), scratch = refs[-19:-14], refs[-14:]
+    normed, x, up, left, packed, d_out, right, wqkv, wout = scratch[:9]
+    scores_ref, d_probs_ref, weights_ref, d_scores_ref, sems = scratch[9:]
     width = x.shape[1]
     size = width // HEADS
     factor = size ** (-0.5)
@@ -253,28 +254,43 @@
     d_out[...] = dot(right[:, 3 * width :], wout[...], NT).astype(BF16)
     keep = same_video(block, frames)
 
+    pairs = pair_windows(width)
+
     def one_block(g, carry):
         rows = pl.multiple_of(g * block, 16)
-        for start, span, offset in pair_windows(width):
+        at = pl.ds(rows, block)
+
+        def parts(pair):
+            start, span, offset = pairs[pair]
             first, both = pair_masks(block, span, offset, size)
-            at = pl.ds(rows, block)
             query = two_heads(packed[at, pl.ds(start, span)], first, both)
             key = packed[at, pl.ds(width + start, span)]
             value = packed[at, pl.ds(2 * width + start, span)]
             d_rows = two_heads(d_out[at, pl.ds(start, span)], first, both)
-            probs = probs_by_key(query, key, factor, keep)
-            weights = probs.astype(BF16)
+            return start, first, both, query, key, value, d_rows
+
+        for pair in range(len(pairs)):
+            _, _, _, query, key, value, d_rows = parts(pair)
+            scores_ref[pair] = dot(key, query, NT)
+            d_probs_ref[pair] = dot(value, d_rows, NT)
+        for pair in range(len(pairs)):
+            probs = softmax_by_key(scores_ref[pair], factor, keep)
+            d_probs = d_probs_ref[pair]
+            total = jnp.sum(probs * d_probs, 0, keepdims=True)
+            weights_ref[pair] = probs.astype(BF16)
+            d_scores_ref[pair] = (probs * (d_probs - total) * factor).astype(BF16)
+        for pair in range(len(pairs)):
+            start, first, both, query, key, value, d_rows = parts(pair)
+            weights, d_scores = weights_ref[pair], d_scores_ref[pair]
             put(left, rows, width + start, both, per_query(weights, value, first))
-            d_probs = dot(value, d_rows, NT)
-            total = jnp.sum(probs * d_probs, 0, keepdims=True)
-            d_scores = (probs * (d_probs - total) * factor).astype(BF16)
             put(right, rows, start, both, per_query(d_scores, key, first))
             put(right, rows, width + start, both, dot(d_scores, query))
             put(right, rows, 2 * width + start, both, dot(weights, d_rows))
         return carry
 
     lax.fori_loop(0, x.shape[0] // block, one_block, 0)
-    stores = unit_stores(copies, core_ref[1] & 1, width, left, right, unit_outs)
+    stores = [copies.start(left, left_out)]
+    stores += unit_stores(copies, core_ref[1] & 1, width, right, unit_outs)
     d_modded = dot(right[:, 0 : 3 * width], wqkv[...], NT)
     d_middle = up[...].astype(F32) + norm_backward(
         d_modded, normed[...], inverse, mod_ref[video, 4:5, :]
@@ -291,21 +307,16 @@
 
 
 def space_backward_kernel(
-    block, video, core_ref, up_ref, mod_ref, wout_ref, gather_ref, packed_ref, modded_ref,
-    attended_ref, weights_ref, *refs
+    block, video, core_ref, up_ref, mod_ref, wout_ref, gather_ref, packed_ref, weights_ref, *refs
 ):
-    d_middle_ref, *unit_outs = refs[-12:-6]
-    d_out, left, right, packed, wout, sems = refs[-6:]
+    d_middle_ref, *unit_outs = refs[-10:-7]
+    d_out, right, packed, wout, d_probs_ref, d_scores_ref, sems = refs[-7:]
     width = wout.shape[0]
     size = width // HEADS
     factor = size ** (-0.5)
     copies = Copies(sems)
     load_out = copies.start(wout_ref, wout)
     load_packed = copies.start(packed_ref, packed)
-    loads = [
-        copies.start(modded_ref, left.at[:, pl.ds(0, width)]),
-        copies.start(attended_ref, left.at[:, pl.ds(width, width)]),
-    ]
     up = dot(gather_ref[...], frame_rows(up_ref[...]))
     d_middle_ref[...] = up.astype(BF16)
     right[:, 3 * width :] = (mod_ref[video, 2:3, :] * up).astype(BF16)
@@ -316,27 +327,29 @@
 
     def one_block(g, carry):
         rows = pl.multiple_of(g * block, 16)
+        at = pl.ds(rows, block)
         for pair, (start, span, offset) in enumerate(pairs):
             first, both = pair_masks(block, span, offset, size)
-            at = pl.ds(rows, block)
+            d_rows = two_heads(d_out[at, pl.ds(start, span)], first, both)
+            d_probs_ref[pair] = dot(packed[at, pl.ds(2 * width + start, span)], d_rows, NT)
+        for pair in range(len(pairs)):
+            probs = weights_ref[g * len(pairs) + pair].astype(F32)
+            d_probs = d_probs_ref[pair]
+            total = jnp.sum(probs * d_probs, 0, keepdims=True) / jnp.sum(probs, 0, keepdims=True)
+            d_scores_ref[pair] = (probs * (d_probs - total) * factor).astype(BF16)
+        for pair, (start, span, offset) in enumerate(pairs):
+            first, both = pair_masks(block, span, offset, size)
             query = two_heads(packed[at, pl.ds(start, span)], first, both)
             key = packed[at, pl.ds(width + start, span)]
-            value = packed[at, pl.ds(2 * width + start, span)]
             d_rows = two_heads(d_out[at, pl.ds(start, span)], first, both)
-            weights = weights_ref[g * len(pairs) + pair]
-            probs = weights.astype(F32)
-            d_probs = dot(value, d_rows, NT)
-            total = jnp.sum(probs * d_probs, 0, keepdims=True) / jnp.sum(probs, 0, keepdims=True)
-            d_scores = (probs * (d_probs - total) * factor).astype(BF16)
+            weights, d_scores = weights_ref[g * len(pairs) + pair], d_scores_ref[pair]
             put(right, rows, start, both, per_query(d_scores, key, first))
             put(right, rows, width + start, both, dot(d_scores, query))
             put(right, rows, 2 * width + start, both, dot(weights, d_rows))
         return carry
 
     lax.fori_loop(0, d_out.shape[0] // block, one_block, 0)
-    for load in loads:
-        load.wait()
-    for store in unit_stores(copies, core_ref[1] & 1, width, left, right, unit_outs):
+    for store in unit_stores(copies, core_ref[1] & 1, width, right, unit_outs):
         store.wait()
 
 
@@ -365,39 +378,41 @@
 
 
 def emit_halves(rows, inner, mine, kept_ref, sent_ref):
+    columns = kept_ref.shape[2]
     for outer in range(kept_ref.shape[0]):
-        low = rows[2 * outer * inner : (2 * outer + 1) * inner, :]
-        high = rows[(2 * outer + 1) * inner : (2 * outer + 2) * inner, :]
+        low = rows[2 * outer * inner : (2 * outer + 1) * inner, :columns]
+        high = rows[(2 * outer + 1) * inner : (2 * outer + 2) * inner, :columns]
         kept_ref[outer] = jnp.where(mine == 0, low, high).astype(BF16)
         sent_ref[outer] = jnp.where(mine == 0, high, low).astype(BF16)
 
 
 def weight_kernel(videos, cuts, steps, grad_scale, place_ref, *refs):
-    right, units = refs[:videos], refs[videos : 9 * videos]
-    sent = [units[4 * v : 4 * v + 4] for v in range(videos)]
-    got = [units[4 * v : 4 * v + 4] for v in range(videos, 2 * videos)]
+    left_own, left_got, right_own, right_got = [
+        refs[at * videos : (at + 1) * videos] for at in range(4)
+    ]
     count = 2 * len(cuts)
     outs, scratch = refs[-4 - 2 * count : -4 - count], refs[-4 - count : -4]
     left_rows, right_rows, total, sems = refs[-4:]
     width = left_rows.shape[1] // 2
-    tokens = right[0].shape[0]
+    tokens = left_own[0].shape[0]
     copies = Copies(sems)
     core = place_ref[1] & 1
     own = pl.multiple_of(core * (2 * width), 128)
     waits = []
     for unit in range(2):
         now = []
+        at = pl.ds(unit * width, width)
+        mine = pl.ds(pl.multiple_of(own + unit * width, 128), width)
         for video in range(videos):
-            for place, (left, mine) in enumerate(((sent[video], right[video]), (got[video], None))):
+            for place, (left, right, columns) in enumerate(
+                (
+                    (left_own[video], right_own[video], mine),
+                    (left_got[video], right_got[video], at),
+                )
+            ):
                 rows = pl.ds((2 * video + place) * tokens, tokens)
-                at = pl.ds(unit * width, width)
-                now.append(copies.start(left[unit], left_rows.at[rows, at]))
-                source = (
-                    left[2 + unit]
-                    if mine is None
-                    else mine.at[:, pl.ds(pl.multiple_of(own + unit * width, 128), width)]
-                )
-                now.append(copies.start(source, right_rows.at[rows, at]))
+                now.append(copies.start(left.at[:, at], left_rows.at[rows, at]))
+                now.append(copies.start(right.at[:, columns], right_rows.at[rows, at]))
         waits.append(now)
     done, stores = 0, []
     for part, ((low, high), (axis, bit, inner)) in enumerate(zip(cuts, steps)):
@@ -428,24 +443,23 @@
         kept, got = refs[part], refs[count + part]
         each = kept.shape[1]
         for outer in range(kept.shape[0]):
-            total[outer * each : (outer + 1) * each, :] = kept[outer].astype(F32) + got[
-                outer
-            ].astype(F32)
+            total[outer * each : (outer + 1) * each, : kept.shape[2]] = kept[outer].astype(
+                F32
+            ) + got[outer].astype(F32)
         emit_halves(
             total, inner, bit_of(place_ref, axis, bit), outs[2 * part], outs[2 * part + 1]
         )
 
 
-def core_stage_kernel(count, place_ref, *refs):
+def core_stage_kernel(cuts, place_ref, *refs):
     kept_out, sent_out = refs[-2:]
-    rows, columns = refs[0].shape[1:]
     core = place_ref[1] & 1
-    for part in range(count):
-        total = refs[part][0].astype(F32) + refs[count + part][0].astype(F32)
-        low, high = total[: rows // 2], total[rows // 2 :]
-        at = slice(part * columns, (part + 1) * columns)
-        kept_out[:, at] = jnp.where(core == 0, low, high).astype(BF16)
-        sent_out[:, at] = jnp.where(core == 0, high, low).astype(BF16)
+    for part, (start, stop) in enumerate(cuts):
+        total = refs[part][0].astype(F32) + refs[len(cuts) + part][0].astype(F32)
+        rows = total.shape[0] // 2
+        low, high = total[:rows], total[rows:]
+        kept_out[:, start:stop] = jnp.where(core == 0, low, high).astype(BF16)
+        sent_out[:, start:stop] = jnp.where(core == 0, high, low).astype(BF16)
 
 
 def assemble_kernel(place_ref, kept_ref, got_ref, qkv_ref, out_ref):
@@ -476,23 +490,24 @@
             )
         else:
             self.orders = (dp_bits + seq_bits, dp_bits[::-1] + seq_bits)
+        tiles = 2 * width // 128
+        ends = [0, (tiles - tiles // 6) * 64, (tiles - tiles // 6) * 128] if late else [0, width]
+        self.cuts = tuple(zip(ends, ends[1:] + [2 * width]))
         self.parts = len(self.orders)
-        self.place, self.width, self.columns = place, width, 2 * width // self.parts
-        self.cuts = tuple(
-            (part * self.columns, (part + 1) * self.columns) for part in range(self.parts)
-        )
+        self.place, self.width = place, width
+        self.columns = max(stop - start for start, stop in self.cuts)
         self.bits = dp_bits[::-1] + seq_bits[::-1]
         self.step = 0
 
     def next_steps(self):
         least = self.width >> len(self.bits)
         steps, shapes = [], []
-        for order in self.orders:
+        for order, (start, stop) in zip(self.orders, self.cuts):
             left = [bit for bit in self.bits if bit not in order[: self.step]]
             above = left.index(order[self.step])
             inner = least << (len(left) - above - 1)
             steps.append((*order[self.step], inner))
-            shapes += 2 * [shaped(1 << above, inner, self.columns)]
+            shapes += 2 * [shaped(1 << above, inner, stop - start)]
         return tuple(steps), tuple(shapes)
 
     def send(self, halves):
@@ -519,7 +534,7 @@
         rows = self.width >> (len(self.bits) + 1)
         half = shaped(rows, 2 * self.width)
         self.mine, sent = call(
-            "core_stage", 1, functools.partial(core_stage_kernel, self.parts),
+            "core_stage", 1, functools.partial(core_stage_kernel, self.cuts),
             "s" + "v" * (2 * self.parts), (half, half), "vv",
         )(self.place, *self.kept, *self.got, deps=deps)
         self.other = swap(sent, "seq", 1)
@@ -574,7 +589,7 @@
     piece = shaped(n, padded, width)
     joint_piece = shaped(n, joint_padded, width)
     row = shaped(tokens, width)
-    three, four = shaped(tokens, 3 * width), shaped(tokens, 4 * width)
+    two, three, four = [shaped(tokens, count * width) for count in (2, 3, 4)]
     all_rows = shaped(videos, tokens, width)
     weights_shape = (frames * (HEADS // 2), patches, 2 * patches)
 
@@ -587,6 +602,9 @@
     weight_refs = [vmem(width, 3 * width), vmem(width, width)]
     x = frames_in.reshape(videos, tokens, width)
     cot = cotangent.reshape(videos, tokens, width)
+
+    def exchange_units(units):
+        return swap(units, "seq", 1)
 
     cot_sent = call("split", 3, functools.partial(split_kernel, n), "vv", piece, "v")(
         cot, to_pieces
@@ -598,12 +616,12 @@
         sent, *keep = call(
             "space_forward", 14, functools.partial(space_forward_kernel, n, patches, v),
             "aavaavv",
-            (joint_piece if v else piece, three, row, row, shaped(*weights_shape)),
-            "vaaaa",
+            (joint_piece if v else piece, three, two, shaped(*weights_shape)),
+            "vaaa",
             [
-                vmem(tokens, width), vmem(tokens, width), vmem(tokens, width),
-                vmem(tokens, 3 * width), vmem(tokens, width), vmem(*weights_shape),
-                *weight_refs, sems(10),
+                vmem(tokens, width), vmem(tokens, width), vmem(tokens, 2 * width),
+                vmem(tokens, 3 * width), vmem(*weights_shape), *weight_refs,
+                vmem(HEADS // 2, patches, 2 * patches, dtype=F32), sems(9),
             ],
         )(
             x, cot, modulation, spatial_qkv, spatial_out, to_joint[0] if v else to_pieces,
@@ -611,22 +629,21 @@
         )
         deps = [keep[0], cot_pieces]
         arrived.append(exchange(sent))
-        saved.append(keep)
-
-    def exchange_units(sent):
-        return [swap(unit, "seq", 1) for unit in sent]
+        saved.append((*keep, exchange_units(keep[1])))
 
     returned, time_units, out_sent = [], [], core
     for v in range(videos):
-        d_middle, out_sent, *sent, right = call(
+        d_middle, out_sent, left, sent, right = call(
             "time", 25, functools.partial(time_kernel, n, time_block, all_frames, v),
             "svvvaavvvv" + ("v" if v else "a"),
-            (piece, joint_piece) + 4 * (row,) + (four,),
-            "vvaaaaa",
+            (piece, joint_piece, two, two, four),
+            "vvaaa",
             [
                 vmem(tokens, width, dtype=F32), vmem(tokens, width), vmem(tokens, width),
                 vmem(tokens, 2 * width), vmem(tokens, 3 * width), vmem(tokens, width),
-                vmem(tokens, 4 * width), *weight_refs, sems(9),
+                vmem(tokens, 4 * width), *weight_refs,
+                *[vmem(HEADS // 2, time_block, 2 * time_block, dtype=d) for d in (F32, F32, BF16, BF16)],
+                sems(9),
             ],
         )(
             core, arrived[v], arrived[v] if v else cot_pieces, modulation, temporal_qkv,
@@ -636,23 +653,23 @@
         )
         deps = [right]
         returned.append(exchange(d_middle))
-        time_units.append((sent, right, exchange_units(sent)))
+        time_units.append((left, exchange_units(left), right, exchange_units(sent)))
 
     grad_scale = (videos * lax.axis_size("dp") * all_frames * patches) ** (-0.5)
 
     def weights(units, late, deps=()):
         reduction = Reduction(core, width, late)
         steps, shapes = reduction.next_steps()
-        sent, right, got = zip(*units)
+        operands = [one for kind in zip(*units) for one in kind]
         halves = call(
             "weights", 10,
             functools.partial(weight_kernel, videos, reduction.cuts, steps, grad_scale),
-            "s" + "a" * (9 * videos), shapes, "a" * len(shapes),
+            "s" + "a" * (4 * videos), shapes, "a" * len(shapes),
             [vmem(*half.shape) for half in shapes] + [
                 vmem(2 * videos * tokens, 2 * width), vmem(2 * videos * tokens, 2 * width),
                 vmem(width, reduction.columns, dtype=F32), sems(8 * videos + len(shapes)),
             ],
-        )(core, *right, *sum(sent, []), *sum(got, []), deps=deps)
+        )(core, *operands, deps=deps)
         reduction.send(halves)
         return reduction, halves[0]
 
@@ -660,28 +677,31 @@
         return call(
             "grad_input", 8, functools.partial(grad_input_kernel, video), "avvva", row, "v",
             [vmem(tokens, 3 * width), vmem(width, 3 * width), sems(6)],
-        )(units[1], d_middle, x, modulation, spatial_qkv, deps=deps)
+        )(units[2], d_middle, x, modulation, spatial_qkv, deps=deps)
 
     d_middles, space_units, grad_input = [], [], []
     for v in range(videos):
-        d_middle, *sent, right = call(
+        packed, left, weights_saved, left_got = saved[v]
+        d_middle, sent, right = call(
             "space_backward", 15, functools.partial(space_backward_kernel, patches, v),
-            "svvavaaav",
-            (row,) + 4 * (row,) + (four,),
-            "vaaaaa",
+            "svvavav",
+            (row, two, four),
+            "vaa",
             [
-                vmem(tokens, width), vmem(tokens, 2 * width), vmem(tokens, 4 * width),
-                vmem(tokens, 3 * width), vmem(width, width), sems(9),
+                vmem(tokens, width), vmem(tokens, 4 * width), vmem(tokens, 3 * width),
+                vmem(width, width),
+                *[vmem(HEADS // 2, patches, 2 * patches, dtype=d) for d in (F32, BF16)], sems(4),
             ],
         )(
-            core, returned[v], modulation, spatial_out, from_pieces, *saved[v], deps=deps
+            core, returned[v], modulation, spatial_out, from_pieces, packed, weights_saved,
+            deps=[*deps, left_got],
         )
         if v == 0:
             time_sum, began = weights(time_units, False, deps=[right])
             deps = [began]
             out_back = exchange(out_sent)
         d_middles.append(d_middle)
-        space_units.append((sent, right, exchange_units(sent)))
+        space_units.append((left, left_got, right, exchange_units(sent)))
     grad_input.append(grad_of(0, space_units[0], d_middles[0], deps=[right]))
     began = time_sum.stage(deps=grad_input)
     space_sum, began = weights(space_units, True, deps=[began])

time: 323 us -> 298 us (0.923)
  Pallas kernels: 180 us -> 159 us
    pallas_call x22, Pallas kernels: 180 us -> 159 us  [run(): pl.pallas_call(body, out_shape=out_shape, in_specs=[pl.BlockSpec(memory_s...]
    ppermute x38 -> x30, waiting for transfers between devices: 46.1 us -> 34.3 us  [swap(): return lax.ppermute(x, axis, [(i, i ^ mask) for i in range(size)])]
    all_to_all x6, waiting for transfers between devices: 13.7 us -> 23.7 us  [exchange(): lax.all_to_all(pieces, 'seq', split_axis=0, concat_axis=0, tiled=True)]
    ppermute x38 -> x30, starting transfers between devices: 31.2 us -> 29.4 us  [swap(): return lax.ppermute(x, axis, [(i, i ^ mask) for i in range(size)])]
    unnamed x67 -> x61, local copies, waits for them, and re-layouts: 14.8 us -> 15.2 us
  transfers between devices with their start and end apart: 44 -> 36, of which waited for: 15 -> 13; matrix products, arithmetic and copies ran while one was open for 1% -> 1% of each run, Pallas kernels for 54% -> 51%
where the time goes in v1:
time: 298 us; the launch traced here: 293 us
  Pallas kernels  159 us (53%)
  waiting for transfers between devices  58 us (19%)
  starting transfers between devices  57.1 us (19%)
  local copies, waits for them, and re-layouts  15.2 us (5%)
    pallas_call x22, Pallas kernels, run(): pl.pallas_call(body, out_shape=out_shape, in_specs=[pl.BlockSpec(memory_s...  159 us
    ppermute x30, waiting for transfers between devices, swap(): return lax.ppermute(x, axis, [(i, i ^ mask) for i in range(size)])  34.3 us
    ppermute x30, starting transfers between devices, swap(): return lax.ppermute(x, axis, [(i, i ^ mask) for i in range(size)])  29.4 us
    all_to_all x6, starting transfers between devices, exchange(): lax.all_to_all(pieces, 'seq', split_axis=0, concat_axis=0, tiled=True)  27.8 us
    all_to_all x6, waiting for transfers between devices, exchange(): lax.all_to_all(pieces, 'seq', split_axis=0, concat_axis=0, tiled=True)  23.7 us
    unnamed x61, local copies, waits for them, and re-layouts  15.2 us
  transfers between devices with their start and end apart: 36, of which 13 were waited for; matrix products, arithmetic and copies ran while one was open for 1% of the time, Pallas kernels for 51%

profile of v1, /device:TPU:0, one launch (start us, length us, event | category | flops | bytes accessed | tf_op | source)
XLA Modules:
  0.0 292.7 jit_solution(4730213221159777311)
XLA Ops:
  0.6 2.8 split.1.refs_0_
  3.4 6.5 %all-to-all-start = ((bf16[8,40,1152]{2,1,0:T(8,128)(2,1)}), bf16[8,40,1152]{2,1,0:T(8,128)(2,1)S(1)}, u32[]{:S(2)}, u32[]{:S(2)}) async-start(bf16[8,40,1152]{2,1,0:T(8,128)(2,1)} %split.1.refs_0_), calls=%async_computation | async-start | bytes 1474560 | tf_op jit(solution)/shard_map/all_to_all | solution.py:587
  10.5 11.8 %space_forward.2 = (bf16[8,40,1152]{2,1,0:T(8,128)(2,1)}, bf16[288,3456]{1,0:T(8,128)(2,1)}, bf16[288,2304]{1,0:T(8,128)(2,1)}, bf16[16,144,288]{2,1,0:T(8,128)(2,1)}) custom-call(bf16[2,288,1152]{2,1,0:T(8,128)(2,1)} %bitcast.13, bf16[2,288,1152]{2,1,0:T(8,128)(2,1)} %bitcast.11, f32[2,6,1152]{2,1,0:T(8,128)} %copy.25.mod_ref, ...), custom_call_target="tpu_custom_call" | custom-call | flops 14000000000 | bytes 14000000 | tf_op jit(solution)/shard_map/space_forward/pallas_call | solution.py:37
  23.4 6.3 %all-to-all-done.refs_1_.cot_ref = bf16[8,40,1152]{2,1,0:T(8,128)(2,1)S(1)} async-done(((bf16[8,40,1152]{2,1,0:T(8,128)(2,1)}), bf16[8,40,1152]{2,1,0:T(8,128)(2,1)S(1)}, u32[]{:S(2)}, u32[]{:S(2)}) %all-to-all-start) | async-done | bytes 737312 | tf_op jit(solution)/shard_map/all_to_all | solution.py:587
  29.8 3.8 %all-to-all-start.2 = ((bf16[8,40,1152]{2,1,0:T(8,128)(2,1)}), bf16[8,40,1152]{2,1,0:T(8,128)(2,1)S(1)}, u32[]{:S(2)}, u32[]{:S(2)}) async-start(bf16[8,40,1152]{2,1,0:T(8,128)(2,1)} %get-tuple-element.80), calls=%async_computation.2 | async-start | bytes 1474560 | tf_op jit(solution)/shard_map/all_to_all | solution.py:587
  33.6 13.4 %space_forward.3 = (bf16[8,72,1152]{2,1,0:T(8,128)(2,1)}, bf16[288,3456]{1,0:T(8,128)(2,1)}, bf16[288,2304]{1,0:T(8,128)(2,1)}, bf16[16,144,288]{2,1,0:T(8,128)(2,1)}) custom-call(bf16[2,288,1152]{2,1,0:T(8,128)(2,1)} %bitcast.14, bf16[2,288,1152]{2,1,0:T(8,128)(2,1)} %bitcast.12, f32[2,6,1152]{2,1,0:T(8,128)} %copy.25.mod_ref, ...), custom_call_target="tpu_custom_call" | custom-call | flops 14000000000 | bytes 14000000 | tf_op jit(solution)/shard_map/space_forward/pallas_call | solution.py:37
  46.9 6.5 %all-to-all-done.2.middle_ref = bf16[8,40,1152]{2,1,0:T(8,128)(2,1)S(1)} async-done(((bf16[8,40,1152]{2,1,0:T(8,128)(2,1)}), bf16[8,40,1152]{2,1,0:T(8,128)(2,1)S(1)}, u32[]{:S(2)}, u32[]{:S(2)}) %all-to-all-start.2) | async-done | bytes 737312 | tf_op jit(solution)/shard_map/all_to_all | solution.py:587
  54.3 3.8 %all-to-all-start.1 = ((bf16[8,72,1152]{2,1,0:T(8,128)(2,1)}), bf16[8,72,1152]{2,1,0:T(8,128)(2,1)S(1)}, u32[]{:S(2)}, u32[]{:S(2)}) async-start(bf16[8,72,1152]{2,1,0:T(8,128)(2,1)} %get-tuple-element.79), calls=%async_computation.1 | async-start | bytes 2654208 | tf_op jit(solution)/shard_map/all_to_all | solution.py:587
  58.1 20.6 %time.2 = (bf16[8,40,1152]{2,1,0:T(8,128)(2,1)}, bf16[8,72,1152]{2,1,0:T(8,128)(2,1)}, bf16[288,2304]{1,0:T(8,128)(2,1)}, bf16[288,2304]{1,0:T(8,128)(2,1)}, bf16[288,4608]{1,0:T(8,128)(2,1)}) custom-call(s32[2]{0:T(128)} %pad_add_fusion.core_ref.others_ref.place_ref, bf16[8,40,1152]{2,1,0:T(8,128)(2,1)} %copy-done.26, bf16[8,40,1152]{2,1,0:T(8,128)(2,1)} %copy-done.24, ...), custom_call_target="tpu_custom_call" | custom-call | flops 24999999488 | bytes 25000000 | tf_op jit(solution)/shard_map/time/pallas_call | solution.py:37
  79.7 10.9 %all-to-all-done.1.middle_ref.cot_ref = bf16[8,72,1152]{2,1,0:T(8,128)(2,1)S(1)} async-done(((bf16[8,72,1152]{2,1,0:T(8,128)(2,1)}), bf16[8,72,1152]{2,1,0:T(8,128)(2,1)S(1)}, u32[]{:S(2)}, u32[]{:S(2)}) %all-to-all-start.1) | async-done | bytes 1327136 | tf_op jit(solution)/shard_map/all_to_all | solution.py:587
  90.6 4.0 %all-to-all-start.4 = ((bf16[8,40,1152]{2,1,0:T(8,128)(2,1)}), bf16[8,40,1152]{2,1,0:T(8,128)(2,1)S(1)}, u32[]{:S(2)}, u32[]{:S(2)}) async-start(bf16[8,40,1152]{2,1,0:T(8,128)(2,1)} %get-tuple-element.87), calls=%async_computation.4 | async-start | bytes 1474560 | tf_op jit(solution)/shard_map/all_to_all | solution.py:587
  94.6 21.5 %time.3 = (bf16[8,40,1152]{2,1,0:T(8,128)(2,1)}, bf16[8,72,1152]{2,1,0:T(8,128)(2,1)}, bf16[288,2304]{1,0:T(8,128)(2,1)}, bf16[288,2304]{1,0:T(8,128)(2,1)}, bf16[288,4608]{1,0:T(8,128)(2,1)}) custom-call(s32[2]{0:T(128)} %pad_add_fusion.core_ref.others_ref.place_ref, bf16[8,72,1152]{2,1,0:T(8,128)(2,1)} %copy-done.22, bf16[8,72,1152]{2,1,0:T(8,128)(2,1)} %copy-done.22, ...), custom_call_target="tpu_custom_call" | custom-call | flops 24999999488 | bytes 25000000 | tf_op jit(solution)/shard_map/time/pallas_call | solution.py:37
  117.7 5.0 %all-to-all-start.5 = ((bf16[8,40,1152]{2,1,0:T(8,128)(2,1)}), bf16[8,40,1152]{2,1,0:T(8,128)(2,1)S(1)}, u32[]{:S(2)}, u32[]{:S(2)}) async-start(bf16[8,40,1152]{2,1,0:T(8,128)(2,1)} %get-tuple-element.91), calls=%async_computation.5 | async-start | bytes 1474560 | tf_op jit(solution)/shard_map/all_to_all | solution.py:587
  122.7 11.4 %space_backward.2 = (bf16[288,1152]{1,0:T(8,128)(2,1)}, bf16[288,2304]{1,0:T(8,128)(2,1)}, bf16[288,4608]{1,0:T(8,128)(2,1)}) custom-call(s32[2]{0:T(128)} %pad_add_fusion.core_ref.others_ref.place_ref, bf16[8,40,1152]{2,1,0:T(8,128)(2,1)} %copy-done.25, f32[2,6,1152]{2,1,0:T(8,128)} %copy.25.mod_ref, bf16[1152,1152]{1,0:T(8,128)(2,1)} %wout_ref.11, ...), custom_call_target="tpu_custom_call" | custom-call | flops 15000000512 | bytes 15000000 | tf_op jit(solution)/shard_map/space_backward/pallas_call | solution.py:37
  135.8 14.3 %weights.2 = (bf16[2,288,1152]{2,1,0:T(8,128)(2,1)}, bf16[2,288,1152]{2,1,0:T(8,128)(2,1)}, bf16[1,576,1152]{2,1,0:T(8,128)(2,1)}, bf16[1,576,1152]{2,1,0:T(8,128)(2,1)}) custom-call(s32[2]{0:T(128)} %pad_add_fusion.core_ref.others_ref.place_ref, bf16[288,2304]{1,0:T(8,128)(2,1)} %get-tuple-element.93.refs_0_, bf16[288,2304]{1,0:T(8,128)(2,1)} %get-tuple-element.94.refs_1_, ...), custom_call_target="tpu_custom_call" | custom-call | flops 10000000000 | bytes 10000000 | tf_op jit(solution)/shard_map/weights/pallas_call | solution.py:37
  150.2 1.6 collective-permute-start.8
  151.7 1.5 collective-permute-start.9
  154.1 4.8 %all-to-all-start.3 = ((bf16[8,72,1152]{2,1,0:T(8,128)(2,1)}), bf16[8,72,1152]{2,1,0:T(8,128)(2,1)S(1)}, u32[]{:S(2)}, u32[]{:S(2)}) async-start(bf16[8,72,1152]{2,1,0:T(8,128)(2,1)} %get-tuple-element.84), calls=%async_computation.3 | async-start | bytes 2654208 | tf_op jit(solution)/shard_map/all_to_all | solution.py:587
  158.9 11.7 %space_backward.3 = (bf16[288,1152]{1,0:T(8,128)(2,1)}, bf16[288,2304]{1,0:T(8,128)(2,1)}, bf16[288,4608]{1,0:T(8,128)(2,1)}) custom-call(s32[2]{0:T(128)} %pad_add_fusion.core_ref.others_ref.place_ref, bf16[8,40,1152]{2,1,0:T(8,128)(2,1)} %copy-done.23, f32[2,6,1152]{2,1,0:T(8,128)} %copy.25.mod_ref, bf16[1152,1152]{1,0:T(8,128)(2,1)} %wout_ref.11, ...), custom_call_target="tpu_custom_call" | custom-call | flops 15000000512 | bytes 15000000 | tf_op jit(solution)/shard_map/space_backward/pallas_call | solution.py:37
  171.2 9.4 %grad_input.2.refs_4_ = bf16[288,1152]{1,0:T(8,128)(2,1)} custom-call(bf16[288,4608]{1,0:T(8,128)(2,1)} %get-tuple-element.90.refs_8_.right_ref.refs_4_, bf16[288,1152]{1,0:T(8,128)(2,1)} %get-tuple-element.104.d_middle_ref, bf16[2,288,1152]{2,1,0:T(8,128)(2,1)} %bitcast.15, f32[2,6,1152]{2,1,0:T(8,128)} %copy.25.mod_ref, bf16[1152,3456]{1,0:T(8,128)(2,1)} %wqkv_ref.11, ...), custom_call_target="tpu_custom_call" | custom-call | flops 8000000000 | bytes 8000000 | tf_op jit(solution)/shard_map/grad_input/pallas_call | solution.py:37
  181.5 1.3 collective-permute-done.9.refs_3_
  183.9 3.0 %stage.6 = (bf16[1,288,1152]{2,1,0:T(8,128)(2,1)S(1)}, bf16[1,288,1152]{2,1,0:T(8,128)(2,1)}, bf16[1,288,1152]{2,1,0:T(8,128)(2,1)S(1)}, bf16[1,288,1152]{2,1,0:T(8,128)(2,1)}) custom-call(s32[2]{0:T(128)S(1)} %copy-done.6, bf16[2,288,1152]{2,1,0:T(8,128)(2,1)S(1)} %copy-done.8, bf16[1,576,1152]{2,1,0:T(8,128)(2,1)S(1)} %copy-done.9, ...), custom_call_target="tpu_custom_call" | custom-call | flops 2000000000 | bytes 2000000 | tf_op jit(solution)/shard_map/stage/pallas_call | solution.py:37
  188.7 1.5 collective-permute-start.13
  190.7 14.5 %weights.3 = (bf16[2,288,960]{2,1,0:T(8,128)(2,1)}, bf16[2,288,960]{2,1,0:T(8,128)(2,1)}, bf16[1,576,960]{2,1,0:T(8,128)(2,1)}, bf16[1,576,960]{2,1,0:T(8,128)(2...) custom-call(s32[2]{0:T(128)} %pad_add_fusion.core_ref.others_ref.place_ref, ...), custom_call_target="tpu_custom_call" | custom-call | flops 10000000000 | bytes 10000000 | tf_op jit(solution)/shard_map/weights/pallas_call | solution.py:37
  205.2 1.6 collective-permute-start.10
  207.3 2.0 collective-permute-start.12
  209.3 1.7 copy-done.10
  213.2 1.5 stage.7
  215.5 2.0 collective-permute-start.16
  217.5 9.3 %grad_input.3.refs_4_ = bf16[288,1152]{1,0:T(8,128)(2,1)} custom-call(bf16[288,4608]{1,0:T(8,128)(2,1)} %get-tuple-element.98.refs_0_.refs_5_.right_ref, bf16[288,1152]{1,0:T(8,128)(2,1)} %get-tuple-element.119.d_middle_ref, bf16[2,288,1152]{2,1,0:T(8,128)(2,1)} %bitcast.16, f32[2,6,1152]{2,1,0:T(8,128)} %copy.25.mod_ref, bf16[1152,3456]{1,0:T(8,128)(2,1)} %wqkv_ref.11, ...), custom_call_target="tpu_custom_call" | custom-call | flops 8000000000 | bytes 8000000 | tf_op jit(solution)/shard_map/grad_input/pallas_call | solution.py:37
  227.2 5.0 %collective-permute-done.16.refs_3_ = bf16[2,72,1152]{2,1,0:T(8,128)(2,1)S(1)} collective-permute-done((bf16[2,72,1152]{2,1,0:T(8,128)(2,1)S(1)}, bf16[2,72,1152]{2,1,0:T(8,128)(2,1)S(1)}, u32[]{:S(2)}, u32[]{:S(2)}) %collective-permute-start.16) | collective-permute-done | bytes 331808 | tf_op jit(solution)/shard_map/ppermute | solution.py:478
  232.2 1.1 copy-done.3
  235.0 2.9 %stage.9 = (bf16[1,288,960]{2,1,0:T(8,128)(2,1)S(1)}, bf16[1,288,960]{2,1,0:T(8,128)(2,1)S(1)}, bf16[4,72,960]{2,1,0:T(8,128)(2,1)S(1)}, bf16[4,72,960]{2,1,0:T(...) custom-call(s32[2]{0:T(128)S(1)} %copy-done.7, bf16[2,288,960]{2,1,0:T(8,128)(2,1)S(1)} %copy-done.11, ...), custom_call_target="tpu_custom_call" | custom-call | flops 2000000000 | bytes 2000000 | tf_op jit(solution)/shard_map/stage/pallas_call | solution.py:37
  238.8 1.5 collective-permute-start.17
  240.3 1.7 collective-permute-start.18
  242.0 2.4 collective-permute-start.20
  245.6 3.9 %join.1.refs_6_ = bf16[2,288,1152]{2,1,0:T(8,128)(2,1)} custom-call(bf16[8,72,1152]{2,1,0:T(8,128)(2,1)} %copy-done, bf16[576,576]{1,0:T(8,128)(2,1)} %constant.30.clone.gather_ref, bf16[1,288,960]{2,1,0:T(8,128)(2,1)} %copy-done.17), custom_call_target="tpu_custom_call" | custom-call | flops 4000000000 | bytes 4000000 | tf_op jit(solution)/shard_map/join/pallas_call | solution.py:37
  249.5 7.7 %collective-permute-done.20.refs_2_ = bf16[1,72,1152]{2,1,0:T(8,128)(2,1)S(1)} collective-permute-done((bf16[1,72,1152]{2,1,0:T(8,128)(2,1)S(1)}, bf16[1,72,1152]{2,1,0:T(8,128)(2,1)S(1)}, u32[]{:S(2)}, u32[]{:S(2)}) %collective-permute-start.20) | collective-permute-done | bytes 165920 | tf_op jit(solution)/shard_map/ppermute | solution.py:478
  257.1 1.8 collective-permute-done.21.refs_3_
  260.6 1.3 stage.10
  261.9 3.8 %collective-permute-start.22 = (bf16[2,72,960]{2,1,0:T(8,128)(2,1)S(1)}, bf16[2,72,960]{2,1,0:T(8,128)(2,1)S(1)}, u32[]{:S(2)}, u32[]{:S(2)}) collective-permute-start(bf16[2,72,960]{2,1,0:T(8,128)(2,1)S(1)} %get-tuple-element.134), channel_id=1, source_target_pairs={{0,2},{1,3},{2,0},{3,1},{4,6},{5,7},{6,4},{7,5},{8,10},{9,11},{10,... | collective-permute-start | bytes 829448 | tf_op jit(solution)/shard_map/ppermute | solution.py:478
  266.8 4.2 %collective-permute-done.24.refs_5_ = bf16[1,144,384]{2,1,0:T(8,128)(2,1)S(1)} collective-permute-done((bf16[1,144,384]{2,1,0:T(8,128)(2,1)S(1)}, bf16[1,144,384]{2,1,0:T(8,128)(2,1)S(1)}, u32[]{:S(2)}, u32[]{:S(2)}) %collective-permute-start.24) | collective-permute-done | bytes 110624 | tf_op jit(solution)/shard_map/ppermute | solution.py:478
  271.1 1.4 collective-permute-done.23.refs_4_
  273.4 2.9 collective-permute-start.26
  276.4 10.7 %collective-permute-done.27.refs_5_ = bf16[1,72,384]{2,1,0:T(8,128)(2,1)S(1)} collective-permute-done((bf16[1,72,384]{2,1,0:T(8,128)(2,1)S(1)}, bf16[1,72,384]{2,1,0:T(8,128)(2,1)S(1)}, u32[]{:S(2)}, u32[]{:S(2)}) %collective-permute-start.27) | collective-permute-done | bytes 55328 | tf_op jit(solution)/shard_map/ppermute | solution.py:478
  288.3 1.2 pad_maximum_fusion
  289.5 1.3 assemble.3
  290.9 1.3 assemble.2
  (109 shorter events, 25.3 us)
Async XLA Ops:
  3.4 6.5 %copy-start.27 = (f32[2,6,1152]{2,0,1:T(2,128)S(1)}, f32[2,6,1152]{2,0,1:T(2,128)}, u32[]{:S(2)}) copy-start(f32[2,6,1152]{2,0,1:T(2,128)} %param.19) | copy-start | bytes 165892
  3.4 26.4 %all-to-all-start = ((bf16[8,40,1152]{2,1,0:T(8,128)(2,1)}), bf16[8,40,1152]{2,1,0:T(8,128)(2,1)S(1)}, u32[]{:S(2)}, u32[]{:S(2)}) async-start(bf16[8,40,1152]{2,1,0:T(8,128)(2,1)} %split.1.refs_0_), calls=%async_computation | async-start | bytes 1474560 | tf_op jit(solution)/shard_map/all_to_all | solution.py:587
  22.3 94.3 %collective-permute-start = (bf16[288,2304]{1,0:T(8,128)(2,1)}, bf16[288,2304]{1,0:T(8,128)(2,1)S(1)}, u32[]{:S(2)}, u32[]{:S(2)}) collective-permute-start(bf16[288,2304]{1,0:T(8,128)(2,1)} %get-tuple-element.85.refs_0_), channel_id=1, source_target_pairs={{0,1},{1,0},{2,3},{3,2},{4,5},{5,4},{6,7},{7,6},{8,9},{9,8},{10,11... | collective-permute-start | bytes 3981320 | tf_op jit(solution)/shard_map/ppermute | solution.py:478
  29.8 3.8 %copy-start.24 = (bf16[8,40,1152]{2,1,0:T(8,128)(2,1)}, bf16[8,40,1152]{2,1,0:T(8,128)(2,1)S(1)}, u32[]{:S(2)}) copy-start(bf16[8,40,1152]{2,1,0:T(8,128)(2,1)S(1)} %all-to-all-done.refs_1_.cot_ref) | copy-start | bytes 2211844
  29.8 23.6 %all-to-all-start.2 = ((bf16[8,40,1152]{2,1,0:T(8,128)(2,1)}), bf16[8,40,1152]{2,1,0:T(8,128)(2,1)S(1)}, u32[]{:S(2)}, u32[]{:S(2)}) async-start(bf16[8,40,1152]{2,1,0:T(8,128)(2,1)} %get-tuple-element.80), calls=%async_computation.2 | async-start | bytes 1474560 | tf_op jit(solution)/shard_map/all_to_all | solution.py:587
  54.3 36.3 %all-to-all-start.1 = ((bf16[8,72,1152]{2,1,0:T(8,128)(2,1)}), bf16[8,72,1152]{2,1,0:T(8,128)(2,1)S(1)}, u32[]{:S(2)}, u32[]{:S(2)}) async-start(bf16[8,72,1152]{2,1,0:T(8,128)(2,1)} %get-tuple-element.79), calls=%async_computation.1 | async-start | bytes 2654208 | tf_op jit(solution)/shard_map/all_to_all | solution.py:587
  78.7 55.4 %collective-permute-start.2 = (bf16[288,2304]{1,0:T(8,128)(2,1)}, bf16[288,2304]{1,0:T(8,128)(2,1)}, u32[]{:S(2)}, u32[]{:S(2)}) collective-permute-start(bf16[288,2304]{1,0:T(8,128)(2,1)} %get-tuple-element.93.refs_0_), channel_id=1, source_target_pairs={{0,1},{1,0},{2,3},{3,2},{4,5},{5,4},{6,7},{7,6},{8,9},{9,8},{10,11... | collective-permute-start | bytes 3981320 | tf_op jit(solution)/shard_map/ppermute | solution.py:478
  79.2 55.5 %collective-permute-start.4 = (bf16[288,2304]{1,0:T(8,128)(2,1)}, bf16[288,2304]{1,0:T(8,128)(2,1)}, u32[]{:S(2)}, u32[]{:S(2)}) collective-permute-start(bf16[288,2304]{1,0:T(8,128)(2,1)} %get-tuple-element.95), channel_id=1, source_target_pairs={{0,1},{1,0},{2,3},{3,2},{4,5},{5,4},{6,7},{7,6},{8,9},{9,8},{10,11... | collective-permute-start | bytes 3981320 | tf_op jit(solution)/shard_map/ppermute | solution.py:478
  79.3 79.6 %collective-permute-start.1 = (bf16[288,2304]{1,0:T(8,128)(2,1)}, bf16[288,2304]{1,0:T(8,128)(2,1)}, u32[]{:S(2)}, u32[]{:S(2)}) collective-permute-start(bf16[288,2304]{1,0:T(8,128)(2,1)} %get-tuple-element.86.refs_1_), channel_id=1, source_target_pairs={{0,1},{1,0},{2,3},{3,2},{4,5},{5,4},{6,7},{7,6},{8,9},{9,8},{10,11... | collective-permute-start | bytes 3981320 | tf_op jit(solution)/shard_map/ppermute | solution.py:478
  90.6 4.0 %copy-start.22 = (bf16[8,72,1152]{2,1,0:T(8,128)(2,1)}, bf16[8,72,1152]{2,1,0:T(8,128)(2,1)S(1)}, u32[]{:S(2)}) copy-start(bf16[8,72,1152]{2,1,0:T(8,128)(2,1)S(1)} %all-to-all-done.1.middle_ref.cot_ref) | copy-start | bytes 3981316
  90.6 26.2 %all-to-all-start.4 = ((bf16[8,40,1152]{2,1,0:T(8,128)(2,1)}), bf16[8,40,1152]{2,1,0:T(8,128)(2,1)S(1)}, u32[]{:S(2)}, u32[]{:S(2)}) async-start(bf16[8,40,1152]{2,1,0:T(8,128)(2,1)} %get-tuple-element.87), calls=%async_computation.4 | async-start | bytes 1474560 | tf_op jit(solution)/shard_map/all_to_all | solution.py:587
  116.1 18.6 %collective-permute-start.3 = (bf16[288,2304]{1,0:T(8,128)(2,1)}, bf16[288,2304]{1,0:T(8,128)(2,1)S(1)}, u32[]{:S(2)}, u32[]{:S(2)}) collective-permute-start(bf16[288,2304]{1,0:T(8,128)(2,1)} %get-tuple-element.94.refs_1_), channel_id=1, source_target_pairs={{0,1},{1,0},{2,3},{3,2},{4,5},{5,4},{6,7},{7,6},{8,9},{9,8},{10,11... | collective-permute-start | bytes 3981320 | tf_op jit(solution)/shard_map/ppermute | solution.py:478
  116.6 18.1 %collective-permute-start.5 = (bf16[288,2304]{1,0:T(8,128)(2,1)}, bf16[288,2304]{1,0:T(8,128)(2,1)}, u32[]{:S(2)}, u32[]{:S(2)}) collective-permute-start(bf16[288,2304]{1,0:T(8,128)(2,1)} %get-tuple-element.96), channel_id=1, source_target_pairs={{0,1},{1,0},{2,3},{3,2},{4,5},{5,4},{6,7},{7,6},{8,9},{9,8},{10,11... | collective-permute-start | bytes 3981320 | tf_op jit(solution)/shard_map/ppermute | solution.py:478
  116.7 6.0 %copy-start.25 = (bf16[8,40,1152]{2,1,0:T(8,128)(2,1)}, bf16[8,40,1152]{2,1,0:T(8,128)(2,1)S(1)}, u32[]{:S(2)}) copy-start(bf16[8,40,1152]{2,1,0:T(8,128)(2,1)S(1)} %all-to-all-done.4.up_ref) | copy-start | bytes 2211844
  117.7 35.6 %all-to-all-start.5 = ((bf16[8,40,1152]{2,1,0:T(8,128)(2,1)}), bf16[8,40,1152]{2,1,0:T(8,128)(2,1)S(1)}, u32[]{:S(2)}, u32[]{:S(2)}) async-start(bf16[8,40,1152]{2,1,0:T(8,128)(2,1)} %get-tuple-element.91), calls=%async_computation.5 | async-start | bytes 1474560 | tf_op jit(solution)/shard_map/all_to_all | solution.py:587
  134.1 56.6 %collective-permute-start.6 = (bf16[288,2304]{1,0:T(8,128)(2,1)}, bf16[288,2304]{1,0:T(8,128)(2,1)}, u32[]{:S(2)}, u32[]{:S(2)}) collective-permute-start(bf16[288,2304]{1,0:T(8,128)(2,1)} %get-tuple-element.99), channel_id=1, source_target_pairs={{0,1},{1,0},{2,3},{3,2},{4,5},{5,4},{6,7},{7,6},{8,9},{9,8},{10,11... | collective-permute-start | bytes 3981320 | tf_op jit(solution)/shard_map/ppermute | solution.py:478
  150.2 31.3 %collective-permute-start.8 = (bf16[2,288,1152]{2,1,0:T(8,128)(2,1)}, bf16[2,288,1152]{2,1,0:T(8,128)(2,1)S(1)}, u32[]{:S(2)}, u32[]{:S(2)}) collective-permute-start(bf16[2,288,1152]{2,1,0:T(8,128)(2,1)} %get-tuple-element.102), channel_id=1, source_target_pairs={{0,8},{8,0},{16,24},{24,16},{1,9},{9,1},{17,25},{25,17},{2,10},{10... | collective-permute-start | bytes 3981320 | tf_op jit(solution)/shard_map/ppermute | solution.py:478
  151.7 31.1 %collective-permute-start.9 = (bf16[1,576,1152]{2,1,0:T(8,128)(2,1)}, bf16[1,576,1152]{2,1,0:T(8,128)(2,1)}, u32[]{:S(2)}, u32[]{:S(2)}) collective-permute-start(bf16[1,576,1152]{2,1,0:T(8,128)(2,1)} %get-tuple-element.103), channel_id=1, source_target_pairs={{0,16},{8,24},{16,0},{24,8},{1,17},{9,25},{17,1},{25,9},{2,18},{10... | collective-permute-start | bytes 3981320 | tf_op jit(solution)/shard_map/ppermute | solution.py:478
  154.1 55.2 %all-to-all-start.3 = ((bf16[8,72,1152]{2,1,0:T(8,128)(2,1)}), bf16[8,72,1152]{2,1,0:T(8,128)(2,1)S(1)}, u32[]{:S(2)}, u32[]{:S(2)}) async-start(bf16[8,72,1152]{2,1,0:T(8,128)(2,1)} %get-tuple-element.84), calls=%async_computation.3 | async-start | bytes 2654208 | tf_op jit(solution)/shard_map/all_to_all | solution.py:587
  170.6 20.1 %collective-permute-start.7 = (bf16[288,2304]{1,0:T(8,128)(2,1)}, bf16[288,2304]{1,0:T(8,128)(2,1)}, u32[]{:S(2)}, u32[]{:S(2)}) collective-permute-start(bf16[288,2304]{1,0:T(8,128)(2,1)} %get-tuple-element.100), channel_id=1, source_target_pairs={{0,1},{1,0},{2,3},{3,2},{4,5},{5,4},{6,7},{7,6},{8,9},{9,8},{10,11... | collective-permute-start | bytes 3981320 | tf_op jit(solution)/shard_map/ppermute | solution.py:478
  171.2 11.7 %copy-start.6 = (s32[2]{0:T(128)S(1)}, s32[2]{0:T(128)}, u32[]{:S(2)}) copy-start(s32[2]{0:T(128)} %pad_add_fusion.core_ref.others_ref.place_ref) | copy-start | bytes 28
  171.2 11.7 %copy-start.8 = (bf16[2,288,1152]{2,1,0:T(8,128)(2,1)S(1)}, bf16[2,288,1152]{2,1,0:T(8,128)(2,1)}, u32[]{:S(2)}) copy-start(bf16[2,288,1152]{2,1,0:T(8,128)(2,1)} %get-tuple-element.97.refs_0_) | copy-start | bytes 3981316
  171.2 11.7 %copy-start.9 = (bf16[1,576,1152]{2,1,0:T(8,128)(2,1)S(1)}, bf16[1,576,1152]{2,1,0:T(8,128)(2,1)}, u32[]{:S(2)}) copy-start(bf16[1,576,1152]{2,1,0:T(8,128)(2,1)} %get-tuple-element.101.refs_1_) | copy-start | bytes 3981316
  188.7 20.6 %collective-permute-start.13 = (bf16[1,288,1152]{2,1,0:T(8,128)(2,1)}, bf16[1,288,1152]{2,1,0:T(8,128)(2,1)S(1)}, u32[]{:S(2)}, u32[]{:S(2)}) collective-permute-start(bf16[1,288,1152]{2,1,0:T(8,128)(2,1)} %get-tuple-element.113), channel_id=1, source_target_pairs={{0,16},{8,24},{16,0},{24,8},{1,17},{9,25},{17,1},{25,9},{2,18},{10... | collective-permute-start | bytes 1990664 | tf_op jit(solution)/shard_map/ppermute | solution.py:478
  190.2 19.1 %collective-permute-start.14 = (bf16[1,288,1152]{2,1,0:T(8,128)(2,1)}, bf16[1,288,1152]{2,1,0:T(8,128)(2,1)}, u32[]{:S(2)}, u32[]{:S(2)}) collective-permute-start(bf16[1,288,1152]{2,1,0:T(8,128)(2,1)} %get-tuple-element.114), channel_id=1, source_target_pairs={{0,8},{8,0},{16,24},{24,16},{1,9},{9,1},{17,25},{25,17},{2,10},{10... | collective-permute-start | bytes 1990664 | tf_op jit(solution)/shard_map/ppermute | solution.py:478
  190.7 18.6 %copy-start.7 = (s32[2]{0:T(128)S(1)}, s32[2]{0:T(128)}, u32[]{:S(2)}) copy-start(s32[2]{0:T(128)} %pad_add_fusion.core_ref.others_ref.place_ref) | copy-start | bytes 28
  205.2 28.8 %collective-permute-start.10 = (bf16[2,288,960]{2,1,0:T(8,128)(2,1)}, bf16[2,288,960]{2,1,0:T(8,128)(2,1)S(1)}, u32[]{:S(2)}, u32[]{:S(2)}) collective-permute-start(bf16[2,288,960]{2,1,0:T(8,128)(2,1)} %get-tuple-element.109), channel_id=1, source_target_pairs={{0,8},{8,0},{16,24},{24,16},{1,9},{9,1},{17,25},{25,17},{2,10},{10... | collective-permute-start | bytes 3317768 | tf_op jit(solution)/shard_map/ppermute | solution.py:478
  206.8 27.3 %collective-permute-start.11 = (bf16[1,576,960]{2,1,0:T(8,128)(2,1)}, bf16[1,576,960]{2,1,0:T(8,128)(2,1)}, u32[]{:S(2)}, u32[]{:S(2)}) collective-permute-start(bf16[1,576,960]{2,1,0:T(8,128)(2,1)} %get-tuple-element.110), channel_id=1, source_target_pairs={{0,16},{8,24},{16,0},{24,8},{1,17},{9,25},{17,1},{25,9},{2,18},{10... | collective-permute-start | bytes 3317768 | tf_op jit(solution)/shard_map/ppermute | solution.py:478
  207.3 26.7 %collective-permute-start.12 = (bf16[8,72,384]{2,1,0:T(8,128)(2,1)}, bf16[8,72,384]{2,1,0:T(8,128)(2,1)}, u32[]{:S(2)}, u32[]{:S(2)}) collective-permute-start(bf16[8,72,384]{2,1,0:T(8,128)(2,1)} %get-tuple-element.111), channel_id=1, source_target_pairs={{0,2},{1,3},{2,0},{3,1},{4,6},{5,7},{6,4},{7,5},{8,10},{9,11},{10,... | collective-permute-start | bytes 1327112 | tf_op jit(solution)/shard_map/ppermute | solution.py:478
  209.3 5.5 %copy-start = (bf16[8,72,1152]{2,1,0:T(8,128)(2,1)}, bf16[8,72,1152]{2,1,0:T(8,128)(2,1)S(1)}, u32[]{:S(2)}) copy-start(bf16[8,72,1152]{2,1,0:T(8,128)(2,1)S(1)} %all-to-all-done.3.refs_5_.pieces_ref) | copy-start | bytes 3981316
  209.3 1.7 copy-start.10
  215.5 11.7 %collective-permute-start.15 = (bf16[2,72,1152]{2,1,0:T(8,128)(2,1)S(1)}, bf16[2,72,1152]{2,1,0:T(8,128)(2,1)S(1)}, u32[]{:S(2)}, u32[]{:S(2)}) collective-permute-start(bf16[2,72,1152]{2,1,0:T(8,128)(2,1)S(1)} %get-tuple-element.117), channel_id=1, source_target_pairs={{0,2},{1,3},{2,0},{3,1},{4,6},{5,7},{6,4},{7,5},{8,10},{9,11},{10,... | collective-permute-start | bytes 995336 | tf_op jit(solution)/shard_map/ppermute | solution.py:478
  215.5 16.6 %collective-permute-start.16 = (bf16[2,72,1152]{2,1,0:T(8,128)(2,1)S(1)}, bf16[2,72,1152]{2,1,0:T(8,128)(2,1)S(1)}, u32[]{:S(2)}, u32[]{:S(2)}) collective-permute-start(bf16[2,72,1152]{2,1,0:T(8,128)(2,1)S(1)} %get-tuple-element.118), channel_id=1, source_target_pairs={{0,2},{1,3},{2,0},{3,1},{4,6},{5,7},{6,4},{7,5},{8,10},{9,11},{10,... | collective-permute-start | bytes 995336 | tf_op jit(solution)/shard_map/ppermute | solution.py:478
  217.5 14.6 %copy-start.21 = (bf16[2,72,1152]{2,1,0:T(8,128)(2,1)S(1)}, bf16[2,72,1152]{2,1,0:T(8,128)(2,1)}, u32[]{:S(2)}) copy-start(bf16[2,72,1152]{2,1,0:T(8,128)(2,1)} %copy-done.20) | copy-start | bytes 995332
  238.8 20.9 %collective-permute-start.17 = (bf16[1,288,960]{2,1,0:T(8,128)(2,1)S(1)}, bf16[1,288,960]{2,1,0:T(8,128)(2,1)S(1)}, u32[]{:S(2)}, u32[]{:S(2)}) collective-permute-start(bf16[1,288,960]{2,1,0:T(8,128)(2,1)S(1)} %get-tuple-element.124), channel_id=1, source_target_pairs={{0,16},{8,24},{16,0},{24,8},{1,17},{9,25},{17,1},{25,9},{2,18},{10... | collective-permute-start | bytes 1658888 | tf_op jit(solution)/shard_map/ppermute | solution.py:478
  240.3 20.4 %collective-permute-start.18 = (bf16[4,72,960]{2,1,0:T(8,128)(2,1)S(1)}, bf16[4,72,960]{2,1,0:T(8,128)(2,1)S(1)}, u32[]{:S(2)}, u32[]{:S(2)}) collective-permute-start(bf16[4,72,960]{2,1,0:T(8,128)(2,1)S(1)} %get-tuple-element.125), channel_id=1, source_target_pairs={{0,2},{1,3},{2,0},{3,1},{4,6},{5,7},{6,4},{7,5},{8,10},{9,11},{10,... | collective-permute-start | bytes 1658888 | tf_op jit(solution)/shard_map/ppermute | solution.py:478
  242.0 15.1 %collective-permute-start.20 = (bf16[1,72,1152]{2,1,0:T(8,128)(2,1)S(1)}, bf16[1,72,1152]{2,1,0:T(8,128)(2,1)S(1)}, u32[]{:S(2)}, u32[]{:S(2)}) collective-permute-start(bf16[1,72,1152]{2,1,0:T(8,128)(2,1)S(1)} %get-tuple-element.128), channel_id=1, source_target_pairs={{0,4},{1,5},{2,6},{3,7},{4,0},{5,1},{6,2},{7,3},{8,12},{9,13},{10,... | collective-permute-start | bytes 497672 | tf_op jit(solution)/shard_map/ppermute | solution.py:478
  244.4 14.5 %collective-permute-start.21 = (bf16[1,72,1152]{2,1,0:T(8,128)(2,1)S(1)}, bf16[1,72,1152]{2,1,0:T(8,128)(2,1)S(1)}, u32[]{:S(2)}, u32[]{:S(2)}) collective-permute-start(bf16[1,72,1152]{2,1,0:T(8,128)(2,1)S(1)} %get-tuple-element.129), channel_id=1, source_target_pairs={{0,4},{1,5},{2,6},{3,7},{4,0},{5,1},{6,2},{7,3},{8,12},{9,13},{10,... | collective-permute-start | bytes 497672 | tf_op jit(solution)/shard_map/ppermute | solution.py:478
  244.9 14.7 %collective-permute-start.19 = (bf16[2,144,384]{2,1,0:T(8,128)(2,1)S(1)}, bf16[2,144,384]{2,1,0:T(8,128)(2,1)S(1)}, u32[]{:S(2)}, u32[]{:S(2)}) collective-permute-start(bf16[2,144,384]{2,1,0:T(8,128)(2,1)S(1)} %get-tuple-element.126), channel_id=1, source_target_pairs={{0,8},{8,0},{16,24},{24,16},{1,9},{9,1},{17,25},{25,17},{2,10},{10... | collective-permute-start | bytes 663560 | tf_op jit(solution)/shard_map/ppermute | solution.py:478
  245.5 13.4 %copy-start.18 = (bf16[1,288,960]{2,1,0:T(8,128)(2,1)S(1)}, bf16[1,288,960]{2,1,0:T(8,128)(2,1)}, u32[]{:S(2)}) copy-start(bf16[1,288,960]{2,1,0:T(8,128)(2,1)} %copy-done.17) | copy-start | bytes 1658884
  261.9 9.1 %collective-permute-start.22 = (bf16[2,72,960]{2,1,0:T(8,128)(2,1)S(1)}, bf16[2,72,960]{2,1,0:T(8,128)(2,1)S(1)}, u32[]{:S(2)}, u32[]{:S(2)}) collective-permute-start(bf16[2,72,960]{2,1,0:T(8,128)(2,1)S(1)} %get-tuple-element.134), channel_id=1, source_target_pairs={{0,2},{1,3},{2,0},{3,1},{4,6},{5,7},{6,4},{7,5},{8,10},{9,11},{10,... | collective-permute-start | bytes 829448 | tf_op jit(solution)/shard_map/ppermute | solution.py:478
  265.7 6.7 %collective-permute-start.23 = (bf16[1,144,960]{2,1,0:T(8,128)(2,1)S(1)}, bf16[1,144,960]{2,1,0:T(8,128)(2,1)S(1)}, u32[]{:S(2)}, u32[]{:S(2)}) collective-permute-start(bf16[1,144,960]{2,1,0:T(8,128)(2,1)S(1)} %get-tuple-element.135), channel_id=1, source_target_pairs={{0,8},{8,0},{16,24},{24,16},{1,9},{9,1},{17,25},{25,17},{2,10},{10... | collective-permute-start | bytes 829448 | tf_op jit(solution)/shard_map/ppermute | solution.py:478
  266.3 4.7 %collective-permute-start.24 = (bf16[1,144,384]{2,1,0:T(8,128)(2,1)S(1)}, bf16[1,144,384]{2,1,0:T(8,128)(2,1)S(1)}, u32[]{:S(2)}, u32[]{:S(2)}) collective-permute-start(bf16[1,144,384]{2,1,0:T(8,128)(2,1)S(1)} %get-tuple-element.136), channel_id=1, source_target_pairs={{0,16},{8,24},{16,0},{24,8},{1,17},{9,25},{17,1},{25,9},{2,18},{10... | collective-permute-start | bytes 331784 | tf_op jit(solution)/shard_map/ppermute | solution.py:478
  273.3 13.7 %collective-permute-start.25 = (bf16[1,72,960]{2,1,0:T(8,128)(2,1)S(1)}, bf16[1,72,960]{2,1,0:T(8,128)(2,1)S(1)}, u32[]{:S(2)}, u32[]{:S(2)}) collective-permute-start(bf16[1,72,960]{2,1,0:T(8,128)(2,1)S(1)} %get-tuple-element.140), channel_id=1, source_target_pairs={{0,4},{1,5},{2,6},{3,7},{4,0},{5,1},{6,2},{7,3},{8,12},{9,13},{10,... | collective-permute-start | bytes 414728 | tf_op jit(solution)/shard_map/ppermute | solution.py:478
  273.4 13.7 %collective-permute-start.26 = (bf16[1,72,960]{2,1,0:T(8,128)(2,1)S(1)}, bf16[1,72,960]{2,1,0:T(8,128)(2,1)S(1)}, u32[]{:S(2)}, u32[]{:S(2)}) collective-permute-start(bf16[1,72,960]{2,1,0:T(8,128)(2,1)S(1)} %get-tuple-element.141), channel_id=1, source_target_pairs={{0,4},{1,5},{2,6},{3,7},{4,0},{5,1},{6,2},{7,3},{8,12},{9,13},{10,... | collective-permute-start | bytes 414728 | tf_op jit(solution)/shard_map/ppermute | solution.py:478
  276.3 10.7 %collective-permute-start.27 = (bf16[1,72,384]{2,1,0:T(8,128)(2,1)S(1)}, bf16[1,72,384]{2,1,0:T(8,128)(2,1)S(1)}, u32[]{:S(2)}, u32[]{:S(2)}) collective-permute-start(bf16[1,72,384]{2,1,0:T(8,128)(2,1)S(1)} %get-tuple-element.142), channel_id=1, source_target_pairs={{0,4},{1,5},{2,6},{3,7},{4,0},{5,1},{6,2},{7,3},{8,12},{9,13},{10,... | collective-permute-start | bytes 165896 | tf_op jit(solution)/shard_map/ppermute | solution.py:478
  276.4 13.2 %collective-permute-start.29 = (bf16[36,2304]{1,0:T(8,128)(2,1)S(1)}, bf16[36,2304]{1,0:T(8,128)(2,1)S(1)}, u32[]{:S(2)}, u32[]{:S(2)}) collective-permute-start(bf16[36,2304]{1,0:T(8,128)(2,1)S(1)} %get-tuple-element.147), channel_id=1, source_target_pairs={{0,1},{1,0},{2,3},{3,2},{4,5},{5,4},{6,7},{7,6},{8,9},{9,8},{10,11... | collective-permute-start | bytes 497672 | tf_op jit(solution)/shard_map/ppermute | solution.py:478
  287.8 3.0 %collective-permute-start.28 = (bf16[36,2304]{1,0:T(8,128)(2,1)S(1)}, bf16[36,2304]{1,0:T(8,128)(2,1)S(1)}, u32[]{:S(2)}, u32[]{:S(2)}) collective-permute-start(bf16[36,2304]{1,0:T(8,128)(2,1)S(1)} %get-tuple-element.144), channel_id=1, source_target_pairs={{0,1},{1,0},{2,3},{3,2},{4,5},{5,4},{6,7},{7,6},{8,9},{9,8},{10,11... | collective-permute-start | bytes 497672 | tf_op jit(solution)/shard_map/ppermute | solution.py:478
  (18 other events, 20.2 us)

commit v2 on v1

--- a/solution.py
+++ b/solution.py
@@ -11,6 +11,7 @@
 HEADS = 16
 NORM_EPSILON = 1e-06
 MASKED = -1e30
+TOKEN = jax.ShapeDtypeStruct((8, 128), jnp.float32)
 LOG2_E = 1.4426950408889634
 MIB = 1024 * 1024
 F32 = jnp.float32
@@ -27,22 +28,24 @@
 
 ROOM = {
     "split": 56, "space_forward": 56, "time": 56, "weights": 56, "space_backward": 56,
-    "grad_input": 56, "stage": 16, "core_stage": 16, "assemble": 16, "join": 56,
+    "grad_input": 56, "stage": 24, "last_stage": 16, "assemble": 16, "join": 56,
 }
-SPACES = {"v": pltpu.VMEM, "s": pltpu.SMEM, "a": pl.ANY}
+SPACES = {"v": pltpu.VMEM, "s": pltpu.SMEM, "a": pl.ANY, "h": pltpu.HBM}
 
 
 def call(name, us, body, ins, out_shape, outs, scratch=()):
     def run(*operands, deps=()):
+        before = len(operands) + len(deps) + len(out_shape)
+
+        def with_token(*refs):
+            refs[before][...] = jnp.zeros(TOKEN.shape, TOKEN.dtype)
+            body(*refs[:before], *refs[before + 1 :])
+
         return pl.pallas_call(
-            body,
-            out_shape=out_shape,
+            with_token,
+            out_shape=(*out_shape, TOKEN),
             in_specs=[pl.BlockSpec(memory_space=SPACES[s]) for s in ins + "a" * len(deps)],
-            out_specs=(
-                tuple(pl.BlockSpec(memory_space=SPACES[s]) for s in outs)
-                if isinstance(out_shape, tuple)
-                else pl.BlockSpec(memory_space=SPACES[outs])
-            ),
+            out_specs=tuple(pl.BlockSpec(memory_space=SPACES[s]) for s in outs + "v"),
             scratch_shapes=list(scratch),
             compiler_params=pltpu.CompilerParams(vmem_limit_bytes=ROOM[name] * MIB),
             cost_estimate=pl.CostEstimate(
@@ -160,9 +163,13 @@
 
 
 def join_kernel(pieces_ref, gather_ref, *refs):
-    out_ref = refs[-1]
+    *grads, out_ref, grad_out, sems = refs
+    copies = Copies(sems)
+    stores = [copies.start(grads[v], grad_out.at[v]) for v in range(grad_out.shape[0])]
     rows = dot(gather_ref[...], frame_rows(pieces_ref[...])).astype(BF16)
     out_ref[...] = rows.reshape(out_ref.shape)
+    for store in stores:
+        store.wait()
 
 
 def space_forward_kernel(
@@ -398,8 +405,8 @@
     copies = Copies(sems)
     core = place_ref[1] & 1
     own = pl.multiple_of(core * (2 * width), 128)
-    waits = []
-    for unit in range(2):
+
+    def load(unit):
         now = []
         at = pl.ds(unit * width, width)
         mine = pl.ds(pl.multiple_of(own + unit * width, 128), width)
@@ -413,7 +420,9 @@
                 rows = pl.ds((2 * video + place) * tokens, tokens)
                 now.append(copies.start(left.at[:, at], left_rows.at[rows, at]))
                 now.append(copies.start(right.at[:, columns], right_rows.at[rows, at]))
-        waits.append(now)
+        return now
+
+    waits = [load(0)]
     done, stores = 0, []
     for part, ((low, high), (axis, bit, inner)) in enumerate(zip(cuts, steps)):
         for unit in range(2):
@@ -424,6 +433,8 @@
                 for wait in waits[done]:
                     wait.wait()
                 done += 1
+                if done == 1:
+                    waits.append(load(1))
             column = pl.multiple_of(core * width, 128) if unit else 0
             left = left_rows[:, pl.ds(column, width)]
             total[:, start - low : stop - low] = (
@@ -436,38 +447,56 @@
         store.wait()
 
 
-def stage_kernel(steps, place_ref, *refs):
+def add_got(total, kept, got):
+    each, columns = kept.shape[1:]
+    for outer in range(kept.shape[0]):
+        total[outer * each : (outer + 1) * each, :columns] = kept[outer].astype(F32) + got[
+            outer
+        ].astype(F32)
+
+
+def stage_kernel(steps, loaded, place_ref, *refs):
     count = len(steps)
-    total, outs = refs[-1], refs[-1 - 2 * count : -1]
+    scratch = count + 2 if loaded else 1
+    outs, total = refs[-scratch - 2 * count : -scratch], refs[-scratch]
+    kept = refs[:count]
+    if loaded:
+        copies = Copies(refs[-1])
+        loads = [copies.start(a, b) for a, b in zip(kept, refs[-count - 1 : -1])]
+        kept = refs[-count - 1 : -1]
     for part, (axis, bit, inner) in enumerate(steps):
-        kept, got = refs[part], refs[count + part]
-        each = kept.shape[1]
-        for outer in range(kept.shape[0]):
-            total[outer * each : (outer + 1) * each, : kept.shape[2]] = kept[outer].astype(
-                F32
-            ) + got[outer].astype(F32)
+        if loaded:
+            loads[part].wait()
+        add_got(total, kept[part], refs[count + part])
         emit_halves(
             total, inner, bit_of(place_ref, axis, bit), outs[2 * part], outs[2 * part + 1]
         )
 
 
-def core_stage_kernel(cuts, place_ref, *refs):
-    kept_out, sent_out = refs[-2:]
-    core = place_ref[1] & 1
+def last_stage_kernel(bit, cuts, place_ref, *refs):
+    count = len(cuts)
+    outs, total = refs[-5:-1], refs[-1]
+    rows = outs[0].shape[0]
+    mine, core = bit_of(place_ref, "seq", bit) == 0, (place_ref[1] & 1) == 0
     for part, (start, stop) in enumerate(cuts):
-        total = refs[part][0].astype(F32) + refs[len(cuts) + part][0].astype(F32)
-        rows = total.shape[0] // 2
-        low, high = total[:rows], total[rows:]
-        kept_out[:, start:stop] = jnp.where(core == 0, low, high).astype(BF16)
-        sent_out[:, start:stop] = jnp.where(core == 0, high, low).astype(BF16)
-
-
-def assemble_kernel(place_ref, kept_ref, got_ref, qkv_ref, out_ref):
+        add_got(total, refs[part], refs[count + part])
+        low, high = total[: 2 * rows, : stop - start], total[2 * rows : 4 * rows, : stop - start]
+        near, far = jnp.where(mine, low, high), jnp.where(mine, high, low)
+        for place, half in enumerate((near, far)):
+            first, second = half[:rows], half[rows:]
+            same, other = jnp.where(core, first, second), jnp.where(core, second, first)
+            outs[2 * place][:, start:stop] = same.astype(BF16)
+            outs[2 * place + 1][:, start:stop] = other.astype(BF16)
+
+
+def assemble_kernel(place_ref, *refs):
+    near, far, near_other, far_other = [ref[...].astype(F32) for ref in refs[:4]]
+    qkv_ref, out_ref = refs[-2:]
     width = out_ref.shape[1]
-    core = place_ref[1] & 1
-    kept, got = kept_ref[...].astype(F32), got_ref[...].astype(F32)
-    low = jnp.where(core == 0, kept, got).astype(BF16)
-    high = jnp.where(core == 0, got, kept).astype(BF16)
+    core = (place_ref[1] & 1) == 0
+    mine, others = near + far, near_other + far_other
+    low = jnp.where(core, mine, others).astype(BF16)
+    high = jnp.where(core, others, mine).astype(BF16)
     qkv_ref[:, : 2 * width] = low
     qkv_ref[:, 2 * width :] = high[:, :width]
     out_ref[...] = high[:, width:]
@@ -520,32 +549,41 @@
 
     def stage(self, deps=()):
         steps, shapes = self.next_steps()
-        halves = call(
-            "stage", 2, functools.partial(stage_kernel, steps), "s" + "v" * len(shapes), shapes,
-            "v" * len(shapes),
-            [pltpu.VMEM((self.width >> self.step, self.columns), F32)],
+        loaded = self.step == 1
+        scratch = [pltpu.VMEM((self.width >> self.step, self.columns), F32)]
+        if loaded:
+            scratch += [pltpu.VMEM(half.shape, BF16) for half in self.kept]
+            scratch += [pltpu.SemaphoreType.DMA((self.parts,))]
+        *halves, token = call(
+            "stage", 2, functools.partial(stage_kernel, steps, loaded),
+            "s" + ("h" if loaded else "v") * self.parts + "v" * self.parts, shapes,
+            "v" * len(shapes), scratch,
         )(self.place, *self.kept, *self.got, deps=deps)
         self.send(halves)
-        return halves[0]
-
-    def core_stage(self, deps=()):
-        while self.step < len(self.bits):
+        return token
+
+    def last_stage(self, deps=()):
+        while self.step < len(self.bits) - 1:
             self.stage()
+        bit = self.orders[0][-1][1]
         rows = self.width >> (len(self.bits) + 1)
-        half = shaped(rows, 2 * self.width)
-        self.mine, sent = call(
-            "core_stage", 1, functools.partial(core_stage_kernel, self.cuts),
-            "s" + "v" * (2 * self.parts), (half, half), "vv",
+        near, near_other, far, far_other, token = call(
+            "last_stage", 1, functools.partial(last_stage_kernel, bit, self.cuts),
+            "s" + "v" * (2 * self.parts), (shaped(rows, 2 * self.width),) * 4, "vvvv",
+            [pltpu.VMEM((4 * rows, self.columns), F32)],
         )(self.place, *self.kept, *self.got, deps=deps)
-        self.other = swap(sent, "seq", 1)
-        return self.mine
-
-    def finish(self):
-        rows = self.mine.shape[0]
+        self.sums = (
+            near, swap(far, "seq", 1 << bit), swap(near_other, "seq", 1),
+            swap(far_other, "seq", (1 << bit) | 1),
+        )
+        return token
+
+    def finish(self, deps=()):
+        rows = self.sums[0].shape[0]
         return call(
-            "assemble", 1, assemble_kernel, "svv",
+            "assemble", 1, assemble_kernel, "svvvv",
             (shaped(rows, 3 * self.width), shaped(rows, self.width)), "vv",
-        )(self.place, self.mine, self.other)
+        )(self.place, *self.sums, deps=deps)
 
 
 def shards(frames_in, modulation, spatial_qkv, spatial_out, temporal_qkv, temporal_out, cotangent):
@@ -606,14 +644,14 @@
     def exchange_units(units):
         return swap(units, "seq", 1)
 
-    cot_sent = call("split", 3, functools.partial(split_kernel, n), "vv", piece, "v")(
+    cot_sent, token = call("split", 3, functools.partial(split_kernel, n), "vv", (piece,), "v")(
         cot, to_pieces
     )
     cot_pieces = exchange(cot_sent)
-    deps = [cot_sent]
+    deps = [token]
     saved, arrived = [], []
     for v in range(videos):
-        sent, *keep = call(
+        sent, *keep, token = call(
             "space_forward", 14, functools.partial(space_forward_kernel, n, patches, v),
             "aavaavv",
             (joint_piece if v else piece, three, two, shaped(*weights_shape)),
@@ -627,13 +665,13 @@
             x, cot, modulation, spatial_qkv, spatial_out, to_joint[0] if v else to_pieces,
             to_joint[1], deps=deps,
         )
-        deps = [keep[0], cot_pieces]
+        deps = [token, cot_pieces]
         arrived.append(exchange(sent))
         saved.append((*keep, exchange_units(keep[1])))
 
     returned, time_units, out_sent = [], [], core
     for v in range(videos):
-        d_middle, out_sent, left, sent, right = call(
+        d_middle, out_sent, left, sent, right, token = call(
             "time", 25, functools.partial(time_kernel, n, time_block, all_frames, v),
             "svvvaavvvv" + ("v" if v else "a"),
             (piece, joint_piece, two, two, four),
@@ -651,7 +689,7 @@
             joint_by_patch[1] if v else by_patch, from_patch, joint_from_patch[v], out_sent,
             deps=deps,
         )
-        deps = [right]
+        deps = [token]
         returned.append(exchange(d_middle))
         time_units.append((left, exchange_units(left), right, exchange_units(sent)))
 
@@ -661,7 +699,7 @@
         reduction = Reduction(core, width, late)
         steps, shapes = reduction.next_steps()
         operands = [one for kind in zip(*units) for one in kind]
-        halves = call(
+        *halves, token = call(
             "weights", 10,
             functools.partial(weight_kernel, videos, reduction.cuts, steps, grad_scale),
             "s" + "a" * (4 * videos), shapes, "a" * len(shapes),
@@ -671,18 +709,18 @@
             ],
         )(core, *operands, deps=deps)
         reduction.send(halves)
-        return reduction, halves[0]
+        return reduction, token
 
     def grad_of(video, units, d_middle, deps=()):
         return call(
-            "grad_input", 8, functools.partial(grad_input_kernel, video), "avvva", row, "v",
+            "grad_input", 8, functools.partial(grad_input_kernel, video), "avvva", (row,), "v",
             [vmem(tokens, 3 * width), vmem(width, 3 * width), sems(6)],
         )(units[2], d_middle, x, modulation, spatial_qkv, deps=deps)
 
-    d_middles, space_units, grad_input = [], [], []
+    d_middles, space_units = [], []
     for v in range(videos):
         packed, left, weights_saved, left_got = saved[v]
-        d_middle, sent, right = call(
+        d_middle, sent, right, token = call(
             "space_backward", 15, functools.partial(space_backward_kernel, patches, v),
             "svvavav",
             (row, two, four),
@@ -697,26 +735,28 @@
             deps=[*deps, left_got],
         )
         if v == 0:
-            time_sum, began = weights(time_units, False, deps=[right])
+            time_sum, began = weights(time_units, False, deps=[token])
             deps = [began]
             out_back = exchange(out_sent)
         d_middles.append(d_middle)
         space_units.append((left, left_got, right, exchange_units(sent)))
-    grad_input.append(grad_of(0, space_units[0], d_middles[0], deps=[right]))
-    began = time_sum.stage(deps=grad_input)
-    space_sum, began = weights(space_units, True, deps=[began])
-    began = time_sum.stage(deps=[began, out_back])
+    first_grad, token = grad_of(0, space_units[0], d_middles[0], deps=[token])
+    grad_input = [first_grad]
+    token = time_sum.stage(deps=[token])
+    space_sum, token = weights(space_units, True, deps=[token])
+    token = time_sum.stage(deps=[token, out_back])
     for v in range(1, videos):
-        grad_input.append(grad_of(v, space_units[v], d_middles[v], deps=[began]))
-    began = time_sum.stage(deps=[grad_input[-1]])
-    began = space_sum.stage(deps=[began])
-    block_out = call("join", 4, join_kernel, "vv", all_rows, "v")(
-        out_back, from_joint, deps=[began]
-    )
-    space_sum.stage(deps=[block_out, time_sum.core_stage(deps=[began])])
-    space_sum.core_stage()
-    grad_input = jnp.stack(grad_input)
-    grad_time, grad_space = time_sum.finish(), space_sum.finish()
+        one_grad, token = grad_of(v, space_units[v], d_middles[v], deps=[token])
+        grad_input.append(one_grad)
+    token = time_sum.last_stage(deps=[token])
+    token = space_sum.stage(deps=[token])
+    block_out, grad_input, token = call(
+        "join", 4, join_kernel, "vv" + "a" * videos, (all_rows, all_rows), "va", [sems(videos)]
+    )(out_back, from_joint, *grad_input, deps=[token])
+    token = space_sum.stage(deps=[token])
+    *grad_time, token = time_sum.finish(deps=[token])
+    space_sum.last_stage(deps=[token])
+    *grad_space, _ = space_sum.finish()
     return (
         block_out.reshape(frames_in.shape), grad_input.reshape(frames_in.shape),
         *grad_space, *grad_time,

time: 298 us -> 335 us (1.12)
  Pallas kernels: 159 us -> 201 us
    pallas_call x22 -> x20, Pallas kernels: 159 us -> 201 us  [run(): pl.pallas_call(with_token, out_shape=(*out_shape, TOKEN), in_specs=[pl.Bl...]
    unnamed x61 -> x55, local copies, waits for them, and re-layouts: 15.2 us -> 12.4 us
    ppermute x30 -> x29, starting transfers between devices: 29.4 us -> 26.9 us  [swap(): return lax.ppermute(x, axis, [(i, i ^ mask) for i in range(size)])]
    ppermute x30 -> x29, waiting for transfers between devices: 34.3 us -> 35 us  [swap(): return lax.ppermute(x, axis, [(i, i ^ mask) for i in range(size)])]
  transfers between devices with their start and end apart: 36 -> 35, of which waited for: 13 -> 11; matrix products, arithmetic and copies ran while one was open for 1% -> 0% of each run, Pallas kernels for 51% -> 58%
where the time goes in v2:
time: 335 us; the launch traced here: 329 us
  Pallas kernels  201 us (60%)
  waiting for transfers between devices  58.5 us (17%)
  starting transfers between devices  55 us (16%)
  local copies, waits for them, and re-layouts  12.4 us (4%)
    pallas_call x20, Pallas kernels, run(): pl.pallas_call(with_token, out_shape=(*out_shape, TOKEN), in_specs=[pl.Bl...  201 us
    ppermute x29, waiting for transfers between devices, swap(): return lax.ppermute(x, axis, [(i, i ^ mask) for i in range(size)])  35 us
    all_to_all x6, starting transfers between devices, exchange(): lax.all_to_all(pieces, 'seq', split_axis=0, concat_axis=0, tiled=True)  28.1 us
    ppermute x29, starting transfers between devices, swap(): return lax.ppermute(x, axis, [(i, i ^ mask) for i in range(size)])  26.9 us
    all_to_all x6, waiting for transfers between devices, exchange(): lax.all_to_all(pieces, 'seq', split_axis=0, concat_axis=0, tiled=True)  23.5 us
    unnamed x55, local copies, waits for them, and re-layouts  12.4 us
  transfers between devices with their start and end apart: 35, of which 11 were waited for; matrix products, arithmetic and copies ran while one was open for 0% of the time, Pallas kernels for 58%

profile of v2, /device:TPU:0, one launch (start us, length us, event | category | flops | bytes accessed | tf_op | source)
XLA Modules:
  0.0 328.7 jit_solution(11170041148700777166)
XLA Ops:
  0.6 2.8 split.1
  3.4 6.5 %all-to-all-start = ((bf16[8,40,1152]{2,1,0:T(8,128)(2,1)}), bf16[8,40,1152]{2,1,0:T(8,128)(2,1)S(1)}, u32[]{:S(2)}, u32[]{:S(2)}) async-start(bf16[8,40,1152]{2,1,0:T(8,128)(2,1)} %get-tuple-element.97), calls=%async_computation | async-start | bytes 1474560 | tf_op jit(solution)/shard_map/all_to_all | solution.py:625
  10.5 11.8 %space_forward.2 = (bf16[8,40,1152]{2,1,0:T(8,128)(2,1)}, bf16[288,3456]{1,0:T(8,128)(2,1)}, bf16[288,2304]{1,0:T(8,128)(2,1)}, bf16[16,144,288]{2,1,0:T(8,128)(2,1)}, f32[8,128]{1,0:T(8,128)}) custom-call(bf16[2,288,1152]{2,1,0:T(8,128)(2,1)} %bitcast.9, bf16[2,288,1152]{2,1,0:T(8,128)(2,1)} %bitcast.7, f32[2,6,1152]{2,1,0:T(8,128)} %copy.25.refs_2_.refs_3_, ...), custom_call_target="tpu_custom_call" | custom-call | flops 14000000000 | bytes 14000000 | tf_op jit(solution)/shard_map/space_forward/pallas_call | solution.py:44
  23.5 6.3 %all-to-all-done.refs_8_.refs_2_.refs_12_ = bf16[8,40,1152]{2,1,0:T(8,128)(2,1)S(1)} async-done(((bf16[8,40,1152]{2,1,0:T(8,128)(2,1)}), bf16[8,40,1152]{2,1,0:T(8,128)(2,1)S(1)}, u32[]{:S(2)}, u32[]{:S(2)}) %all-to-all-start) | async-done | bytes 737312 | tf_op jit(solution)/shard_map/all_to_all | solution.py:625
  29.8 4.1 %all-to-all-start.2 = ((bf16[8,40,1152]{2,1,0:T(8,128)(2,1)}), bf16[8,40,1152]{2,1,0:T(8,128)(2,1)S(1)}, u32[]{:S(2)}, u32[]{:S(2)}) async-start(bf16[8,40,1152]{2,1,0:T(8,128)(2,1)} %get-tuple-element.99), calls=%async_computation.2 | async-start | bytes 1474560 | tf_op jit(solution)/shard_map/all_to_all | solution.py:625
  33.9 13.4 %space_forward.3 = (bf16[8,72,1152]{2,1,0:T(8,128)(2,1)}, bf16[288,3456]{1,0:T(8,128)(2,1)}, bf16[288,2304]{1,0:T(8,128)(2,1)}, bf16[16,144,288]{2,1,0:T(8,128)(2,1)}, f32[8,128]{1,0:T(8,128)}) custom-call(bf16[2,288,1152]{2,1,0:T(8,128)(2,1)} %bitcast.10, bf16[2,288,1152]{2,1,0:T(8,128)(2,1)} %bitcast.8, f32[2,6,1152]{2,1,0:T(8,128)} %copy.25.refs_2_.refs_3_, ...), custom_call_target="tpu_custom_call" | custom-call | flops 14000000000 | bytes 14000000 | tf_op jit(solution)/shard_map/space_forward/pallas_call | solution.py:44
  47.3 6.4 %all-to-all-done.2.refs_1_ = bf16[8,40,1152]{2,1,0:T(8,128)(2,1)S(1)} async-done(((bf16[8,40,1152]{2,1,0:T(8,128)(2,1)}), bf16[8,40,1152]{2,1,0:T(8,128)(2,1)S(1)}, u32[]{:S(2)}, u32[]{:S(2)}) %all-to-all-start.2) | async-done | bytes 737312 | tf_op jit(solution)/shard_map/all_to_all | solution.py:625
  54.6 3.7 %all-to-all-start.1 = ((bf16[8,72,1152]{2,1,0:T(8,128)(2,1)}), bf16[8,72,1152]{2,1,0:T(8,128)(2,1)S(1)}, u32[]{:S(2)}, u32[]{:S(2)}) async-start(bf16[8,72,1152]{2,1,0:T(8,128)(2,1)} %get-tuple-element.98), calls=%async_computation.1 | async-start | bytes 2654208 | tf_op jit(solution)/shard_map/all_to_all | solution.py:625
  58.3 20.7 %time.2 = (bf16[8,40,1152]{2,1,0:T(8,128)(2,1)}, bf16[8,72,1152]{2,1,0:T(8,128)(2,1)}, bf16[288,2304]{1,0:T(8,128)(2,1)}, bf16[288,2304]{1,0:T(8,128)(2,1)}, bf1...) custom-call(s32[2]{0:T(128)} %pad_add_fusion.refs_0_.refs_10_, bf16[8,40,1152]{2,1,0:T(8,128)(2,1)} %copy-done.23, ...), custom_call_target="tpu_custom_call" | custom-call | flops 24999999488 | bytes 25000000 | tf_op jit(solution)/shard_map/time/pallas_call | solution.py:44
  80.0 10.8 %all-to-all-done.1.refs_1_.refs_2_ = bf16[8,72,1152]{2,1,0:T(8,128)(2,1)S(1)} async-done(((bf16[8,72,1152]{2,1,0:T(8,128)(2,1)}), bf16[8,72,1152]{2,1,0:T(8,128)(2,1)S(1)}, u32[]{:S(2)}, u32[]{:S(2)}) %all-to-all-start.1) | async-done | bytes 1327136 | tf_op jit(solution)/shard_map/all_to_all | solution.py:625
  90.8 3.9 %all-to-all-start.4 = ((bf16[8,40,1152]{2,1,0:T(8,128)(2,1)}), bf16[8,40,1152]{2,1,0:T(8,128)(2,1)S(1)}, u32[]{:S(2)}, u32[]{:S(2)}) async-start(bf16[8,40,1152]{2,1,0:T(8,128)(2,1)} %get-tuple-element.104), calls=%async_computation.4 | async-start | bytes 1474560 | tf_op jit(solution)/shard_map/all_to_all | solution.py:625
  94.8 21.6 %time.3 = (bf16[8,40,1152]{2,1,0:T(8,128)(2,1)}, bf16[8,72,1152]{2,1,0:T(8,128)(2,1)}, bf16[288,2304]{1,0:T(8,128)(2,1)}, bf16[288,2304]{1,0:T(8,128)(2,1)}, bf1...) custom-call(s32[2]{0:T(128)} %pad_add_fusion.refs_0_.refs_10_, bf16[8,72,1152]{2,1,0:T(8,128)(2,1)} %copy-done.19, ...), custom_call_target="tpu_custom_call" | custom-call | flops 24999999488 | bytes 25000000 | tf_op jit(solution)/shard_map/time/pallas_call | solution.py:44
  116.8 5.0 %all-to-all-start.5 = ((bf16[8,40,1152]{2,1,0:T(8,128)(2,1)}), bf16[8,40,1152]{2,1,0:T(8,128)(2,1)S(1)}, u32[]{:S(2)}, u32[]{:S(2)}) async-start(bf16[8,40,1152]{2,1,0:T(8,128)(2,1)} %get-tuple-element.111), calls=%async_computation.5 | async-start | bytes 1474560 | tf_op jit(solution)/shard_map/all_to_all | solution.py:625
  122.9 11.4 %space_backward.2 = (bf16[288,1152]{1,0:T(8,128)(2,1)}, bf16[288,2304]{1,0:T(8,128)(2,1)}, bf16[288,4608]{1,0:T(8,128)(2,1)}, f32[8,128]{1,0:T(8,128)}) custom-call(s32[2]{0:T(128)} %pad_add_fusion.refs_0_.refs_10_, bf16[8,40,1152]{2,1,0:T(8,128)(2,1)} %copy-done.22, f32[2,6,1152]{2,1,0:T(8,128)} %copy.25.refs_2_.refs_3_, bf16[1152,1152]{1,0:T(8,128)(2,1)} %refs_3_.11, ...), custom_call_target="tpu_custom_call" | custom-call | flops 15000000512 | bytes 15000000 | tf_op jit(solution)/shard_map/space_backward/pallas_call | solution.py:44
  136.0 14.9 %weights.2 = (bf16[2,288,1152]{2,1,0:T(8,128)(2,1)}, bf16[2,288,1152]{2,1,0:T(8,128)(2,1)}, bf16[1,576,1152]{2,1,0:T(8,128)(2,1)}, bf16[1,576,1152]{2,1,0:T(8,128)(2,1)}, f32[8,128]{1,0:T(8,128)}) custom-call(s32[2]{0:T(128)} %pad_add_fusion.refs_0_.refs_10_, bf16[288,2304]{1,0:T(8,128)(2,1)} %get-tuple-element.114.refs_1_, ...), custom_call_target="tpu_custom_call" | custom-call | flops 10000000000 | bytes 10000000 | tf_op jit(solution)/shard_map/weights/pallas_call | solution.py:44
  151.0 1.6 collective-permute-start.6
  152.5 1.5 collective-permute-start.7
  154.9 11.5 %space_backward.3 = (bf16[288,1152]{1,0:T(8,128)(2,1)}, bf16[288,2304]{1,0:T(8,128)(2,1)}, bf16[288,4608]{1,0:T(8,128)(2,1)}, f32[8,128]{1,0:T(8,128)}) custom-call(s32[2]{0:T(128)} %pad_add_fusion.refs_0_.refs_10_, bf16[8,40,1152]{2,1,0:T(8,128)(2,1)} %copy-done.20, f32[2,6,1152]{2,1,0:T(8,128)} %copy.25.refs_2_.refs_3_, bf16[1152,1152]{1,0:T(8,128)(2,1)} %refs_3_.11, ...), custom_call_target="tpu_custom_call" | custom-call | flops 15000000512 | bytes 15000000 | tf_op jit(solution)/shard_map/space_backward/pallas_call | solution.py:44
  166.5 4.9 %all-to-all-start.3 = ((bf16[8,72,1152]{2,1,0:T(8,128)(2,1)}), bf16[8,72,1152]{2,1,0:T(8,128)(2,1)S(1)}, u32[]{:S(2)}, u32[]{:S(2)}) async-start(bf16[8,72,1152]{2,1,0:T(8,128)(2,1)} %get-tuple-element.103), calls=%async_computation.3 | async-start | bytes 2654208 | tf_op jit(solution)/shard_map/all_to_all | solution.py:625
  171.4 9.4 %grad_input.2 = (bf16[288,1152]{1,0:T(8,128)(2,1)}, f32[8,128]{1,0:T(8,128)}) custom-call(bf16[288,4608]{1,0:T(8,128)(2,1)} %get-tuple-element.109.refs_0_.refs_5_, bf16[288,1152]{1,0:T(8,128)(2,1)} %get-tuple-element.110.refs_1_, bf16[2,288,1152]{2,1,0:T(8,128)(2,1)} %bitcast.11, f32[2,6,1152]{2,1,0:T(8,128)} %copy.25.refs_2_.refs_3_, ...), custom_call_target="tpu_custom_call" | custom-call | flops 8000000000 | bytes 8000000 | tf_op jit(solution)/shard_map/grad_input/pallas_call | solution.py:44
  180.8 1.5 collective-permute-done.6.refs_3_
  182.3 1.3 collective-permute-done.7.refs_4_
  184.4 3.6 %stage.4 = (bf16[1,288,1152]{2,1,0:T(8,128)(2,1)S(1)}, bf16[1,288,1152]{2,1,0:T(8,128)(2,1)}, bf16[1,288,1152]{2,1,0:T(8,128)(2,1)S(1)}, bf16[1,288,1152]{2,1,0:T(8,128)(2,1)}, f32[8,128]{1,0:T(8,128)S(1)}) custom-call(s32[2]{0:T(128)S(1)} %copy-done.1, bf16[2,288,1152]{2,1,0:T(8,128)(2,1)S(1)} %copy-done.5, bf16[1,576,1152]{2,1,0:T(8,128)(2,1)S(1)} %copy-done.6, ...), custom_call_target="tpu_custom_call" | custom-call | flops 2000000000 | bytes 2000000 | tf_op jit(solution)/shard_map/stage/pallas_call | solution.py:44
  190.2 1.5 collective-permute-start.8
  192.3 14.8 %weights.3 = (bf16[2,288,960]{2,1,0:T(8,128)(2,1)}, bf16[2,288,960]{2,1,0:T(8,128)(2,1)}, bf16[1,576,960]{2,1,0:T(8,128)(2,1)}, bf16[1,576,960]{2,1,0:T(8,128)(2...) custom-call(s32[2]{0:T(128)} %pad_add_fusion.refs_0_.refs_10_, ...), custom_call_target="tpu_custom_call" | custom-call | flops 10000000000 | bytes 10000000 | tf_op jit(solution)/shard_map/weights/pallas_call | solution.py:44
  207.1 1.6 collective-permute-start.12
  209.1 2.0 collective-permute-start.14
  211.2 1.6 copy-done.8
  212.7 1.1 copy-done.10
  214.5 1.5 stage.5
  216.2 2.0 collective-permute-start.16
  218.2 9.4 %grad_input.3 = (bf16[288,1152]{1,0:T(8,128)(2,1)}, f32[8,128]{1,0:T(8,128)}) custom-call(bf16[288,4608]{1,0:T(8,128)(2,1)} %get-tuple-element.125.refs_6_.refs_0_, bf16[288,1152]{1,0:T(8,128)(2,1)} %get-tuple-element.126.refs_1_, bf16[2,288,1152]{2,1,0:T(8,128)(2,1)} %bitcast.12, f32[2,6,1152]{2,1,0:T(8,128)} %copy.25.refs_2_.refs_3_, ...), custom_call_target="tpu_custom_call" | custom-call | flops 8000000000 | bytes 8000000 | tf_op jit(solution)/shard_map/grad_input/pallas_call | solution.py:44
  227.6 2.0 collective-permute-done.15.refs_3_
  229.6 4.5 %collective-permute-done.16.refs_4_ = bf16[2,72,1152]{2,1,0:T(8,128)(2,1)S(1)} collective-permute-done((bf16[2,72,1152]{2,1,0:T(8,128)(2,1)S(1)}, bf16[2,72,1152]{2,1,0:T(8,128)(2,1)S(1)}, u32[]{:S(2)}, u32[]{:S(2)}) %collective-permute-start.16) | collective-permute-done | bytes 331808 | tf_op jit(solution)/shard_map/ppermute | solution.py:507
  236.4 3.8 %stage.6 = (bf16[1,288,960]{2,1,0:T(8,128)(2,1)S(1)}, bf16[1,288,960]{2,1,0:T(8,128)(2,1)S(1)}, bf16[4,72,960]{2,1,0:T(8,128)(2,1)S(1)}, bf16[4,72,960]{2,1,0:T(...) custom-call(s32[2]{0:T(128)S(1)} %copy-done.2, ...), custom_call_target="tpu_custom_call" | custom-call | flops 2000000000 | bytes 2000000 | tf_op jit(solution)/shard_map/stage/pallas_call | solution.py:44
  240.3 1.6 collective-permute-start.17
  241.8 1.7 collective-permute-start.18
  243.6 2.4 collective-permute-start.23
  246.6 43.9 %join.1 = (bf16[2,288,1152]{2,1,0:T(8,128)(2,1)}, bf16[2,288,1152]{2,1,0:T(8,128)(2,1)}, f32[8,128]{1,0:T(8,128)}) custom-call(bf16[8,72,1152]{2,1,0:T(8,128)(2,1)} %copy-done, bf16[576,576]{1,0:T(8,128)(2,1)} %constant.30.clone.refs_1_, bf16[288,1152]{1,0:T(8,128)(2,1)} %get-tuple-element.124.refs_2_, bf16[288,1152]{1,0:T(8,128)(2,1)} %get-tuple-element.141.refs_3_, ...), custom_call_target="tpu_custom_call" | custom-call | flops 4000000000 | bytes 4000000 | tf_op jit(solution)/shard_map/join/pallas_call | solution.py:44
  291.2 1.3 stage.7
  293.2 1.4 collective-permute-start.21
  296.0 9.7 %collective-permute-done.25.refs_4_ = bf16[36,2304]{1,0:T(8,128)(2,1)S(1)} collective-permute-done((bf16[36,2304]{1,0:T(8,128)(2,1)S(1)}, bf16[36,2304]{1,0:T(8,128)(2,1)S(1)}, u32[]{:S(2)}, u32[]{:S(2)}) %collective-permute-start.25) | collective-permute-done | bytes 165920 | tf_op jit(solution)/shard_map/ppermute | solution.py:507
  305.7 1.4 assemble.2
  307.1 1.6 last_stage.3
  309.2 2.6 collective-permute-start.28
  311.7 11.6 %collective-permute-done.26.refs_2_ = bf16[36,2304]{1,0:T(8,128)(2,1)S(1)} collective-permute-done((bf16[36,2304]{1,0:T(8,128)(2,1)S(1)}, bf16[36,2304]{1,0:T(8,128)(2,1)S(1)}, u32[]{:S(2)}, u32[]{:S(2)}) %collective-permute-start.26) | collective-permute-done | bytes 165920 | tf_op jit(solution)/shard_map/ppermute | solution.py:507
  323.3 3.9 %collective-permute-done.28.refs_4_ = bf16[36,2304]{1,0:T(8,128)(2,1)S(1)} collective-permute-done((bf16[36,2304]{1,0:T(8,128)(2,1)S(1)}, bf16[36,2304]{1,0:T(8,128)(2,1)S(1)}, u32[]{:S(2)}, u32[]{:S(2)}) %collective-permute-start.28) | collective-permute-done | bytes 165920 | tf_op jit(solution)/shard_map/ppermute | solution.py:507
  327.2 1.4 assemble.3
  (98 shorter events, 19.0 us)
Async XLA Ops:
  3.4 6.5 %copy-start.24 = (f32[2,6,1152]{2,0,1:T(2,128)S(1)}, f32[2,6,1152]{2,0,1:T(2,128)}, u32[]{:S(2)}) copy-start(f32[2,6,1152]{2,0,1:T(2,128)} %param.19) | copy-start | bytes 165892
  3.4 26.4 %all-to-all-start = ((bf16[8,40,1152]{2,1,0:T(8,128)(2,1)}), bf16[8,40,1152]{2,1,0:T(8,128)(2,1)S(1)}, u32[]{:S(2)}, u32[]{:S(2)}) async-start(bf16[8,40,1152]{2,1,0:T(8,128)(2,1)} %get-tuple-element.97), calls=%async_computation | async-start | bytes 1474560 | tf_op jit(solution)/shard_map/all_to_all | solution.py:625
  22.3 99.6 %collective-permute-start = (bf16[288,2304]{1,0:T(8,128)(2,1)}, bf16[288,2304]{1,0:T(8,128)(2,1)S(1)}, u32[]{:S(2)}, u32[]{:S(2)}) collective-permute-start(bf16[288,2304]{1,0:T(8,128)(2,1)} %get-tuple-element.108.refs_1_), channel_id=1, source_target_pairs={{0,1},{1,0},{2,3},{3,2},{4,5},{5,4},{6,7},{7,6},{8,9},{9,8},{10,11... | collective-permute-start | bytes 3981320 | tf_op jit(solution)/shard_map/ppermute | solution.py:507
  29.8 4.1 %copy-start.21 = (bf16[8,40,1152]{2,1,0:T(8,128)(2,1)}, bf16[8,40,1152]{2,1,0:T(8,128)(2,1)S(1)}, u32[]{:S(2)}) copy-start(bf16[8,40,1152]{2,1,0:T(8,128)(2,1)S(1)} %all-to-all-done.refs_8_.refs_2_.refs_12_) | copy-start | bytes 2211844
  29.8 23.9 %all-to-all-start.2 = ((bf16[8,40,1152]{2,1,0:T(8,128)(2,1)}), bf16[8,40,1152]{2,1,0:T(8,128)(2,1)S(1)}, u32[]{:S(2)}, u32[]{:S(2)}) async-start(bf16[8,40,1152]{2,1,0:T(8,128)(2,1)} %get-tuple-element.99), calls=%async_computation.2 | async-start | bytes 1474560 | tf_op jit(solution)/shard_map/all_to_all | solution.py:625
  54.6 36.2 %all-to-all-start.1 = ((bf16[8,72,1152]{2,1,0:T(8,128)(2,1)}), bf16[8,72,1152]{2,1,0:T(8,128)(2,1)S(1)}, u32[]{:S(2)}, u32[]{:S(2)}) async-start(bf16[8,72,1152]{2,1,0:T(8,128)(2,1)} %get-tuple-element.98), calls=%async_computation.1 | async-start | bytes 2654208 | tf_op jit(solution)/shard_map/all_to_all | solution.py:625
  79.0 55.3 %collective-permute-start.1 = (bf16[288,2304]{1,0:T(8,128)(2,1)}, bf16[288,2304]{1,0:T(8,128)(2,1)}, u32[]{:S(2)}, u32[]{:S(2)}) collective-permute-start(bf16[288,2304]{1,0:T(8,128)(2,1)} %get-tuple-element.114.refs_1_), channel_id=1, source_target_pairs={{0,1},{1,0},{2,3},{3,2},{4,5},{5,4},{6,7},{7,6},{8,9},{9,8},{10,11... | collective-permute-start | bytes 3981320 | tf_op jit(solution)/shard_map/ppermute | solution.py:507
  79.5 55.4 %collective-permute-start.3 = (bf16[288,2304]{1,0:T(8,128)(2,1)}, bf16[288,2304]{1,0:T(8,128)(2,1)}, u32[]{:S(2)}, u32[]{:S(2)}) collective-permute-start(bf16[288,2304]{1,0:T(8,128)(2,1)} %get-tuple-element.118), channel_id=1, source_target_pairs={{0,1},{1,0},{2,3},{3,2},{4,5},{5,4},{6,7},{7,6},{8,9},{9,8},{10,11... | collective-permute-start | bytes 3981320 | tf_op jit(solution)/shard_map/ppermute | solution.py:507
  79.6 74.4 %collective-permute-start.5 = (bf16[288,2304]{1,0:T(8,128)(2,1)}, bf16[288,2304]{1,0:T(8,128)(2,1)}, u32[]{:S(2)}, u32[]{:S(2)}) collective-permute-start(bf16[288,2304]{1,0:T(8,128)(2,1)} %get-tuple-element.122.refs_2_), channel_id=1, source_target_pairs={{0,1},{1,0},{2,3},{3,2},{4,5},{5,4},{6,7},{7,6},{8,9},{9,8},{10,11... | collective-permute-start | bytes 3981320 | tf_op jit(solution)/shard_map/ppermute | solution.py:507
  90.8 4.0 %copy-start.19 = (bf16[8,72,1152]{2,1,0:T(8,128)(2,1)}, bf16[8,72,1152]{2,1,0:T(8,128)(2,1)S(1)}, u32[]{:S(2)}) copy-start(bf16[8,72,1152]{2,1,0:T(8,128)(2,1)S(1)} %all-to-all-done.1.refs_1_.refs_2_) | copy-start | bytes 3981316
  90.8 26.0 %all-to-all-start.4 = ((bf16[8,40,1152]{2,1,0:T(8,128)(2,1)}), bf16[8,40,1152]{2,1,0:T(8,128)(2,1)S(1)}, u32[]{:S(2)}, u32[]{:S(2)}) async-start(bf16[8,40,1152]{2,1,0:T(8,128)(2,1)} %get-tuple-element.104), calls=%async_computation.4 | async-start | bytes 1474560 | tf_op jit(solution)/shard_map/all_to_all | solution.py:625
  116.3 18.6 %collective-permute-start.2 = (bf16[288,2304]{1,0:T(8,128)(2,1)}, bf16[288,2304]{1,0:T(8,128)(2,1)}, u32[]{:S(2)}, u32[]{:S(2)}) collective-permute-start(bf16[288,2304]{1,0:T(8,128)(2,1)} %get-tuple-element.115.refs_2_), channel_id=1, source_target_pairs={{0,1},{1,0},{2,3},{3,2},{4,5},{5,4},{6,7},{7,6},{8,9},{9,8},{10,11... | collective-permute-start | bytes 3981320 | tf_op jit(solution)/shard_map/ppermute | solution.py:507
  116.8 5.6 %copy-start.22 = (bf16[8,40,1152]{2,1,0:T(8,128)(2,1)}, bf16[8,40,1152]{2,1,0:T(8,128)(2,1)S(1)}, u32[]{:S(2)}) copy-start(bf16[8,40,1152]{2,1,0:T(8,128)(2,1)S(1)} %all-to-all-done.4.refs_1_) | copy-start | bytes 2211844
  116.8 37.2 %all-to-all-start.5 = ((bf16[8,40,1152]{2,1,0:T(8,128)(2,1)}), bf16[8,40,1152]{2,1,0:T(8,128)(2,1)S(1)}, u32[]{:S(2)}, u32[]{:S(2)}) async-start(bf16[8,40,1152]{2,1,0:T(8,128)(2,1)} %get-tuple-element.111), calls=%async_computation.5 | async-start | bytes 1474560 | tf_op jit(solution)/shard_map/all_to_all | solution.py:625
  121.8 13.1 %collective-permute-start.4 = (bf16[288,2304]{1,0:T(8,128)(2,1)}, bf16[288,2304]{1,0:T(8,128)(2,1)S(1)}, u32[]{:S(2)}, u32[]{:S(2)}) collective-permute-start(bf16[288,2304]{1,0:T(8,128)(2,1)} %get-tuple-element.119), channel_id=1, source_target_pairs={{0,1},{1,0},{2,3},{3,2},{4,5},{5,4},{6,7},{7,6},{8,9},{9,8},{10,11... | collective-permute-start | bytes 3981320 | tf_op jit(solution)/shard_map/ppermute | solution.py:507
  134.3 57.9 %collective-permute-start.10 = (bf16[288,2304]{1,0:T(8,128)(2,1)}, bf16[288,2304]{1,0:T(8,128)(2,1)}, u32[]{:S(2)}, u32[]{:S(2)}) collective-permute-start(bf16[288,2304]{1,0:T(8,128)(2,1)} %get-tuple-element.136), channel_id=1, source_target_pairs={{0,1},{1,0},{2,3},{3,2},{4,5},{5,4},{6,7},{7,6},{8,9},{9,8},{10,11... | collective-permute-start | bytes 3981320 | tf_op jit(solution)/shard_map/ppermute | solution.py:507
  151.0 31.4 %collective-permute-start.6 = (bf16[2,288,1152]{2,1,0:T(8,128)(2,1)}, bf16[2,288,1152]{2,1,0:T(8,128)(2,1)S(1)}, u32[]{:S(2)}, u32[]{:S(2)}) collective-permute-start(bf16[2,288,1152]{2,1,0:T(8,128)(2,1)} %get-tuple-element.129), channel_id=1, source_target_pairs={{0,8},{8,0},{16,24},{24,16},{1,9},{9,1},{17,25},{25,17},{2,10},{10... | collective-permute-start | bytes 3981320 | tf_op jit(solution)/shard_map/ppermute | solution.py:507
  152.5 31.1 %collective-permute-start.7 = (bf16[1,576,1152]{2,1,0:T(8,128)(2,1)}, bf16[1,576,1152]{2,1,0:T(8,128)(2,1)}, u32[]{:S(2)}, u32[]{:S(2)}) collective-permute-start(bf16[1,576,1152]{2,1,0:T(8,128)(2,1)} %get-tuple-element.130), channel_id=1, source_target_pairs={{0,16},{8,24},{16,0},{24,8},{1,17},{9,25},{17,1},{25,9},{2,18},{10... | collective-permute-start | bytes 3981320 | tf_op jit(solution)/shard_map/ppermute | solution.py:507
  166.4 25.9 %collective-permute-start.11 = (bf16[288,2304]{1,0:T(8,128)(2,1)}, bf16[288,2304]{1,0:T(8,128)(2,1)}, u32[]{:S(2)}, u32[]{:S(2)}) collective-permute-start(bf16[288,2304]{1,0:T(8,128)(2,1)} %get-tuple-element.137), channel_id=1, source_target_pairs={{0,1},{1,0},{2,3},{3,2},{4,5},{5,4},{6,7},{7,6},{8,9},{9,8},{10,11... | collective-permute-start | bytes 3981320 | tf_op jit(solution)/shard_map/ppermute | solution.py:507
  166.5 44.6 %all-to-all-start.3 = ((bf16[8,72,1152]{2,1,0:T(8,128)(2,1)}), bf16[8,72,1152]{2,1,0:T(8,128)(2,1)S(1)}, u32[]{:S(2)}, u32[]{:S(2)}) async-start(bf16[8,72,1152]{2,1,0:T(8,128)(2,1)} %get-tuple-element.103), calls=%async_computation.3 | async-start | bytes 2654208 | tf_op jit(solution)/shard_map/all_to_all | solution.py:625
  171.4 12.3 %copy-start.1 = (s32[2]{0:T(128)S(1)}, s32[2]{0:T(128)}, u32[]{:S(2)}) copy-start(s32[2]{0:T(128)} %pad_add_fusion.refs_0_.refs_10_) | copy-start | bytes 28
  171.4 12.3 %copy-start.5 = (bf16[2,288,1152]{2,1,0:T(8,128)(2,1)S(1)}, bf16[2,288,1152]{2,1,0:T(8,128)(2,1)}, u32[]{:S(2)}) copy-start(bf16[2,288,1152]{2,1,0:T(8,128)(2,1)} %get-tuple-element.127.refs_1_) | copy-start | bytes 3981316
  171.4 12.3 %copy-start.6 = (bf16[1,576,1152]{2,1,0:T(8,128)(2,1)S(1)}, bf16[1,576,1152]{2,1,0:T(8,128)(2,1)}, u32[]{:S(2)}) copy-start(bf16[1,576,1152]{2,1,0:T(8,128)(2,1)} %get-tuple-element.128.refs_2_) | copy-start | bytes 3981316
  190.2 20.9 %collective-permute-start.8 = (bf16[1,288,1152]{2,1,0:T(8,128)(2,1)}, bf16[1,288,1152]{2,1,0:T(8,128)(2,1)S(1)}, u32[]{:S(2)}, u32[]{:S(2)}) collective-permute-start(bf16[1,288,1152]{2,1,0:T(8,128)(2,1)} %get-tuple-element.134), channel_id=1, source_target_pairs={{0,16},{8,24},{16,0},{24,8},{1,17},{9,25},{17,1},{25,9},{2,18},{10... | collective-permute-start | bytes 1990664 | tf_op jit(solution)/shard_map/ppermute | solution.py:507
  191.7 19.4 %collective-permute-start.9 = (bf16[1,288,1152]{2,1,0:T(8,128)(2,1)}, bf16[1,288,1152]{2,1,0:T(8,128)(2,1)}, u32[]{:S(2)}, u32[]{:S(2)}) collective-permute-start(bf16[1,288,1152]{2,1,0:T(8,128)(2,1)} %get-tuple-element.135), channel_id=1, source_target_pairs={{0,8},{8,0},{16,24},{24,16},{1,9},{9,1},{17,25},{25,17},{2,10},{10... | collective-permute-start | bytes 1990664 | tf_op jit(solution)/shard_map/ppermute | solution.py:507
  192.3 18.9 %copy-start.2 = (s32[2]{0:T(128)S(1)}, s32[2]{0:T(128)}, u32[]{:S(2)}) copy-start(s32[2]{0:T(128)} %pad_add_fusion.refs_0_.refs_10_) | copy-start | bytes 28
  207.1 28.6 %collective-permute-start.12 = (bf16[2,288,960]{2,1,0:T(8,128)(2,1)}, bf16[2,288,960]{2,1,0:T(8,128)(2,1)S(1)}, u32[]{:S(2)}, u32[]{:S(2)}) collective-permute-start(bf16[2,288,960]{2,1,0:T(8,128)(2,1)} %get-tuple-element.145), channel_id=1, source_target_pairs={{0,8},{8,0},{16,24},{24,16},{1,9},{9,1},{17,25},{25,17},{2,10},{10... | collective-permute-start | bytes 3317768 | tf_op jit(solution)/shard_map/ppermute | solution.py:507
  208.6 27.1 %collective-permute-start.13 = (bf16[1,576,960]{2,1,0:T(8,128)(2,1)}, bf16[1,576,960]{2,1,0:T(8,128)(2,1)}, u32[]{:S(2)}, u32[]{:S(2)}) collective-permute-start(bf16[1,576,960]{2,1,0:T(8,128)(2,1)} %get-tuple-element.146), channel_id=1, source_target_pairs={{0,16},{8,24},{16,0},{24,8},{1,17},{9,25},{17,1},{25,9},{2,18},{10... | collective-permute-start | bytes 3317768 | tf_op jit(solution)/shard_map/ppermute | solution.py:507
  209.1 26.6 %collective-permute-start.14 = (bf16[8,72,384]{2,1,0:T(8,128)(2,1)}, bf16[8,72,384]{2,1,0:T(8,128)(2,1)}, u32[]{:S(2)}, u32[]{:S(2)}) collective-permute-start(bf16[8,72,384]{2,1,0:T(8,128)(2,1)} %get-tuple-element.147), channel_id=1, source_target_pairs={{0,2},{1,3},{2,0},{3,1},{4,6},{5,7},{6,4},{7,5},{8,10},{9,11},{10,... | collective-permute-start | bytes 1327112 | tf_op jit(solution)/shard_map/ppermute | solution.py:507
  211.1 4.9 %copy-start = (bf16[8,72,1152]{2,1,0:T(8,128)(2,1)}, bf16[8,72,1152]{2,1,0:T(8,128)(2,1)S(1)}, u32[]{:S(2)}) copy-start(bf16[8,72,1152]{2,1,0:T(8,128)(2,1)S(1)} %all-to-all-done.3.refs_6_.refs_0_) | copy-start | bytes 3981316
  216.1 2.1 copy-start.17
  216.1 13.5 %collective-permute-start.15 = (bf16[2,72,1152]{2,1,0:T(8,128)(2,1)S(1)}, bf16[2,72,1152]{2,1,0:T(8,128)(2,1)S(1)}, u32[]{:S(2)}, u32[]{:S(2)}) collective-permute-start(bf16[2,72,1152]{2,1,0:T(8,128)(2,1)S(1)} %get-tuple-element.150), channel_id=1, source_target_pairs={{0,2},{1,3},{2,0},{3,1},{4,6},{5,7},{6,4},{7,5},{8,10},{9,11},{10,... | collective-permute-start | bytes 995336 | tf_op jit(solution)/shard_map/ppermute | solution.py:507
  216.2 17.9 %collective-permute-start.16 = (bf16[2,72,1152]{2,1,0:T(8,128)(2,1)S(1)}, bf16[2,72,1152]{2,1,0:T(8,128)(2,1)S(1)}, u32[]{:S(2)}, u32[]{:S(2)}) collective-permute-start(bf16[2,72,1152]{2,1,0:T(8,128)(2,1)S(1)} %get-tuple-element.151), channel_id=1, source_target_pairs={{0,2},{1,3},{2,0},{3,1},{4,6},{5,7},{6,4},{7,5},{8,10},{9,11},{10,... | collective-permute-start | bytes 995336 | tf_op jit(solution)/shard_map/ppermute | solution.py:507
  234.7 1.6 copy-start.4
  234.7 1.7 copy-start.11
  240.2 6.3 %copy-start.12 = (f32[8,128]{1,0:T(8,128)}, f32[8,128]{1,0:T(8,128)S(1)}, u32[]{:S(2)}) copy-start(f32[8,128]{1,0:T(8,128)S(1)} %get-tuple-element.154.refs_4_) | copy-start | bytes 12292
  240.3 50.3 %collective-permute-start.17 = (bf16[1,288,960]{2,1,0:T(8,128)(2,1)S(1)}, bf16[1,288,960]{2,1,0:T(8,128)(2,1)S(1)}, u32[]{:S(2)}, u32[]{:S(2)}) collective-permute-start(bf16[1,288,960]{2,1,0:T(8,128)(2,1)S(1)} %get-tuple-element.160), channel_id=1, source_target_pairs={{0,16},{8,24},{16,0},{24,8},{1,17},{9,25},{17,1},{25,9},{2,18},{10... | collective-permute-start | bytes 1658888 | tf_op jit(solution)/shard_map/ppermute | solution.py:507
  241.8 48.7 %collective-permute-start.18 = (bf16[4,72,960]{2,1,0:T(8,128)(2,1)S(1)}, bf16[4,72,960]{2,1,0:T(8,128)(2,1)S(1)}, u32[]{:S(2)}, u32[]{:S(2)}) collective-permute-start(bf16[4,72,960]{2,1,0:T(8,128)(2,1)S(1)} %get-tuple-element.161), channel_id=1, source_target_pairs={{0,2},{1,3},{2,0},{3,1},{4,6},{5,7},{6,4},{7,5},{8,10},{9,11},{10,... | collective-permute-start | bytes 1658888 | tf_op jit(solution)/shard_map/ppermute | solution.py:507
  243.6 51.4 %collective-permute-start.23 = (bf16[36,2304]{1,0:T(8,128)(2,1)S(1)}, bf16[36,2304]{1,0:T(8,128)(2,1)S(1)}, u32[]{:S(2)}, u32[]{:S(2)}) collective-permute-start(bf16[36,2304]{1,0:T(8,128)(2,1)S(1)} %get-tuple-element.171), channel_id=1, source_target_pairs={{0,4},{1,5},{2,6},{3,7},{4,0},{5,1},{6,2},{7,3},{8,12},{9,13},{10,... | collective-permute-start | bytes 497672 | tf_op jit(solution)/shard_map/ppermute | solution.py:507
  246.0 44.5 %collective-permute-start.19 = (bf16[2,144,384]{2,1,0:T(8,128)(2,1)S(1)}, bf16[2,144,384]{2,1,0:T(8,128)(2,1)S(1)}, u32[]{:S(2)}, u32[]{:S(2)}) collective-permute-start(bf16[2,144,384]{2,1,0:T(8,128)(2,1)S(1)} %get-tuple-element.162), channel_id=1, source_target_pairs={{0,8},{8,0},{16,24},{24,16},{1,9},{9,1},{17,25},{25,17},{2,10},{10... | collective-permute-start | bytes 663560 | tf_op jit(solution)/shard_map/ppermute | solution.py:507
  292.5 14.5 %collective-permute-start.20 = (bf16[2,72,960]{2,1,0:T(8,128)(2,1)S(1)}, bf16[2,72,960]{2,1,0:T(8,128)(2,1)S(1)}, u32[]{:S(2)}, u32[]{:S(2)}) collective-permute-start(bf16[2,72,960]{2,1,0:T(8,128)(2,1)S(1)} %get-tuple-element.167), channel_id=1, source_target_pairs={{0,2},{1,3},{2,0},{3,1},{4,6},{5,7},{6,4},{7,5},{8,10},{9,11},{10,... | collective-permute-start | bytes 829448 | tf_op jit(solution)/shard_map/ppermute | solution.py:507
  293.2 13.9 %collective-permute-start.21 = (bf16[1,144,960]{2,1,0:T(8,128)(2,1)S(1)}, bf16[1,144,960]{2,1,0:T(8,128)(2,1)S(1)}, u32[]{:S(2)}, u32[]{:S(2)}) collective-permute-start(bf16[1,144,960]{2,1,0:T(8,128)(2,1)S(1)} %get-tuple-element.168), channel_id=1, source_target_pairs={{0,8},{8,0},{16,24},{24,16},{1,9},{9,1},{17,25},{25,17},{2,10},{10... | collective-permute-start | bytes 829448 | tf_op jit(solution)/shard_map/ppermute | solution.py:507
  294.5 1.4 collective-permute-start.24
  294.5 11.1 %collective-permute-start.25 = (bf16[36,2304]{1,0:T(8,128)(2,1)S(1)}, bf16[36,2304]{1,0:T(8,128)(2,1)S(1)}, u32[]{:S(2)}, u32[]{:S(2)}) collective-permute-start(bf16[36,2304]{1,0:T(8,128)(2,1)S(1)} %get-tuple-element.173), channel_id=1, source_target_pairs={{0,5},{1,4},{2,7},{3,6},{4,1},{5,0},{6,3},{7,2},{8,13},{9,12},{10,... | collective-permute-start | bytes 497672 | tf_op jit(solution)/shard_map/ppermute | solution.py:507
  295.0 12.1 %collective-permute-start.22 = (bf16[1,144,384]{2,1,0:T(8,128)(2,1)S(1)}, bf16[1,144,384]{2,1,0:T(8,128)(2,1)S(1)}, u32[]{:S(2)}, u32[]{:S(2)}) collective-permute-start(bf16[1,144,384]{2,1,0:T(8,128)(2,1)S(1)} %get-tuple-element.169), channel_id=1, source_target_pairs={{0,16},{8,24},{16,0},{24,8},{1,17},{9,25},{17,1},{25,9},{2,18},{10... | collective-permute-start | bytes 331784 | tf_op jit(solution)/shard_map/ppermute | solution.py:507
  308.7 14.6 %collective-permute-start.26 = (bf16[36,2304]{1,0:T(8,128)(2,1)S(1)}, bf16[36,2304]{1,0:T(8,128)(2,1)S(1)}, u32[]{:S(2)}, u32[]{:S(2)}) collective-permute-start(bf16[36,2304]{1,0:T(8,128)(2,1)S(1)} %get-tuple-element.177), channel_id=1, source_target_pairs={{0,4},{1,5},{2,6},{3,7},{4,0},{5,1},{6,2},{7,3},{8,12},{9,13},{10,... | collective-permute-start | bytes 497672 | tf_op jit(solution)/shard_map/ppermute | solution.py:507
  308.9 14.4 %collective-permute-start.27 = (bf16[36,2304]{1,0:T(8,128)(2,1)S(1)}, bf16[36,2304]{1,0:T(8,128)(2,1)S(1)}, u32[]{:S(2)}, u32[]{:S(2)}) collective-permute-start(bf16[36,2304]{1,0:T(8,128)(2,1)S(1)} %get-tuple-element.178), channel_id=1, source_target_pairs={{0,1},{1,0},{2,3},{3,2},{4,5},{5,4},{6,7},{7,6},{8,9},{9,8},{10,11... | collective-permute-start | bytes 497672 | tf_op jit(solution)/shard_map/ppermute | solution.py:507
  309.2 18.0 %collective-permute-start.28 = (bf16[36,2304]{1,0:T(8,128)(2,1)S(1)}, bf16[36,2304]{1,0:T(8,128)(2,1)S(1)}, u32[]{:S(2)}, u32[]{:S(2)}) collective-permute-start(bf16[36,2304]{1,0:T(8,128)(2,1)S(1)} %get-tuple-element.179), channel_id=1, source_target_pairs={{0,5},{1,4},{2,7},{3,6},{4,1},{5,0},{6,3},{7,2},{8,13},{9,12},{10,... | collective-permute-start | bytes 497672 | tf_op jit(solution)/shard_map/ppermute | solution.py:507
  (14 other events, 12.9 us)

commit v3 on v2

--- a/solution.py
+++ b/solution.py
@@ -30,7 +30,7 @@
     "split": 56, "space_forward": 56, "time": 56, "weights": 56, "space_backward": 56,
     "grad_input": 56, "stage": 24, "last_stage": 16, "assemble": 16, "join": 56,
 }
-SPACES = {"v": pltpu.VMEM, "s": pltpu.SMEM, "a": pl.ANY, "h": pltpu.HBM}
+SPACES = {"v": pltpu.VMEM, "s": pltpu.SMEM, "a": pl.ANY}
 
 
 def call(name, us, body, ins, out_shape, outs, scratch=()):
@@ -163,13 +163,11 @@
 
 
 def join_kernel(pieces_ref, gather_ref, *refs):
-    *grads, out_ref, grad_out, sems = refs
-    copies = Copies(sems)
-    stores = [copies.start(grads[v], grad_out.at[v]) for v in range(grad_out.shape[0])]
+    *grads, out_ref, grad_out = refs
+    for video in range(grad_out.shape[0]):
+        grad_out[video] = grads[video][...]
     rows = dot(gather_ref[...], frame_rows(pieces_ref[...])).astype(BF16)
     out_ref[...] = rows.reshape(out_ref.shape)
-    for store in stores:
-        store.wait()
 
 
 def space_forward_kernel(
@@ -422,7 +420,7 @@
                 now.append(copies.start(right.at[:, columns], right_rows.at[rows, at]))
         return now
 
-    waits = [load(0)]
+    waits = [load(0), load(1)]
     done, stores = 0, []
     for part, ((low, high), (axis, bit, inner)) in enumerate(zip(cuts, steps)):
         for unit in range(2):
@@ -433,8 +431,6 @@
                 for wait in waits[done]:
                     wait.wait()
                 done += 1
-                if done == 1:
-                    waits.append(load(1))
             column = pl.multiple_of(core * width, 128) if unit else 0
             left = left_rows[:, pl.ds(column, width)]
             total[:, start - low : stop - low] = (
@@ -455,19 +451,11 @@
         ].astype(F32)
 
 
-def stage_kernel(steps, loaded, place_ref, *refs):
+def stage_kernel(steps, place_ref, *refs):
     count = len(steps)
-    scratch = count + 2 if loaded else 1
-    outs, total = refs[-scratch - 2 * count : -scratch], refs[-scratch]
-    kept = refs[:count]
-    if loaded:
-        copies = Copies(refs[-1])
-        loads = [copies.start(a, b) for a, b in zip(kept, refs[-count - 1 : -1])]
-        kept = refs[-count - 1 : -1]
+    total, outs = refs[-1], refs[-1 - 2 * count : -1]
     for part, (axis, bit, inner) in enumerate(steps):
-        if loaded:
-            loads[part].wait()
-        add_got(total, kept[part], refs[count + part])
+        add_got(total, refs[part], refs[count + part])
         emit_halves(
             total, inner, bit_of(place_ref, axis, bit), outs[2 * part], outs[2 * part + 1]
         )
@@ -549,15 +537,10 @@
 
     def stage(self, deps=()):
         steps, shapes = self.next_steps()
-        loaded = self.step == 1
-        scratch = [pltpu.VMEM((self.width >> self.step, self.columns), F32)]
-        if loaded:
-            scratch += [pltpu.VMEM(half.shape, BF16) for half in self.kept]
-            scratch += [pltpu.SemaphoreType.DMA((self.parts,))]
         *halves, token = call(
-            "stage", 2, functools.partial(stage_kernel, steps, loaded),
-            "s" + ("h" if loaded else "v") * self.parts + "v" * self.parts, shapes,
-            "v" * len(shapes), scratch,
+            "stage", 2, functools.partial(stage_kernel, steps), "s" + "v" * (2 * self.parts),
+            shapes, "v" * len(shapes),
+            [pltpu.VMEM((self.width >> self.step, self.columns), F32)],
         )(self.place, *self.kept, *self.got, deps=deps)
         self.send(halves)
         return token
@@ -740,23 +723,24 @@
             out_back = exchange(out_sent)
         d_middles.append(d_middle)
         space_units.append((left, left_got, right, exchange_units(sent)))
-    first_grad, token = grad_of(0, space_units[0], d_middles[0], deps=[token])
-    grad_input = [first_grad]
     token = time_sum.stage(deps=[token])
     space_sum, token = weights(space_units, True, deps=[token])
-    token = time_sum.stage(deps=[token, out_back])
-    for v in range(1, videos):
-        one_grad, token = grad_of(v, space_units[v], d_middles[v], deps=[token])
+    token = time_sum.stage(deps=[token])
+    grad_input = []
+    for v in range(videos):
+        one_grad, token = grad_of(
+            v, space_units[v], d_middles[v], deps=[token, out_back] if v else [token]
+        )
         grad_input.append(one_grad)
     token = time_sum.last_stage(deps=[token])
     token = space_sum.stage(deps=[token])
     block_out, grad_input, token = call(
-        "join", 4, join_kernel, "vv" + "a" * videos, (all_rows, all_rows), "va", [sems(videos)]
+        "join", 4, join_kernel, "vv" + "v" * videos, (all_rows, all_rows), "vv"
     )(out_back, from_joint, *grad_input, deps=[token])
     token = space_sum.stage(deps=[token])
+    token = space_sum.last_stage(deps=[token])
     *grad_time, token = time_sum.finish(deps=[token])
-    space_sum.last_stage(deps=[token])
-    *grad_space, _ = space_sum.finish()
+    *grad_space, _ = space_sum.finish(deps=[token])
     return (
         block_out.reshape(frames_in.shape), grad_input.reshape(frames_in.shape),
         *grad_space, *grad_time,

time: 335 us -> 294 us (0.88)
  Pallas kernels: 201 us -> 158 us
  waiting for transfers between devices: 58.5 us -> 67.2 us
    pallas_call x20, Pallas kernels: 201 us -> 158 us  [run(): pl.pallas_call(with_token, out_shape=(*out_shape, TOKEN), in_specs=[pl.Bl...]
    ppermute x29, waiting for transfers between devices: 35 us -> 43.8 us  [swap(): return lax.ppermute(x, axis, [(i, i ^ mask) for i in range(size)])]
    ppermute x29, starting transfers between devices: 26.9 us -> 23.5 us  [swap(): return lax.ppermute(x, axis, [(i, i ^ mask) for i in range(size)])]
    unnamed x55 -> x51, local copies, waits for them, and re-layouts: 12.4 us -> 9.41 us
  transfers between devices with their start and end apart: 35 -> 35, of which waited for: 11 -> 13; matrix products, arithmetic and copies ran while one was open for 0% -> 0% of each run, Pallas kernels for 58% -> 52%
where the time goes in v3:
time: 294 us; the launch traced here: 289 us
  Pallas kernels  158 us (54%)
  waiting for transfers between devices  67.2 us (23%)
  starting transfers between devices  51.9 us (18%)
  local copies, waits for them, and re-layouts  9.41 us (3%)
    pallas_call x20, Pallas kernels, run(): pl.pallas_call(with_token, out_shape=(*out_shape, TOKEN), in_specs=[pl.Bl...  158 us
    ppermute x29, waiting for transfers between devices, swap(): return lax.ppermute(x, axis, [(i, i ^ mask) for i in range(size)])  43.8 us
    all_to_all x6, starting transfers between devices, exchange(): lax.all_to_all(pieces, 'seq', split_axis=0, concat_axis=0, tiled=True)  28.5 us
    ppermute x29, starting transfers between devices, swap(): return lax.ppermute(x, axis, [(i, i ^ mask) for i in range(size)])  23.5 us
    all_to_all x6, waiting for transfers between devices, exchange(): lax.all_to_all(pieces, 'seq', split_axis=0, concat_axis=0, tiled=True)  23.4 us
    unnamed x51, local copies, waits for them, and re-layouts  9.41 us
  transfers between devices with their start and end apart: 35, of which 13 were waited for; matrix products, arithmetic and copies ran while one was open for 0% of the time, Pallas kernels for 52%

profile of v3, /device:TPU:0, one launch (start us, length us, event | category | flops | bytes accessed | tf_op | source)
XLA Modules:
  0.0 288.6 jit_solution(3647765075797236802)
XLA Ops:
  0.6 2.8 split.1
  3.4 6.5 %all-to-all-start = ((bf16[8,40,1152]{2,1,0:T(8,128)(2,1)}), bf16[8,40,1152]{2,1,0:T(8,128)(2,1)S(1)}, u32[]{:S(2)}, u32[]{:S(2)}) async-start(bf16[8,40,1152]{2,1,0:T(8,128)(2,1)} %get-tuple-element.98), calls=%async_computation | async-start | bytes 1474560 | tf_op jit(solution)/shard_map/all_to_all | solution.py:608
  10.5 11.8 %space_forward.2 = (bf16[8,40,1152]{2,1,0:T(8,128)(2,1)}, bf16[288,3456]{1,0:T(8,128)(2,1)}, bf16[288,2304]{1,0:T(8,128)(2,1)}, bf16[16,144,288]{2,1,0:T(8,128)(2,1)}, f32[8,128]{1,0:T(8,128)}) custom-call(bf16[2,288,1152]{2,1,0:T(8,128)(2,1)} %bitcast.9, bf16[2,288,1152]{2,1,0:T(8,128)(2,1)} %bitcast.7, f32[2,6,1152]{2,1,0:T(8,128)} %copy.25.refs_2_.refs_3_, ...), custom_call_target="tpu_custom_call" | custom-call | flops 14000000000 | bytes 14000000 | tf_op jit(solution)/shard_map/space_forward/pallas_call | solution.py:44
  23.5 6.3 %all-to-all-done.refs_8_.refs_2_.refs_12_ = bf16[8,40,1152]{2,1,0:T(8,128)(2,1)S(1)} async-done(((bf16[8,40,1152]{2,1,0:T(8,128)(2,1)}), bf16[8,40,1152]{2,1,0:T(8,128)(2,1)S(1)}, u32[]{:S(2)}, u32[]{:S(2)}) %all-to-all-start) | async-done | bytes 737312 | tf_op jit(solution)/shard_map/all_to_all | solution.py:608
  29.8 3.8 %all-to-all-start.2 = ((bf16[8,40,1152]{2,1,0:T(8,128)(2,1)}), bf16[8,40,1152]{2,1,0:T(8,128)(2,1)S(1)}, u32[]{:S(2)}, u32[]{:S(2)}) async-start(bf16[8,40,1152]{2,1,0:T(8,128)(2,1)} %get-tuple-element.100), calls=%async_computation.2 | async-start | bytes 1474560 | tf_op jit(solution)/shard_map/all_to_all | solution.py:608
  33.6 13.4 %space_forward.3 = (bf16[8,72,1152]{2,1,0:T(8,128)(2,1)}, bf16[288,3456]{1,0:T(8,128)(2,1)}, bf16[288,2304]{1,0:T(8,128)(2,1)}, bf16[16,144,288]{2,1,0:T(8,128)(2,1)}, f32[8,128]{1,0:T(8,128)}) custom-call(bf16[2,288,1152]{2,1,0:T(8,128)(2,1)} %bitcast.10, bf16[2,288,1152]{2,1,0:T(8,128)(2,1)} %bitcast.8, f32[2,6,1152]{2,1,0:T(8,128)} %copy.25.refs_2_.refs_3_, ...), custom_call_target="tpu_custom_call" | custom-call | flops 14000000000 | bytes 14000000 | tf_op jit(solution)/shard_map/space_forward/pallas_call | solution.py:44
  46.9 6.4 %all-to-all-done.2.refs_1_ = bf16[8,40,1152]{2,1,0:T(8,128)(2,1)S(1)} async-done(((bf16[8,40,1152]{2,1,0:T(8,128)(2,1)}), bf16[8,40,1152]{2,1,0:T(8,128)(2,1)S(1)}, u32[]{:S(2)}, u32[]{:S(2)}) %all-to-all-start.2) | async-done | bytes 737312 | tf_op jit(solution)/shard_map/all_to_all | solution.py:608
  54.3 3.8 %all-to-all-start.1 = ((bf16[8,72,1152]{2,1,0:T(8,128)(2,1)}), bf16[8,72,1152]{2,1,0:T(8,128)(2,1)S(1)}, u32[]{:S(2)}, u32[]{:S(2)}) async-start(bf16[8,72,1152]{2,1,0:T(8,128)(2,1)} %get-tuple-element.99), calls=%async_computation.1 | async-start | bytes 2654208 | tf_op jit(solution)/shard_map/all_to_all | solution.py:608
  58.1 20.8 %time.2 = (bf16[8,40,1152]{2,1,0:T(8,128)(2,1)}, bf16[8,72,1152]{2,1,0:T(8,128)(2,1)}, bf16[288,2304]{1,0:T(8,128)(2,1)}, bf16[288,2304]{1,0:T(8,128)(2,1)}, bf1...) custom-call(s32[2]{0:T(128)} %pad_add_fusion.refs_0_.refs_10_, bf16[8,40,1152]{2,1,0:T(8,128)(2,1)} %copy-done.22, ...), custom_call_target="tpu_custom_call" | custom-call | flops 24999999488 | bytes 25000000 | tf_op jit(solution)/shard_map/time/pallas_call | solution.py:44
  79.9 10.7 %all-to-all-done.1.refs_1_.refs_2_ = bf16[8,72,1152]{2,1,0:T(8,128)(2,1)S(1)} async-done(((bf16[8,72,1152]{2,1,0:T(8,128)(2,1)}), bf16[8,72,1152]{2,1,0:T(8,128)(2,1)S(1)}, u32[]{:S(2)}, u32[]{:S(2)}) %all-to-all-start.1) | async-done | bytes 1327136 | tf_op jit(solution)/shard_map/all_to_all | solution.py:608
  90.6 4.0 %all-to-all-start.4 = ((bf16[8,40,1152]{2,1,0:T(8,128)(2,1)}), bf16[8,40,1152]{2,1,0:T(8,128)(2,1)S(1)}, u32[]{:S(2)}, u32[]{:S(2)}) async-start(bf16[8,40,1152]{2,1,0:T(8,128)(2,1)} %get-tuple-element.105), calls=%async_computation.4 | async-start | bytes 1474560 | tf_op jit(solution)/shard_map/all_to_all | solution.py:608
  94.6 21.5 %time.3 = (bf16[8,40,1152]{2,1,0:T(8,128)(2,1)}, bf16[8,72,1152]{2,1,0:T(8,128)(2,1)}, bf16[288,2304]{1,0:T(8,128)(2,1)}, bf16[288,2304]{1,0:T(8,128)(2,1)}, bf1...) custom-call(s32[2]{0:T(128)} %pad_add_fusion.refs_0_.refs_10_, bf16[8,72,1152]{2,1,0:T(8,128)(2,1)} %copy-done.18, ...), custom_call_target="tpu_custom_call" | custom-call | flops 24999999488 | bytes 25000000 | tf_op jit(solution)/shard_map/time/pallas_call | solution.py:44
  116.7 5.2 %all-to-all-start.5 = ((bf16[8,40,1152]{2,1,0:T(8,128)(2,1)}), bf16[8,40,1152]{2,1,0:T(8,128)(2,1)S(1)}, u32[]{:S(2)}, u32[]{:S(2)}) async-start(bf16[8,40,1152]{2,1,0:T(8,128)(2,1)} %get-tuple-element.123), calls=%async_computation.5 | async-start | bytes 1474560 | tf_op jit(solution)/shard_map/all_to_all | solution.py:608
  122.0 11.4 %space_backward.2 = (bf16[288,1152]{1,0:T(8,128)(2,1)}, bf16[288,2304]{1,0:T(8,128)(2,1)}, bf16[288,4608]{1,0:T(8,128)(2,1)}, f32[8,128]{1,0:T(8,128)}) custom-call(s32[2]{0:T(128)} %pad_add_fusion.refs_0_.refs_10_, bf16[8,40,1152]{2,1,0:T(8,128)(2,1)} %copy-done.21, f32[2,6,1152]{2,1,0:T(8,128)} %copy.25.refs_2_.refs_3_, bf16[1152,1152]{1,0:T(8,128)(2,1)} %refs_3_.11, ...), custom_call_target="tpu_custom_call" | custom-call | flops 15000000512 | bytes 15000000 | tf_op jit(solution)/shard_map/space_backward/pallas_call | solution.py:44
  134.0 14.9 %weights.2 = (bf16[2,288,1152]{2,1,0:T(8,128)(2,1)}, bf16[2,288,1152]{2,1,0:T(8,128)(2,1)}, bf16[1,576,1152]{2,1,0:T(8,128)(2,1)}, bf16[1,576,1152]{2,1,0:T(8,128)(2,1)}, f32[8,128]{1,0:T(8,128)}) custom-call(s32[2]{0:T(128)} %pad_add_fusion.refs_0_.refs_10_, bf16[288,2304]{1,0:T(8,128)(2,1)} %get-tuple-element.112.refs_1_, ...), custom_call_target="tpu_custom_call" | custom-call | flops 10000000000 | bytes 10000000 | tf_op jit(solution)/shard_map/weights/pallas_call | solution.py:44
  148.9 1.6 collective-permute-start.5
  150.4 1.5 collective-permute-start.6
  152.9 11.5 %space_backward.3 = (bf16[288,1152]{1,0:T(8,128)(2,1)}, bf16[288,2304]{1,0:T(8,128)(2,1)}, bf16[288,4608]{1,0:T(8,128)(2,1)}, f32[8,128]{1,0:T(8,128)}) custom-call(s32[2]{0:T(128)} %pad_add_fusion.refs_0_.refs_10_, bf16[8,40,1152]{2,1,0:T(8,128)(2,1)} %copy-done.19, f32[2,6,1152]{2,1,0:T(8,128)} %copy.25.refs_2_.refs_3_, bf16[1152,1152]{1,0:T(8,128)(2,1)} %refs_3_.11, ...), custom_call_target="tpu_custom_call" | custom-call | flops 15000000512 | bytes 15000000 | tf_op jit(solution)/shard_map/space_backward/pallas_call | solution.py:44
  164.5 5.2 %all-to-all-start.3 = ((bf16[8,72,1152]{2,1,0:T(8,128)(2,1)}), bf16[8,72,1152]{2,1,0:T(8,128)(2,1)}, u32[]{:S(2)}, u32[]{:S(2)}) async-start(bf16[8,72,1152]{2,1,0:T(8,128)(2,1)} %get-tuple-element.104), calls=%async_computation.3 | async-start | bytes 2654208 | tf_op jit(solution)/shard_map/all_to_all | solution.py:608
  169.7 10.6 %collective-permute-done.5.refs_3_ = bf16[2,288,1152]{2,1,0:T(8,128)(2,1)S(1)} collective-permute-done((bf16[2,288,1152]{2,1,0:T(8,128)(2,1)}, bf16[2,288,1152]{2,1,0:T(8,128)(2,1)S(1)}, u32[]{:S(2)}, u32[]{:S(2)}) %collective-permute-start.5) | collective-permute-done | bytes 1327136 | tf_op jit(solution)/shard_map/ppermute | solution.py:495
  180.3 1.2 collective-permute-done.6.refs_4_
  181.5 1.3 copy-done.4
  182.8 1.3 copy-done.5
  184.1 1.4 stage.4
  185.5 1.6 collective-permute-start.8
  187.7 14.8 %weights.3 = (bf16[2,288,960]{2,1,0:T(8,128)(2,1)}, bf16[2,288,960]{2,1,0:T(8,128)(2,1)}, bf16[1,576,960]{2,1,0:T(8,128)(2,1)}, bf16[1,576,960]{2,1,0:T(8,128)(2...) custom-call(s32[2]{0:T(128)} %pad_add_fusion.refs_0_.refs_10_, ...), custom_call_target="tpu_custom_call" | custom-call | flops 10000000000 | bytes 10000000 | tf_op jit(solution)/shard_map/weights/pallas_call | solution.py:44
  202.4 1.6 collective-permute-start.12
  204.5 2.0 collective-permute-start.14
  207.2 1.5 stage.5
  210.8 2.0 collective-permute-start.16
  212.7 9.5 %grad_input.2 = (bf16[288,1152]{1,0:T(8,128)(2,1)}, f32[8,128]{1,0:T(8,128)}) custom-call(bf16[288,4608]{1,0:T(8,128)(2,1)} %get-tuple-element.110.refs_5_.refs_0_, bf16[288,1152]{1,0:T(8,128)(2,1)} %get-tuple-element.111.refs_1_, bf16[2,288,1152]{2,1,0:T(8,128)(2,1)} %bitcast.11, f32[2,6,1152]{2,1,0:T(8,128)} %copy.25.refs_2_.refs_3_, ...), custom_call_target="tpu_custom_call" | custom-call | flops 8000000000 | bytes 8000000 | tf_op jit(solution)/shard_map/grad_input/pallas_call | solution.py:44
  222.3 9.3 %grad_input.3 = (bf16[288,1152]{1,0:T(8,128)(2,1)}, f32[8,128]{1,0:T(8,128)}) custom-call(bf16[288,4608]{1,0:T(8,128)(2,1)} %get-tuple-element.133.refs_6_.refs_0_, bf16[288,1152]{1,0:T(8,128)(2,1)} %get-tuple-element.140.refs_1_, bf16[2,288,1152]{2,1,0:T(8,128)(2,1)} %bitcast.12, f32[2,6,1152]{2,1,0:T(8,128)} %copy.25.refs_2_.refs_3_, ...), custom_call_target="tpu_custom_call" | custom-call | flops 8000000000 | bytes 8000000 | tf_op jit(solution)/shard_map/grad_input/pallas_call | solution.py:44
  232.3 1.6 last_stage.2
  234.1 2.1 stage.6
  236.2 1.6 collective-permute-start.17
  238.4 4.7 %join.1 = (bf16[2,288,1152]{2,1,0:T(8,128)(2,1)}, bf16[2,288,1152]{2,1,0:T(8,128)(2,1)}, f32[8,128]{1,0:T(8,128)}) custom-call(bf16[8,72,1152]{2,1,0:T(8,128)(2,1)} %all-to-all-done.3.refs_6_.refs_0_, bf16[576,576]{1,0:T(8,128)(2,1)} %constant.30.clone.refs_1_, bf16[288,1152]{1,0:T(8,128)(2,1)} %get-tuple-element.139.refs_2_, ...), custom_call_target="tpu_custom_call" | custom-call | flops 4000000000 | bytes 4000000 | tf_op jit(solution)/shard_map/join/pallas_call | solution.py:44
  243.8 5.1 %collective-permute-done.17.refs_4_ = bf16[1,288,960]{2,1,0:T(8,128)(2,1)S(1)} collective-permute-done((bf16[1,288,960]{2,1,0:T(8,128)(2,1)S(1)}, bf16[1,288,960]{2,1,0:T(8,128)(2,1)S(1)}, u32[]{:S(2)}, u32[]{:S(2)}) %collective-permute-start.17) | collective-permute-done | bytes 552992 | tf_op jit(solution)/shard_map/ppermute | solution.py:495
  248.9 1.2 collective-permute-done.18.refs_5_
  250.9 1.3 stage.7
  253.7 2.6 collective-permute-start.26
  256.3 1.6 collective-permute-done.22.refs_6_
  257.9 3.4 %collective-permute-done.20.refs_4_ = bf16[2,72,960]{2,1,0:T(8,128)(2,1)S(1)} collective-permute-done((bf16[2,72,960]{2,1,0:T(8,128)(2,1)S(1)}, bf16[2,72,960]{2,1,0:T(8,128)(2,1)S(1)}, u32[]{:S(2)}, u32[]{:S(2)}) %collective-permute-start.20) | collective-permute-done | bytes 276512 | tf_op jit(solution)/shard_map/ppermute | solution.py:495
  263.1 2.4 collective-permute-start.25
  265.5 9.4 %collective-permute-done.28.refs_4_ = bf16[36,2304]{1,0:T(8,128)(2,1)S(1)} collective-permute-done((bf16[36,2304]{1,0:T(8,128)(2,1)S(1)}, bf16[36,2304]{1,0:T(8,128)(2,1)S(1)}, u32[]{:S(2)}, u32[]{:S(2)}) %collective-permute-start.28) | collective-permute-done | bytes 165920 | tf_op jit(solution)/shard_map/ppermute | solution.py:495
  274.9 1.4 assemble.2
  276.3 2.6 collective-permute-done.23.refs_2_
  278.9 7.8 %collective-permute-done.25.refs_4_ = bf16[36,2304]{1,0:T(8,128)(2,1)S(1)} collective-permute-done((bf16[36,2304]{1,0:T(8,128)(2,1)S(1)}, bf16[36,2304]{1,0:T(8,128)(2,1)S(1)}, u32[]{:S(2)}, u32[]{:S(2)}) %collective-permute-start.25) | collective-permute-done | bytes 165920 | tf_op jit(solution)/shard_map/ppermute | solution.py:495
  286.8 1.4 assemble.3
  (94 shorter events, 15.9 us)
Async XLA Ops:
  3.4 6.5 %copy-start.23 = (f32[2,6,1152]{2,0,1:T(2,128)S(1)}, f32[2,6,1152]{2,0,1:T(2,128)}, u32[]{:S(2)}) copy-start(f32[2,6,1152]{2,0,1:T(2,128)} %param.19) | copy-start | bytes 165892
  3.4 26.4 %all-to-all-start = ((bf16[8,40,1152]{2,1,0:T(8,128)(2,1)}), bf16[8,40,1152]{2,1,0:T(8,128)(2,1)S(1)}, u32[]{:S(2)}, u32[]{:S(2)}) async-start(bf16[8,40,1152]{2,1,0:T(8,128)(2,1)} %get-tuple-element.98), calls=%async_computation | async-start | bytes 1474560 | tf_op jit(solution)/shard_map/all_to_all | solution.py:608
  22.3 94.3 %collective-permute-start = (bf16[288,2304]{1,0:T(8,128)(2,1)}, bf16[288,2304]{1,0:T(8,128)(2,1)S(1)}, u32[]{:S(2)}, u32[]{:S(2)}) collective-permute-start(bf16[288,2304]{1,0:T(8,128)(2,1)} %get-tuple-element.109.refs_1_), channel_id=1, source_target_pairs={{0,1},{1,0},{2,3},{3,2},{4,5},{5,4},{6,7},{7,6},{8,9},{9,8},{10,11... | collective-permute-start | bytes 3981320 | tf_op jit(solution)/shard_map/ppermute | solution.py:495
  29.8 3.8 %copy-start.20 = (bf16[8,40,1152]{2,1,0:T(8,128)(2,1)}, bf16[8,40,1152]{2,1,0:T(8,128)(2,1)S(1)}, u32[]{:S(2)}) copy-start(bf16[8,40,1152]{2,1,0:T(8,128)(2,1)S(1)} %all-to-all-done.refs_8_.refs_2_.refs_12_) | copy-start | bytes 2211844
  29.8 23.6 %all-to-all-start.2 = ((bf16[8,40,1152]{2,1,0:T(8,128)(2,1)}), bf16[8,40,1152]{2,1,0:T(8,128)(2,1)S(1)}, u32[]{:S(2)}, u32[]{:S(2)}) async-start(bf16[8,40,1152]{2,1,0:T(8,128)(2,1)} %get-tuple-element.100), calls=%async_computation.2 | async-start | bytes 1474560 | tf_op jit(solution)/shard_map/all_to_all | solution.py:608
  54.3 36.3 %all-to-all-start.1 = ((bf16[8,72,1152]{2,1,0:T(8,128)(2,1)}), bf16[8,72,1152]{2,1,0:T(8,128)(2,1)S(1)}, u32[]{:S(2)}, u32[]{:S(2)}) async-start(bf16[8,72,1152]{2,1,0:T(8,128)(2,1)} %get-tuple-element.99), calls=%async_computation.1 | async-start | bytes 2654208 | tf_op jit(solution)/shard_map/all_to_all | solution.py:608
  78.9 54.6 %collective-permute-start.1 = (bf16[288,2304]{1,0:T(8,128)(2,1)}, bf16[288,2304]{1,0:T(8,128)(2,1)}, u32[]{:S(2)}, u32[]{:S(2)}) collective-permute-start(bf16[288,2304]{1,0:T(8,128)(2,1)} %get-tuple-element.112.refs_1_), channel_id=1, source_target_pairs={{0,1},{1,0},{2,3},{3,2},{4,5},{5,4},{6,7},{7,6},{8,9},{9,8},{10,11... | collective-permute-start | bytes 3981320 | tf_op jit(solution)/shard_map/ppermute | solution.py:495
  79.4 54.6 %collective-permute-start.3 = (bf16[288,2304]{1,0:T(8,128)(2,1)}, bf16[288,2304]{1,0:T(8,128)(2,1)}, u32[]{:S(2)}, u32[]{:S(2)}) collective-permute-start(bf16[288,2304]{1,0:T(8,128)(2,1)} %get-tuple-element.116), channel_id=1, source_target_pairs={{0,1},{1,0},{2,3},{3,2},{4,5},{5,4},{6,7},{7,6},{8,9},{9,8},{10,11... | collective-permute-start | bytes 3981320 | tf_op jit(solution)/shard_map/ppermute | solution.py:495
  79.5 72.5 %collective-permute-start.7 = (bf16[288,2304]{1,0:T(8,128)(2,1)}, bf16[288,2304]{1,0:T(8,128)(2,1)}, u32[]{:S(2)}, u32[]{:S(2)}) collective-permute-start(bf16[288,2304]{1,0:T(8,128)(2,1)} %get-tuple-element.127.refs_2_), channel_id=1, source_target_pairs={{0,1},{1,0},{2,3},{3,2},{4,5},{5,4},{6,7},{7,6},{8,9},{9,8},{10,11... | collective-permute-start | bytes 3981320 | tf_op jit(solution)/shard_map/ppermute | solution.py:495
  90.6 4.0 %copy-start.18 = (bf16[8,72,1152]{2,1,0:T(8,128)(2,1)}, bf16[8,72,1152]{2,1,0:T(8,128)(2,1)S(1)}, u32[]{:S(2)}) copy-start(bf16[8,72,1152]{2,1,0:T(8,128)(2,1)S(1)} %all-to-all-done.1.refs_1_.refs_2_) | copy-start | bytes 3981316
  90.6 26.2 %all-to-all-start.4 = ((bf16[8,40,1152]{2,1,0:T(8,128)(2,1)}), bf16[8,40,1152]{2,1,0:T(8,128)(2,1)S(1)}, u32[]{:S(2)}, u32[]{:S(2)}) async-start(bf16[8,40,1152]{2,1,0:T(8,128)(2,1)} %get-tuple-element.105), calls=%async_computation.4 | async-start | bytes 1474560 | tf_op jit(solution)/shard_map/all_to_all | solution.py:608
  116.1 17.9 %collective-permute-start.2 = (bf16[288,2304]{1,0:T(8,128)(2,1)}, bf16[288,2304]{1,0:T(8,128)(2,1)}, u32[]{:S(2)}, u32[]{:S(2)}) collective-permute-start(bf16[288,2304]{1,0:T(8,128)(2,1)} %get-tuple-element.113.refs_2_), channel_id=1, source_target_pairs={{0,1},{1,0},{2,3},{3,2},{4,5},{5,4},{6,7},{7,6},{8,9},{9,8},{10,11... | collective-permute-start | bytes 3981320 | tf_op jit(solution)/shard_map/ppermute | solution.py:495
  116.6 5.4 %copy-start.24 = (bf16[288,2304]{1,0:T(8,128)(2,1)}, bf16[288,2304]{1,0:T(8,128)(2,1)S(1)}, u32[]{:S(2)}) copy-start(bf16[288,2304]{1,0:T(8,128)(2,1)S(1)} %collective-permute-done.refs_8_.refs_3_) | copy-start | bytes 3981316
  116.6 17.4 %collective-permute-start.4 = (bf16[288,2304]{1,0:T(8,128)(2,1)}, bf16[288,2304]{1,0:T(8,128)(2,1)}, u32[]{:S(2)}, u32[]{:S(2)}) collective-permute-start(bf16[288,2304]{1,0:T(8,128)(2,1)} %get-tuple-element.117), channel_id=1, source_target_pairs={{0,1},{1,0},{2,3},{3,2},{4,5},{5,4},{6,7},{7,6},{8,9},{9,8},{10,11... | collective-permute-start | bytes 3981320 | tf_op jit(solution)/shard_map/ppermute | solution.py:495
  116.7 5.3 %copy-start.21 = (bf16[8,40,1152]{2,1,0:T(8,128)(2,1)}, bf16[8,40,1152]{2,1,0:T(8,128)(2,1)S(1)}, u32[]{:S(2)}) copy-start(bf16[8,40,1152]{2,1,0:T(8,128)(2,1)S(1)} %all-to-all-done.4.refs_1_) | copy-start | bytes 2211844
  116.7 35.2 %all-to-all-start.5 = ((bf16[8,40,1152]{2,1,0:T(8,128)(2,1)}), bf16[8,40,1152]{2,1,0:T(8,128)(2,1)S(1)}, u32[]{:S(2)}, u32[]{:S(2)}) async-start(bf16[8,40,1152]{2,1,0:T(8,128)(2,1)} %get-tuple-element.123), calls=%async_computation.5 | async-start | bytes 1474560 | tf_op jit(solution)/shard_map/all_to_all | solution.py:608
  133.4 54.2 %collective-permute-start.10 = (bf16[288,2304]{1,0:T(8,128)(2,1)}, bf16[288,2304]{1,0:T(8,128)(2,1)}, u32[]{:S(2)}, u32[]{:S(2)}) collective-permute-start(bf16[288,2304]{1,0:T(8,128)(2,1)} %get-tuple-element.134), channel_id=1, source_target_pairs={{0,1},{1,0},{2,3},{3,2},{4,5},{5,4},{6,7},{7,6},{8,9},{9,8},{10,11... | collective-permute-start | bytes 3981320 | tf_op jit(solution)/shard_map/ppermute | solution.py:495
  148.9 31.4 %collective-permute-start.5 = (bf16[2,288,1152]{2,1,0:T(8,128)(2,1)}, bf16[2,288,1152]{2,1,0:T(8,128)(2,1)S(1)}, u32[]{:S(2)}, u32[]{:S(2)}) collective-permute-start(bf16[2,288,1152]{2,1,0:T(8,128)(2,1)} %get-tuple-element.121), channel_id=1, source_target_pairs={{0,8},{8,0},{16,24},{24,16},{1,9},{9,1},{17,25},{25,17},{2,10},{10... | collective-permute-start | bytes 3981320 | tf_op jit(solution)/shard_map/ppermute | solution.py:495
  150.4 31.0 %collective-permute-start.6 = (bf16[1,576,1152]{2,1,0:T(8,128)(2,1)}, bf16[1,576,1152]{2,1,0:T(8,128)(2,1)S(1)}, u32[]{:S(2)}, u32[]{:S(2)}) collective-permute-start(bf16[1,576,1152]{2,1,0:T(8,128)(2,1)} %get-tuple-element.122), channel_id=1, source_target_pairs={{0,16},{8,24},{16,0},{24,8},{1,17},{9,25},{17,1},{25,9},{2,18},{10... | collective-permute-start | bytes 3981320 | tf_op jit(solution)/shard_map/ppermute | solution.py:495
  164.4 23.3 %collective-permute-start.11 = (bf16[288,2304]{1,0:T(8,128)(2,1)}, bf16[288,2304]{1,0:T(8,128)(2,1)}, u32[]{:S(2)}, u32[]{:S(2)}) collective-permute-start(bf16[288,2304]{1,0:T(8,128)(2,1)} %get-tuple-element.135), channel_id=1, source_target_pairs={{0,1},{1,0},{2,3},{3,2},{4,5},{5,4},{6,7},{7,6},{8,9},{9,8},{10,11... | collective-permute-start | bytes 3981320 | tf_op jit(solution)/shard_map/ppermute | solution.py:495
  164.5 17.0 %copy-start = (s32[2]{0:T(128)S(1)}, s32[2]{0:T(128)}, u32[]{:S(2)}) copy-start(s32[2]{0:T(128)} %pad_add_fusion.refs_0_.refs_10_) | copy-start | bytes 28
  164.5 17.0 %copy-start.13 = (f32[8,128]{1,0:T(8,128)S(1)}, f32[8,128]{1,0:T(8,128)}, u32[]{:S(2)}) copy-start(f32[8,128]{1,0:T(8,128)} %get-tuple-element.128.refs_5_) | copy-start | bytes 12292
  164.5 57.7 %all-to-all-start.3 = ((bf16[8,72,1152]{2,1,0:T(8,128)(2,1)}), bf16[8,72,1152]{2,1,0:T(8,128)(2,1)}, u32[]{:S(2)}, u32[]{:S(2)}) async-start(bf16[8,72,1152]{2,1,0:T(8,128)(2,1)} %get-tuple-element.104), calls=%async_computation.3 | async-start | bytes 2654208 | tf_op jit(solution)/shard_map/all_to_all | solution.py:608
  185.5 2.1 copy-start.12
  185.5 21.0 %collective-permute-start.8 = (bf16[1,288,1152]{2,1,0:T(8,128)(2,1)S(1)}, bf16[1,288,1152]{2,1,0:T(8,128)(2,1)S(1)}, u32[]{:S(2)}, u32[]{:S(2)}) collective-permute-start(bf16[1,288,1152]{2,1,0:T(8,128)(2,1)S(1)} %get-tuple-element.131), channel_id=1, source_target_pairs={{0,16},{8,24},{16,0},{24,8},{1,17},{9,25},{17,1},{25,9},{2,18},{10... | collective-permute-start | bytes 1990664 | tf_op jit(solution)/shard_map/ppermute | solution.py:495
  187.1 19.4 %collective-permute-start.9 = (bf16[1,288,1152]{2,1,0:T(8,128)(2,1)S(1)}, bf16[1,288,1152]{2,1,0:T(8,128)(2,1)S(1)}, u32[]{:S(2)}, u32[]{:S(2)}) collective-permute-start(bf16[1,288,1152]{2,1,0:T(8,128)(2,1)S(1)} %get-tuple-element.132), channel_id=1, source_target_pairs={{0,8},{8,0},{16,24},{24,16},{1,9},{9,1},{17,25},{25,17},{2,10},{10... | collective-permute-start | bytes 1990664 | tf_op jit(solution)/shard_map/ppermute | solution.py:495
  187.7 18.8 %copy-start.1 = (s32[2]{0:T(128)S(1)}, s32[2]{0:T(128)}, u32[]{:S(2)}) copy-start(s32[2]{0:T(128)} %pad_add_fusion.refs_0_.refs_10_) | copy-start | bytes 28
  202.4 31.4 %collective-permute-start.12 = (bf16[2,288,960]{2,1,0:T(8,128)(2,1)}, bf16[2,288,960]{2,1,0:T(8,128)(2,1)S(1)}, u32[]{:S(2)}, u32[]{:S(2)}) collective-permute-start(bf16[2,288,960]{2,1,0:T(8,128)(2,1)} %get-tuple-element.146), channel_id=1, source_target_pairs={{0,8},{8,0},{16,24},{24,16},{1,9},{9,1},{17,25},{25,17},{2,10},{10... | collective-permute-start | bytes 3317768 | tf_op jit(solution)/shard_map/ppermute | solution.py:495
  204.0 29.9 %collective-permute-start.13 = (bf16[1,576,960]{2,1,0:T(8,128)(2,1)}, bf16[1,576,960]{2,1,0:T(8,128)(2,1)S(1)}, u32[]{:S(2)}, u32[]{:S(2)}) collective-permute-start(bf16[1,576,960]{2,1,0:T(8,128)(2,1)} %get-tuple-element.147), channel_id=1, source_target_pairs={{0,16},{8,24},{16,0},{24,8},{1,17},{9,25},{17,1},{25,9},{2,18},{10... | collective-permute-start | bytes 3317768 | tf_op jit(solution)/shard_map/ppermute | solution.py:495
  204.5 29.4 %collective-permute-start.14 = (bf16[8,72,384]{2,1,0:T(8,128)(2,1)}, bf16[8,72,384]{2,1,0:T(8,128)(2,1)S(1)}, u32[]{:S(2)}, u32[]{:S(2)}) collective-permute-start(bf16[8,72,384]{2,1,0:T(8,128)(2,1)} %get-tuple-element.148), channel_id=1, source_target_pairs={{0,2},{1,3},{2,0},{3,1},{4,6},{5,7},{6,4},{7,5},{8,10},{9,11},{10,... | collective-permute-start | bytes 1327112 | tf_op jit(solution)/shard_map/ppermute | solution.py:495
  210.7 20.9 %collective-permute-start.15 = (bf16[2,72,1152]{2,1,0:T(8,128)(2,1)}, bf16[2,72,1152]{2,1,0:T(8,128)(2,1)S(1)}, u32[]{:S(2)}, u32[]{:S(2)}) collective-permute-start(bf16[2,72,1152]{2,1,0:T(8,128)(2,1)} %get-tuple-element.151), channel_id=1, source_target_pairs={{0,2},{1,3},{2,0},{3,1},{4,6},{5,7},{6,4},{7,5},{8,10},{9,11},{10,... | collective-permute-start | bytes 995336 | tf_op jit(solution)/shard_map/ppermute | solution.py:495
  210.8 20.8 %collective-permute-start.16 = (bf16[2,72,1152]{2,1,0:T(8,128)(2,1)S(1)}, bf16[2,72,1152]{2,1,0:T(8,128)(2,1)}, u32[]{:S(2)}, u32[]{:S(2)}) collective-permute-start(bf16[2,72,1152]{2,1,0:T(8,128)(2,1)S(1)} %get-tuple-element.152), channel_id=1, source_target_pairs={{0,2},{1,3},{2,0},{3,1},{4,6},{5,7},{6,4},{7,5},{8,10},{9,11},{10,... | collective-permute-start | bytes 995336 | tf_op jit(solution)/shard_map/ppermute | solution.py:495
  222.2 9.4 %copy-start.8 = (bf16[2,72,1152]{2,1,0:T(8,128)(2,1)S(1)}, bf16[2,72,1152]{2,1,0:T(8,128)(2,1)}, u32[]{:S(2)}) copy-start(bf16[2,72,1152]{2,1,0:T(8,128)(2,1)} %copy-done.7) | copy-start | bytes 995332
  222.2 9.4 %copy-start.10 = (bf16[2,72,1152]{2,1,0:T(8,128)(2,1)S(1)}, bf16[2,72,1152]{2,1,0:T(8,128)(2,1)}, u32[]{:S(2)}) copy-start(bf16[2,72,1152]{2,1,0:T(8,128)(2,1)} %copy-done.9) | copy-start | bytes 995332
  232.3 1.8 copy-start.6
  236.2 2.2 copy-start.11
  236.2 12.7 %collective-permute-start.17 = (bf16[1,288,960]{2,1,0:T(8,128)(2,1)S(1)}, bf16[1,288,960]{2,1,0:T(8,128)(2,1)S(1)}, u32[]{:S(2)}, u32[]{:S(2)}) collective-permute-start(bf16[1,288,960]{2,1,0:T(8,128)(2,1)S(1)} %get-tuple-element.161), channel_id=1, source_target_pairs={{0,16},{8,24},{16,0},{24,8},{1,17},{9,25},{17,1},{25,9},{2,18},{10... | collective-permute-start | bytes 1658888 | tf_op jit(solution)/shard_map/ppermute | solution.py:495
  237.8 12.3 %collective-permute-start.18 = (bf16[4,72,960]{2,1,0:T(8,128)(2,1)S(1)}, bf16[4,72,960]{2,1,0:T(8,128)(2,1)S(1)}, u32[]{:S(2)}, u32[]{:S(2)}) collective-permute-start(bf16[4,72,960]{2,1,0:T(8,128)(2,1)S(1)} %get-tuple-element.162), channel_id=1, source_target_pairs={{0,2},{1,3},{2,0},{3,1},{4,6},{5,7},{6,4},{7,5},{8,10},{9,11},{10,... | collective-permute-start | bytes 1658888 | tf_op jit(solution)/shard_map/ppermute | solution.py:495
  237.9 5.9 %collective-permute-start.19 = (bf16[2,144,384]{2,1,0:T(8,128)(2,1)S(1)}, bf16[2,144,384]{2,1,0:T(8,128)(2,1)S(1)}, u32[]{:S(2)}, u32[]{:S(2)}) collective-permute-start(bf16[2,144,384]{2,1,0:T(8,128)(2,1)S(1)} %get-tuple-element.163), channel_id=1, source_target_pairs={{0,8},{8,0},{16,24},{24,16},{1,9},{9,1},{17,25},{25,17},{2,10},{10... | collective-permute-start | bytes 663560 | tf_op jit(solution)/shard_map/ppermute | solution.py:495
  252.2 9.1 %collective-permute-start.20 = (bf16[2,72,960]{2,1,0:T(8,128)(2,1)S(1)}, bf16[2,72,960]{2,1,0:T(8,128)(2,1)S(1)}, u32[]{:S(2)}, u32[]{:S(2)}) collective-permute-start(bf16[2,72,960]{2,1,0:T(8,128)(2,1)S(1)} %get-tuple-element.168), channel_id=1, source_target_pairs={{0,2},{1,3},{2,0},{3,1},{4,6},{5,7},{6,4},{7,5},{8,10},{9,11},{10,... | collective-permute-start | bytes 829448 | tf_op jit(solution)/shard_map/ppermute | solution.py:495
  252.6 8.7 %collective-permute-start.21 = (bf16[1,144,960]{2,1,0:T(8,128)(2,1)S(1)}, bf16[1,144,960]{2,1,0:T(8,128)(2,1)S(1)}, u32[]{:S(2)}, u32[]{:S(2)}) collective-permute-start(bf16[1,144,960]{2,1,0:T(8,128)(2,1)S(1)} %get-tuple-element.169), channel_id=1, source_target_pairs={{0,8},{8,0},{16,24},{24,16},{1,9},{9,1},{17,25},{25,17},{2,10},{10... | collective-permute-start | bytes 829448 | tf_op jit(solution)/shard_map/ppermute | solution.py:495
  253.2 4.7 %collective-permute-start.22 = (bf16[1,144,384]{2,1,0:T(8,128)(2,1)S(1)}, bf16[1,144,384]{2,1,0:T(8,128)(2,1)S(1)}, u32[]{:S(2)}, u32[]{:S(2)}) collective-permute-start(bf16[1,144,384]{2,1,0:T(8,128)(2,1)S(1)} %get-tuple-element.170), channel_id=1, source_target_pairs={{0,16},{8,24},{16,0},{24,8},{1,17},{9,25},{17,1},{25,9},{2,18},{10... | collective-permute-start | bytes 331784 | tf_op jit(solution)/shard_map/ppermute | solution.py:495
  253.7 9.4 %collective-permute-start.26 = (bf16[36,2304]{1,0:T(8,128)(2,1)S(1)}, bf16[36,2304]{1,0:T(8,128)(2,1)S(1)}, u32[]{:S(2)}, u32[]{:S(2)}) collective-permute-start(bf16[36,2304]{1,0:T(8,128)(2,1)S(1)} %get-tuple-element.177), channel_id=1, source_target_pairs={{0,4},{1,5},{2,6},{3,7},{4,0},{5,1},{6,2},{7,3},{8,12},{9,13},{10,... | collective-permute-start | bytes 497672 | tf_op jit(solution)/shard_map/ppermute | solution.py:495
  256.3 9.2 %collective-permute-start.27 = (bf16[36,2304]{1,0:T(8,128)(2,1)S(1)}, bf16[36,2304]{1,0:T(8,128)(2,1)S(1)}, u32[]{:S(2)}, u32[]{:S(2)}) collective-permute-start(bf16[36,2304]{1,0:T(8,128)(2,1)S(1)} %get-tuple-element.178), channel_id=1, source_target_pairs={{0,1},{1,0},{2,3},{3,2},{4,5},{5,4},{6,7},{7,6},{8,9},{9,8},{10,11... | collective-permute-start | bytes 497672 | tf_op jit(solution)/shard_map/ppermute | solution.py:495
  257.9 17.0 %collective-permute-start.28 = (bf16[36,2304]{1,0:T(8,128)(2,1)S(1)}, bf16[36,2304]{1,0:T(8,128)(2,1)S(1)}, u32[]{:S(2)}, u32[]{:S(2)}) collective-permute-start(bf16[36,2304]{1,0:T(8,128)(2,1)S(1)} %get-tuple-element.179), channel_id=1, source_target_pairs={{0,5},{1,4},{2,7},{3,6},{4,1},{5,0},{6,3},{7,2},{8,13},{9,12},{10,... | collective-permute-start | bytes 497672 | tf_op jit(solution)/shard_map/ppermute | solution.py:495
  262.4 16.5 %collective-permute-start.23 = (bf16[36,2304]{1,0:T(8,128)(2,1)S(1)}, bf16[36,2304]{1,0:T(8,128)(2,1)S(1)}, u32[]{:S(2)}, u32[]{:S(2)}) collective-permute-start(bf16[36,2304]{1,0:T(8,128)(2,1)S(1)} %get-tuple-element.173), channel_id=1, source_target_pairs={{0,4},{1,5},{2,6},{3,7},{4,0},{5,1},{6,2},{7,3},{8,12},{9,13},{10,... | collective-permute-start | bytes 497672 | tf_op jit(solution)/shard_map/ppermute | solution.py:495
  263.1 15.9 %collective-permute-start.24 = (bf16[36,2304]{1,0:T(8,128)(2,1)S(1)}, bf16[36,2304]{1,0:T(8,128)(2,1)S(1)}, u32[]{:S(2)}, u32[]{:S(2)}) collective-permute-start(bf16[36,2304]{1,0:T(8,128)(2,1)S(1)} %get-tuple-element.174), channel_id=1, source_target_pairs={{0,1},{1,0},{2,3},{3,2},{4,5},{5,4},{6,7},{7,6},{8,9},{9,8},{10,11... | collective-permute-start | bytes 497672 | tf_op jit(solution)/shard_map/ppermute | solution.py:495
  263.1 23.7 %collective-permute-start.25 = (bf16[36,2304]{1,0:T(8,128)(2,1)S(1)}, bf16[36,2304]{1,0:T(8,128)(2,1)S(1)}, u32[]{:S(2)}, u32[]{:S(2)}) collective-permute-start(bf16[36,2304]{1,0:T(8,128)(2,1)S(1)} %get-tuple-element.175), channel_id=1, source_target_pairs={{0,5},{1,4},{2,7},{3,6},{4,1},{5,0},{6,3},{7,2},{8,13},{9,12},{10,... | collective-permute-start | bytes 497672 | tf_op jit(solution)/shard_map/ppermute | solution.py:495
  (12 other events, 11.8 us)

commit v4 on v3

--- a/solution.py
+++ b/solution.py
@@ -723,24 +723,29 @@
             out_back = exchange(out_sent)
         d_middles.append(d_middle)
         space_units.append((left, left_got, right, exchange_units(sent)))
+    grad_input = []
+
+    def next_grad(deps):
+        v = len(grad_input)
+        one_grad, token = grad_of(v, space_units[v], d_middles[v], deps=deps)
+        grad_input.append(one_grad)
+        return token
+
+    token = next_grad([token])
     token = time_sum.stage(deps=[token])
     space_sum, token = weights(space_units, True, deps=[token])
     token = time_sum.stage(deps=[token])
-    grad_input = []
-    for v in range(videos):
-        one_grad, token = grad_of(
-            v, space_units[v], d_middles[v], deps=[token, out_back] if v else [token]
-        )
-        grad_input.append(one_grad)
+    while len(grad_input) < videos:
+        token = next_grad([token, out_back])
     token = time_sum.last_stage(deps=[token])
     token = space_sum.stage(deps=[token])
     block_out, grad_input, token = call(
         "join", 4, join_kernel, "vv" + "v" * videos, (all_rows, all_rows), "vv"
     )(out_back, from_joint, *grad_input, deps=[token])
+    *grad_time, token = time_sum.finish(deps=[token])
     token = space_sum.stage(deps=[token])
-    token = space_sum.last_stage(deps=[token])
-    *grad_time, token = time_sum.finish(deps=[token])
-    *grad_space, _ = space_sum.finish(deps=[token])
+    space_sum.last_stage(deps=[token])
+    *grad_space, _ = space_sum.finish()
     return (
         block_out.reshape(frames_in.shape), grad_input.reshape(frames_in.shape),
         *grad_space, *grad_time,

time: 294 us -> 298 us (1.014)
  starting transfers between devices: 51.9 us -> 55 us
    ppermute x29, starting transfers between devices: 23.5 us -> 27 us  [swap(): return lax.ppermute(x, axis, [(i, i ^ mask) for i in range(size)])]
    unnamed x51 -> x57, local copies, waits for them, and re-layouts: 9.41 us -> 11 us
  transfers between devices with their start and end apart: 35 -> 35, of which waited for: 13 -> 14; matrix products, arithmetic and copies ran while one was open for 0% -> 0% of each run, Pallas kernels for 52% -> 52%
where the time goes in v4:
time: 298 us; the launch traced here: 293 us
  Pallas kernels  159 us (53%)
  waiting for transfers between devices  66.1 us (22%)
  starting transfers between devices  55 us (18%)
  local copies, waits for them, and re-layouts  11 us (4%)
    pallas_call x20, Pallas kernels, run(): pl.pallas_call(with_token, out_shape=(*out_shape, TOKEN), in_specs=[pl.Bl...  159 us
    ppermute x29, waiting for transfers between devices, swap(): return lax.ppermute(x, axis, [(i, i ^ mask) for i in range(size)])  42.6 us
    all_to_all x6, starting transfers between devices, exchange(): lax.all_to_all(pieces, 'seq', split_axis=0, concat_axis=0, tiled=True)  28.1 us
    ppermute x29, starting transfers between devices, swap(): return lax.ppermute(x, axis, [(i, i ^ mask) for i in range(size)])  27 us
    all_to_all x6, waiting for transfers between devices, exchange(): lax.all_to_all(pieces, 'seq', split_axis=0, concat_axis=0, tiled=True)  23.5 us
    unnamed x57, local copies, waits for them, and re-layouts  11 us
  transfers between devices with their start and end apart: 35, of which 14 were waited for; matrix products, arithmetic and copies ran while one was open for 0% of the time, Pallas kernels for 52%

profile of v4, /device:TPU:0, one launch (start us, length us, event | category | flops | bytes accessed | tf_op | source)
XLA Modules:
  0.0 292.9 jit_solution(11318187756715274026)
XLA Ops:
  0.6 2.8 split.1
  3.4 6.5 %all-to-all-start = ((bf16[8,40,1152]{2,1,0:T(8,128)(2,1)}), bf16[8,40,1152]{2,1,0:T(8,128)(2,1)S(1)}, u32[]{:S(2)}, u32[]{:S(2)}) async-start(bf16[8,40,1152]{2,1,0:T(8,128)(2,1)} %get-tuple-element.97), calls=%async_computation | async-start | bytes 1474560 | tf_op jit(solution)/shard_map/all_to_all | solution.py:608
  10.5 11.8 %space_forward.2 = (bf16[8,40,1152]{2,1,0:T(8,128)(2,1)}, bf16[288,3456]{1,0:T(8,128)(2,1)}, bf16[288,2304]{1,0:T(8,128)(2,1)}, bf16[16,144,288]{2,1,0:T(8,128)(2,1)}, f32[8,128]{1,0:T(8,128)}) custom-call(bf16[2,288,1152]{2,1,0:T(8,128)(2,1)} %bitcast.9, bf16[2,288,1152]{2,1,0:T(8,128)(2,1)} %bitcast.7, f32[2,6,1152]{2,1,0:T(8,128)} %copy.25.refs_2_.refs_3_, ...), custom_call_target="tpu_custom_call" | custom-call | flops 14000000000 | bytes 14000000 | tf_op jit(solution)/shard_map/space_forward/pallas_call | solution.py:44
  23.4 6.3 %all-to-all-done.refs_8_.refs_2_.refs_12_ = bf16[8,40,1152]{2,1,0:T(8,128)(2,1)S(1)} async-done(((bf16[8,40,1152]{2,1,0:T(8,128)(2,1)}), bf16[8,40,1152]{2,1,0:T(8,128)(2,1)S(1)}, u32[]{:S(2)}, u32[]{:S(2)}) %all-to-all-start) | async-done | bytes 737312 | tf_op jit(solution)/shard_map/all_to_all | solution.py:608
  29.8 3.8 %all-to-all-start.2 = ((bf16[8,40,1152]{2,1,0:T(8,128)(2,1)}), bf16[8,40,1152]{2,1,0:T(8,128)(2,1)S(1)}, u32[]{:S(2)}, u32[]{:S(2)}) async-start(bf16[8,40,1152]{2,1,0:T(8,128)(2,1)} %get-tuple-element.99), calls=%async_computation.2 | async-start | bytes 1474560 | tf_op jit(solution)/shard_map/all_to_all | solution.py:608
  33.6 13.4 %space_forward.3 = (bf16[8,72,1152]{2,1,0:T(8,128)(2,1)}, bf16[288,3456]{1,0:T(8,128)(2,1)}, bf16[288,2304]{1,0:T(8,128)(2,1)}, bf16[16,144,288]{2,1,0:T(8,128)(2,1)}, f32[8,128]{1,0:T(8,128)}) custom-call(bf16[2,288,1152]{2,1,0:T(8,128)(2,1)} %bitcast.10, bf16[2,288,1152]{2,1,0:T(8,128)(2,1)} %bitcast.8, f32[2,6,1152]{2,1,0:T(8,128)} %copy.25.refs_2_.refs_3_, ...), custom_call_target="tpu_custom_call" | custom-call | flops 14000000000 | bytes 14000000 | tf_op jit(solution)/shard_map/space_forward/pallas_call | solution.py:44
  46.9 6.4 %all-to-all-done.2.refs_1_ = bf16[8,40,1152]{2,1,0:T(8,128)(2,1)S(1)} async-done(((bf16[8,40,1152]{2,1,0:T(8,128)(2,1)}), bf16[8,40,1152]{2,1,0:T(8,128)(2,1)S(1)}, u32[]{:S(2)}, u32[]{:S(2)}) %all-to-all-start.2) | async-done | bytes 737312 | tf_op jit(solution)/shard_map/all_to_all | solution.py:608
  54.3 3.8 %all-to-all-start.1 = ((bf16[8,72,1152]{2,1,0:T(8,128)(2,1)}), bf16[8,72,1152]{2,1,0:T(8,128)(2,1)S(1)}, u32[]{:S(2)}, u32[]{:S(2)}) async-start(bf16[8,72,1152]{2,1,0:T(8,128)(2,1)} %get-tuple-element.98), calls=%async_computation.1 | async-start | bytes 2654208 | tf_op jit(solution)/shard_map/all_to_all | solution.py:608
  58.1 20.7 %time.2 = (bf16[8,40,1152]{2,1,0:T(8,128)(2,1)}, bf16[8,72,1152]{2,1,0:T(8,128)(2,1)}, bf16[288,2304]{1,0:T(8,128)(2,1)}, bf16[288,2304]{1,0:T(8,128)(2,1)}, bf1...) custom-call(s32[2]{0:T(128)} %pad_add_fusion.refs_0_.refs_10_, bf16[8,40,1152]{2,1,0:T(8,128)(2,1)} %copy-done.24, ...), custom_call_target="tpu_custom_call" | custom-call | flops 24999999488 | bytes 25000000 | tf_op jit(solution)/shard_map/time/pallas_call | solution.py:44
  79.8 10.8 %all-to-all-done.1.refs_1_.refs_2_ = bf16[8,72,1152]{2,1,0:T(8,128)(2,1)S(1)} async-done(((bf16[8,72,1152]{2,1,0:T(8,128)(2,1)}), bf16[8,72,1152]{2,1,0:T(8,128)(2,1)S(1)}, u32[]{:S(2)}, u32[]{:S(2)}) %all-to-all-start.1) | async-done | bytes 1327136 | tf_op jit(solution)/shard_map/all_to_all | solution.py:608
  90.6 4.0 %all-to-all-start.4 = ((bf16[8,40,1152]{2,1,0:T(8,128)(2,1)}), bf16[8,40,1152]{2,1,0:T(8,128)(2,1)S(1)}, u32[]{:S(2)}, u32[]{:S(2)}) async-start(bf16[8,40,1152]{2,1,0:T(8,128)(2,1)} %get-tuple-element.104), calls=%async_computation.4 | async-start | bytes 1474560 | tf_op jit(solution)/shard_map/all_to_all | solution.py:608
  94.6 21.6 %time.3 = (bf16[8,40,1152]{2,1,0:T(8,128)(2,1)}, bf16[8,72,1152]{2,1,0:T(8,128)(2,1)}, bf16[288,2304]{1,0:T(8,128)(2,1)}, bf16[288,2304]{1,0:T(8,128)(2,1)}, bf1...) custom-call(s32[2]{0:T(128)} %pad_add_fusion.refs_0_.refs_10_, bf16[8,72,1152]{2,1,0:T(8,128)(2,1)} %copy-done.20, ...), custom_call_target="tpu_custom_call" | custom-call | flops 24999999488 | bytes 25000000 | tf_op jit(solution)/shard_map/time/pallas_call | solution.py:44
  116.7 5.0 %all-to-all-start.5 = ((bf16[8,40,1152]{2,1,0:T(8,128)(2,1)}), bf16[8,40,1152]{2,1,0:T(8,128)(2,1)S(1)}, u32[]{:S(2)}, u32[]{:S(2)}) async-start(bf16[8,40,1152]{2,1,0:T(8,128)(2,1)} %get-tuple-element.111), calls=%async_computation.5 | async-start | bytes 1474560 | tf_op jit(solution)/shard_map/all_to_all | solution.py:608
  122.7 11.4 %space_backward.2 = (bf16[288,1152]{1,0:T(8,128)(2,1)}, bf16[288,2304]{1,0:T(8,128)(2,1)}, bf16[288,4608]{1,0:T(8,128)(2,1)}, f32[8,128]{1,0:T(8,128)}) custom-call(s32[2]{0:T(128)} %pad_add_fusion.refs_0_.refs_10_, bf16[8,40,1152]{2,1,0:T(8,128)(2,1)} %copy-done.23, f32[2,6,1152]{2,1,0:T(8,128)} %copy.25.refs_2_.refs_3_, bf16[1152,1152]{1,0:T(8,128)(2,1)} %refs_3_.11, ...), custom_call_target="tpu_custom_call" | custom-call | flops 15000000512 | bytes 15000000 | tf_op jit(solution)/shard_map/space_backward/pallas_call | solution.py:44
  135.9 14.9 %weights.2 = (bf16[2,288,1152]{2,1,0:T(8,128)(2,1)}, bf16[2,288,1152]{2,1,0:T(8,128)(2,1)}, bf16[1,576,1152]{2,1,0:T(8,128)(2,1)}, bf16[1,576,1152]{2,1,0:T(8,128)(2,1)}, f32[8,128]{1,0:T(8,128)}) custom-call(s32[2]{0:T(128)} %pad_add_fusion.refs_0_.refs_10_, bf16[288,2304]{1,0:T(8,128)(2,1)} %get-tuple-element.114.refs_1_, ...), custom_call_target="tpu_custom_call" | custom-call | flops 10000000000 | bytes 10000000 | tf_op jit(solution)/shard_map/weights/pallas_call | solution.py:44
  150.8 1.5 collective-permute-start.6
  152.3 1.5 collective-permute-start.7
  154.7 11.5 %space_backward.3 = (bf16[288,1152]{1,0:T(8,128)(2,1)}, bf16[288,2304]{1,0:T(8,128)(2,1)}, bf16[288,4608]{1,0:T(8,128)(2,1)}, f32[8,128]{1,0:T(8,128)}) custom-call(s32[2]{0:T(128)} %pad_add_fusion.refs_0_.refs_10_, bf16[8,40,1152]{2,1,0:T(8,128)(2,1)} %copy-done.21, f32[2,6,1152]{2,1,0:T(8,128)} %copy.25.refs_2_.refs_3_, bf16[1152,1152]{1,0:T(8,128)(2,1)} %refs_3_.11, ...), custom_call_target="tpu_custom_call" | custom-call | flops 15000000512 | bytes 15000000 | tf_op jit(solution)/shard_map/space_backward/pallas_call | solution.py:44
  166.3 5.0 %all-to-all-start.3 = ((bf16[8,72,1152]{2,1,0:T(8,128)(2,1)}), bf16[8,72,1152]{2,1,0:T(8,128)(2,1)}, u32[]{:S(2)}, u32[]{:S(2)}) async-start(bf16[8,72,1152]{2,1,0:T(8,128)(2,1)} %get-tuple-element.103), calls=%async_computation.3 | async-start | bytes 2654208 | tf_op jit(solution)/shard_map/all_to_all | solution.py:608
  171.4 9.3 %grad_input.2 = (bf16[288,1152]{1,0:T(8,128)(2,1)}, f32[8,128]{1,0:T(8,128)}) custom-call(bf16[288,4608]{1,0:T(8,128)(2,1)} %get-tuple-element.109.refs_0_.refs_5_, bf16[288,1152]{1,0:T(8,128)(2,1)} %get-tuple-element.110.refs_1_, bf16[2,288,1152]{2,1,0:T(8,128)(2,1)} %bitcast.11, f32[2,6,1152]{2,1,0:T(8,128)} %copy.25.refs_2_.refs_3_, ...), custom_call_target="tpu_custom_call" | custom-call | flops 8000000000 | bytes 8000000 | tf_op jit(solution)/shard_map/grad_input/pallas_call | solution.py:44
  180.7 1.5 collective-permute-done.6.refs_3_
  183.5 1.3 copy-done.5
  185.5 1.4 stage.4
  187.8 1.5 collective-permute-start.8
  189.9 15.1 %weights.3 = (bf16[2,288,960]{2,1,0:T(8,128)(2,1)}, bf16[2,288,960]{2,1,0:T(8,128)(2,1)}, bf16[1,576,960]{2,1,0:T(8,128)(2,1)}, bf16[1,576,960]{2,1,0:T(8,128)(2...) custom-call(s32[2]{0:T(128)} %pad_add_fusion.refs_0_.refs_10_, ...), custom_call_target="tpu_custom_call" | custom-call | flops 10000000000 | bytes 10000000 | tf_op jit(solution)/shard_map/weights/pallas_call | solution.py:44
  204.9 1.5 collective-permute-start.12
  207.0 2.0 collective-permute-start.14
  209.7 1.5 stage.5
  213.3 2.0 collective-permute-start.16
  215.3 9.3 %grad_input.3 = (bf16[288,1152]{1,0:T(8,128)(2,1)}, f32[8,128]{1,0:T(8,128)}) custom-call(bf16[288,4608]{1,0:T(8,128)(2,1)} %get-tuple-element.125.refs_6_.refs_0_, bf16[288,1152]{1,0:T(8,128)(2,1)} %get-tuple-element.126.refs_1_, bf16[2,288,1152]{2,1,0:T(8,128)(2,1)} %bitcast.12, f32[2,6,1152]{2,1,0:T(8,128)} %copy.25.refs_2_.refs_3_, ...), custom_call_target="tpu_custom_call" | custom-call | flops 8000000000 | bytes 8000000 | tf_op jit(solution)/shard_map/grad_input/pallas_call | solution.py:44
  224.6 2.9 collective-permute-done.15.refs_3_
  227.4 4.8 %collective-permute-done.16.refs_4_ = bf16[2,72,1152]{2,1,0:T(8,128)(2,1)} collective-permute-done((bf16[2,72,1152]{2,1,0:T(8,128)(2,1)S(1)}, bf16[2,72,1152]{2,1,0:T(8,128)(2,1)}, u32[]{:S(2)}, u32[]{:S(2)}) %collective-permute-start.16) | collective-permute-done | bytes 331808 | tf_op jit(solution)/shard_map/ppermute | solution.py:495
  232.9 1.6 last_stage.2
  234.5 2.7 collective-permute-start.20
  237.3 2.1 stage.6
  239.4 1.6 collective-permute-start.17
  241.0 1.5 collective-permute-start.18
  244.2 4.7 %join.1 = (bf16[2,288,1152]{2,1,0:T(8,128)(2,1)}, bf16[2,288,1152]{2,1,0:T(8,128)(2,1)}, f32[8,128]{1,0:T(8,128)}) custom-call(bf16[8,72,1152]{2,1,0:T(8,128)(2,1)} %all-to-all-done.3.refs_6_.refs_0_, bf16[576,576]{1,0:T(8,128)(2,1)} %constant.30.clone.refs_1_, bf16[288,1152]{1,0:T(8,128)(2,1)} %get-tuple-element.124.refs_2_, ...), custom_call_target="tpu_custom_call" | custom-call | flops 4000000000 | bytes 4000000 | tf_op jit(solution)/shard_map/join/pallas_call | solution.py:44
  248.9 8.0 %collective-permute-done.22.refs_4_ = bf16[36,2304]{1,0:T(8,128)(2,1)S(1)} collective-permute-done((bf16[36,2304]{1,0:T(8,128)(2,1)S(1)}, bf16[36,2304]{1,0:T(8,128)(2,1)S(1)}, u32[]{:S(2)}, u32[]{:S(2)}) %collective-permute-start.22) | collective-permute-done | bytes 165920 | tf_op jit(solution)/shard_map/ppermute | solution.py:495
  257.6 1.4 assemble.2
  259.0 1.3 stage.7
  262.5 4.3 %collective-permute-done.25.refs_6_ = bf16[1,144,384]{2,1,0:T(8,128)(2,1)S(1)} collective-permute-done((bf16[1,144,384]{2,1,0:T(8,128)(2,1)S(1)}, bf16[1,144,384]{2,1,0:T(8,128)(2,1)S(1)}, u32[]{:S(2)}, u32[]{:S(2)}) %collective-permute-start.25) | collective-permute-done | bytes 110624 | tf_op jit(solution)/shard_map/ppermute | solution.py:495
  266.9 2.9 collective-permute-done.23.refs_4_
  269.9 1.6 last_stage.3
  271.5 2.7 collective-permute-start.26
  274.6 13.0 %collective-permute-done.26.refs_2_ = bf16[36,2304]{1,0:T(8,128)(2,1)S(1)} collective-permute-done((bf16[36,2304]{1,0:T(8,128)(2,1)S(1)}, bf16[36,2304]{1,0:T(8,128)(2,1)S(1)}, u32[]{:S(2)}, u32[]{:S(2)}) %collective-permute-start.26) | collective-permute-done | bytes 165920 | tf_op jit(solution)/shard_map/ppermute | solution.py:495
  287.6 3.4 %collective-permute-done.28.refs_4_ = bf16[36,2304]{1,0:T(8,128)(2,1)S(1)} collective-permute-done((bf16[36,2304]{1,0:T(8,128)(2,1)S(1)}, bf16[36,2304]{1,0:T(8,128)(2,1)S(1)}, u32[]{:S(2)}, u32[]{:S(2)}) %collective-permute-start.28) | collective-permute-done | bytes 165920 | tf_op jit(solution)/shard_map/ppermute | solution.py:495
  291.0 1.4 assemble.3
  (100 shorter events, 20.4 us)
Async XLA Ops:
  3.4 6.5 %copy-start.25 = (f32[2,6,1152]{2,0,1:T(2,128)S(1)}, f32[2,6,1152]{2,0,1:T(2,128)}, u32[]{:S(2)}) copy-start(f32[2,6,1152]{2,0,1:T(2,128)} %param.19) | copy-start | bytes 165892
  3.4 26.4 %all-to-all-start = ((bf16[8,40,1152]{2,1,0:T(8,128)(2,1)}), bf16[8,40,1152]{2,1,0:T(8,128)(2,1)S(1)}, u32[]{:S(2)}, u32[]{:S(2)}) async-start(bf16[8,40,1152]{2,1,0:T(8,128)(2,1)} %get-tuple-element.97), calls=%async_computation | async-start | bytes 1474560 | tf_op jit(solution)/shard_map/all_to_all | solution.py:608
  22.3 99.4 %collective-permute-start = (bf16[288,2304]{1,0:T(8,128)(2,1)}, bf16[288,2304]{1,0:T(8,128)(2,1)S(1)}, u32[]{:S(2)}, u32[]{:S(2)}) collective-permute-start(bf16[288,2304]{1,0:T(8,128)(2,1)} %get-tuple-element.108.refs_1_), channel_id=1, source_target_pairs={{0,1},{1,0},{2,3},{3,2},{4,5},{5,4},{6,7},{7,6},{8,9},{9,8},{10,11... | collective-permute-start | bytes 3981320 | tf_op jit(solution)/shard_map/ppermute | solution.py:495
  29.8 23.6 %all-to-all-start.2 = ((bf16[8,40,1152]{2,1,0:T(8,128)(2,1)}), bf16[8,40,1152]{2,1,0:T(8,128)(2,1)S(1)}, u32[]{:S(2)}, u32[]{:S(2)}) async-start(bf16[8,40,1152]{2,1,0:T(8,128)(2,1)} %get-tuple-element.99), calls=%async_computation.2 | async-start | bytes 1474560 | tf_op jit(solution)/shard_map/all_to_all | solution.py:608
  54.3 36.3 %all-to-all-start.1 = ((bf16[8,72,1152]{2,1,0:T(8,128)(2,1)}), bf16[8,72,1152]{2,1,0:T(8,128)(2,1)S(1)}, u32[]{:S(2)}, u32[]{:S(2)}) async-start(bf16[8,72,1152]{2,1,0:T(8,128)(2,1)} %get-tuple-element.98), calls=%async_computation.1 | async-start | bytes 2654208 | tf_op jit(solution)/shard_map/all_to_all | solution.py:608
  78.8 55.4 %collective-permute-start.1 = (bf16[288,2304]{1,0:T(8,128)(2,1)}, bf16[288,2304]{1,0:T(8,128)(2,1)}, u32[]{:S(2)}, u32[]{:S(2)}) collective-permute-start(bf16[288,2304]{1,0:T(8,128)(2,1)} %get-tuple-element.114.refs_1_), channel_id=1, source_target_pairs={{0,1},{1,0},{2,3},{3,2},{4,5},{5,4},{6,7},{7,6},{8,9},{9,8},{10,11... | collective-permute-start | bytes 3981320 | tf_op jit(solution)/shard_map/ppermute | solution.py:495
  79.3 55.5 %collective-permute-start.3 = (bf16[288,2304]{1,0:T(8,128)(2,1)}, bf16[288,2304]{1,0:T(8,128)(2,1)}, u32[]{:S(2)}, u32[]{:S(2)}) collective-permute-start(bf16[288,2304]{1,0:T(8,128)(2,1)} %get-tuple-element.118), channel_id=1, source_target_pairs={{0,1},{1,0},{2,3},{3,2},{4,5},{5,4},{6,7},{7,6},{8,9},{9,8},{10,11... | collective-permute-start | bytes 3981320 | tf_op jit(solution)/shard_map/ppermute | solution.py:495
  79.4 74.5 %collective-permute-start.5 = (bf16[288,2304]{1,0:T(8,128)(2,1)}, bf16[288,2304]{1,0:T(8,128)(2,1)}, u32[]{:S(2)}, u32[]{:S(2)}) collective-permute-start(bf16[288,2304]{1,0:T(8,128)(2,1)} %get-tuple-element.122.refs_2_), channel_id=1, source_target_pairs={{0,1},{1,0},{2,3},{3,2},{4,5},{5,4},{6,7},{7,6},{8,9},{9,8},{10,11... | collective-permute-start | bytes 3981320 | tf_op jit(solution)/shard_map/ppermute | solution.py:495
  90.6 4.0 %copy-start.20 = (bf16[8,72,1152]{2,1,0:T(8,128)(2,1)}, bf16[8,72,1152]{2,1,0:T(8,128)(2,1)S(1)}, u32[]{:S(2)}) copy-start(bf16[8,72,1152]{2,1,0:T(8,128)(2,1)S(1)} %all-to-all-done.1.refs_1_.refs_2_) | copy-start | bytes 3981316
  90.6 26.1 %all-to-all-start.4 = ((bf16[8,40,1152]{2,1,0:T(8,128)(2,1)}), bf16[8,40,1152]{2,1,0:T(8,128)(2,1)S(1)}, u32[]{:S(2)}, u32[]{:S(2)}) async-start(bf16[8,40,1152]{2,1,0:T(8,128)(2,1)} %get-tuple-element.104), calls=%async_computation.4 | async-start | bytes 1474560 | tf_op jit(solution)/shard_map/all_to_all | solution.py:608
  116.2 18.6 %collective-permute-start.2 = (bf16[288,2304]{1,0:T(8,128)(2,1)}, bf16[288,2304]{1,0:T(8,128)(2,1)}, u32[]{:S(2)}, u32[]{:S(2)}) collective-permute-start(bf16[288,2304]{1,0:T(8,128)(2,1)} %get-tuple-element.115.refs_2_), channel_id=1, source_target_pairs={{0,1},{1,0},{2,3},{3,2},{4,5},{5,4},{6,7},{7,6},{8,9},{9,8},{10,11... | collective-permute-start | bytes 3981320 | tf_op jit(solution)/shard_map/ppermute | solution.py:495
  116.7 5.6 %copy-start.23 = (bf16[8,40,1152]{2,1,0:T(8,128)(2,1)}, bf16[8,40,1152]{2,1,0:T(8,128)(2,1)S(1)}, u32[]{:S(2)}) copy-start(bf16[8,40,1152]{2,1,0:T(8,128)(2,1)S(1)} %all-to-all-done.4.refs_1_) | copy-start | bytes 2211844
  116.7 37.2 %all-to-all-start.5 = ((bf16[8,40,1152]{2,1,0:T(8,128)(2,1)}), bf16[8,40,1152]{2,1,0:T(8,128)(2,1)S(1)}, u32[]{:S(2)}, u32[]{:S(2)}) async-start(bf16[8,40,1152]{2,1,0:T(8,128)(2,1)} %get-tuple-element.111), calls=%async_computation.5 | async-start | bytes 1474560 | tf_op jit(solution)/shard_map/all_to_all | solution.py:608
  121.7 13.1 %collective-permute-start.4 = (bf16[288,2304]{1,0:T(8,128)(2,1)}, bf16[288,2304]{1,0:T(8,128)(2,1)S(1)}, u32[]{:S(2)}, u32[]{:S(2)}) collective-permute-start(bf16[288,2304]{1,0:T(8,128)(2,1)} %get-tuple-element.119), channel_id=1, source_target_pairs={{0,1},{1,0},{2,3},{3,2},{4,5},{5,4},{6,7},{7,6},{8,9},{9,8},{10,11... | collective-permute-start | bytes 3981320 | tf_op jit(solution)/shard_map/ppermute | solution.py:495
  134.2 55.6 %collective-permute-start.10 = (bf16[288,2304]{1,0:T(8,128)(2,1)}, bf16[288,2304]{1,0:T(8,128)(2,1)}, u32[]{:S(2)}, u32[]{:S(2)}) collective-permute-start(bf16[288,2304]{1,0:T(8,128)(2,1)} %get-tuple-element.136), channel_id=1, source_target_pairs={{0,1},{1,0},{2,3},{3,2},{4,5},{5,4},{6,7},{7,6},{8,9},{9,8},{10,11... | collective-permute-start | bytes 3981320 | tf_op jit(solution)/shard_map/ppermute | solution.py:495
  150.8 31.4 %collective-permute-start.6 = (bf16[2,288,1152]{2,1,0:T(8,128)(2,1)}, bf16[2,288,1152]{2,1,0:T(8,128)(2,1)S(1)}, u32[]{:S(2)}, u32[]{:S(2)}) collective-permute-start(bf16[2,288,1152]{2,1,0:T(8,128)(2,1)} %get-tuple-element.129), channel_id=1, source_target_pairs={{0,8},{8,0},{16,24},{24,16},{1,9},{9,1},{17,25},{25,17},{2,10},{10... | collective-permute-start | bytes 3981320 | tf_op jit(solution)/shard_map/ppermute | solution.py:495
  152.3 31.1 %collective-permute-start.7 = (bf16[1,576,1152]{2,1,0:T(8,128)(2,1)}, bf16[1,576,1152]{2,1,0:T(8,128)(2,1)S(1)}, u32[]{:S(2)}, u32[]{:S(2)}) collective-permute-start(bf16[1,576,1152]{2,1,0:T(8,128)(2,1)} %get-tuple-element.130), channel_id=1, source_target_pairs={{0,16},{8,24},{16,0},{24,8},{1,17},{9,25},{17,1},{25,9},{2,18},{10... | collective-permute-start | bytes 3981320 | tf_op jit(solution)/shard_map/ppermute | solution.py:495
  166.2 23.6 %collective-permute-start.11 = (bf16[288,2304]{1,0:T(8,128)(2,1)}, bf16[288,2304]{1,0:T(8,128)(2,1)}, u32[]{:S(2)}, u32[]{:S(2)}) collective-permute-start(bf16[288,2304]{1,0:T(8,128)(2,1)} %get-tuple-element.137), channel_id=1, source_target_pairs={{0,1},{1,0},{2,3},{3,2},{4,5},{5,4},{6,7},{7,6},{8,9},{9,8},{10,11... | collective-permute-start | bytes 3981320 | tf_op jit(solution)/shard_map/ppermute | solution.py:495
  166.3 49.0 %all-to-all-start.3 = ((bf16[8,72,1152]{2,1,0:T(8,128)(2,1)}), bf16[8,72,1152]{2,1,0:T(8,128)(2,1)}, u32[]{:S(2)}, u32[]{:S(2)}) async-start(bf16[8,72,1152]{2,1,0:T(8,128)(2,1)} %get-tuple-element.103), calls=%async_computation.3 | async-start | bytes 2654208 | tf_op jit(solution)/shard_map/all_to_all | solution.py:608
  171.4 12.1 %copy-start = (s32[2]{0:T(128)S(1)}, s32[2]{0:T(128)}, u32[]{:S(2)}) copy-start(s32[2]{0:T(128)} %pad_add_fusion.refs_0_.refs_10_) | copy-start | bytes 28
  171.4 12.1 %copy-start.4 = (bf16[2,288,1152]{2,1,0:T(8,128)(2,1)S(1)}, bf16[2,288,1152]{2,1,0:T(8,128)(2,1)}, u32[]{:S(2)}) copy-start(bf16[2,288,1152]{2,1,0:T(8,128)(2,1)} %get-tuple-element.127.refs_1_) | copy-start | bytes 3981316
  187.8 21.2 %collective-permute-start.8 = (bf16[1,288,1152]{2,1,0:T(8,128)(2,1)S(1)}, bf16[1,288,1152]{2,1,0:T(8,128)(2,1)S(1)}, u32[]{:S(2)}, u32[]{:S(2)}) collective-permute-start(bf16[1,288,1152]{2,1,0:T(8,128)(2,1)S(1)} %get-tuple-element.134), channel_id=1, source_target_pairs={{0,16},{8,24},{16,0},{24,8},{1,17},{9,25},{17,1},{25,9},{2,18},{10... | collective-permute-start | bytes 1990664 | tf_op jit(solution)/shard_map/ppermute | solution.py:495
  189.3 19.7 %collective-permute-start.9 = (bf16[1,288,1152]{2,1,0:T(8,128)(2,1)S(1)}, bf16[1,288,1152]{2,1,0:T(8,128)(2,1)S(1)}, u32[]{:S(2)}, u32[]{:S(2)}) collective-permute-start(bf16[1,288,1152]{2,1,0:T(8,128)(2,1)S(1)} %get-tuple-element.135), channel_id=1, source_target_pairs={{0,8},{8,0},{16,24},{24,16},{1,9},{9,1},{17,25},{25,17},{2,10},{10... | collective-permute-start | bytes 1990664 | tf_op jit(solution)/shard_map/ppermute | solution.py:495
  189.8 19.2 %copy-start.1 = (s32[2]{0:T(128)S(1)}, s32[2]{0:T(128)}, u32[]{:S(2)}) copy-start(s32[2]{0:T(128)} %pad_add_fusion.refs_0_.refs_10_) | copy-start | bytes 28
  189.8 19.2 %copy-start.7 = (bf16[1,288,1152]{2,1,0:T(8,128)(2,1)S(1)}, bf16[1,288,1152]{2,1,0:T(8,128)(2,1)}, u32[]{:S(2)}) copy-start(bf16[1,288,1152]{2,1,0:T(8,128)(2,1)} %copy-done.6) | copy-start | bytes 1990660
  204.9 32.3 %collective-permute-start.12 = (bf16[2,288,960]{2,1,0:T(8,128)(2,1)}, bf16[2,288,960]{2,1,0:T(8,128)(2,1)S(1)}, u32[]{:S(2)}, u32[]{:S(2)}) collective-permute-start(bf16[2,288,960]{2,1,0:T(8,128)(2,1)} %get-tuple-element.145), channel_id=1, source_target_pairs={{0,8},{8,0},{16,24},{24,16},{1,9},{9,1},{17,25},{25,17},{2,10},{10... | collective-permute-start | bytes 3317768 | tf_op jit(solution)/shard_map/ppermute | solution.py:495
  206.5 30.7 %collective-permute-start.13 = (bf16[1,576,960]{2,1,0:T(8,128)(2,1)}, bf16[1,576,960]{2,1,0:T(8,128)(2,1)S(1)}, u32[]{:S(2)}, u32[]{:S(2)}) collective-permute-start(bf16[1,576,960]{2,1,0:T(8,128)(2,1)} %get-tuple-element.146), channel_id=1, source_target_pairs={{0,16},{8,24},{16,0},{24,8},{1,17},{9,25},{17,1},{25,9},{2,18},{10... | collective-permute-start | bytes 3317768 | tf_op jit(solution)/shard_map/ppermute | solution.py:495
  207.0 30.2 %collective-permute-start.14 = (bf16[8,72,384]{2,1,0:T(8,128)(2,1)}, bf16[8,72,384]{2,1,0:T(8,128)(2,1)S(1)}, u32[]{:S(2)}, u32[]{:S(2)}) collective-permute-start(bf16[8,72,384]{2,1,0:T(8,128)(2,1)} %get-tuple-element.147), channel_id=1, source_target_pairs={{0,2},{1,3},{2,0},{3,1},{4,6},{5,7},{6,4},{7,5},{8,10},{9,11},{10,... | collective-permute-start | bytes 1327112 | tf_op jit(solution)/shard_map/ppermute | solution.py:495
  213.3 14.2 %collective-permute-start.15 = (bf16[2,72,1152]{2,1,0:T(8,128)(2,1)}, bf16[2,72,1152]{2,1,0:T(8,128)(2,1)S(1)}, u32[]{:S(2)}, u32[]{:S(2)}) collective-permute-start(bf16[2,72,1152]{2,1,0:T(8,128)(2,1)} %get-tuple-element.150), channel_id=1, source_target_pairs={{0,2},{1,3},{2,0},{3,1},{4,6},{5,7},{6,4},{7,5},{8,10},{9,11},{10,... | collective-permute-start | bytes 995336 | tf_op jit(solution)/shard_map/ppermute | solution.py:495
  213.3 18.9 %collective-permute-start.16 = (bf16[2,72,1152]{2,1,0:T(8,128)(2,1)S(1)}, bf16[2,72,1152]{2,1,0:T(8,128)(2,1)}, u32[]{:S(2)}, u32[]{:S(2)}) collective-permute-start(bf16[2,72,1152]{2,1,0:T(8,128)(2,1)S(1)} %get-tuple-element.151), channel_id=1, source_target_pairs={{0,2},{1,3},{2,0},{3,1},{4,6},{5,7},{6,4},{7,5},{8,10},{9,11},{10,... | collective-permute-start | bytes 995336 | tf_op jit(solution)/shard_map/ppermute | solution.py:495
  215.3 17.0 %copy-start.10 = (bf16[2,72,1152]{2,1,0:T(8,128)(2,1)S(1)}, bf16[2,72,1152]{2,1,0:T(8,128)(2,1)}, u32[]{:S(2)}) copy-start(bf16[2,72,1152]{2,1,0:T(8,128)(2,1)} %copy-done.9) | copy-start | bytes 995332
  215.3 17.0 %copy-start.12 = (bf16[2,72,1152]{2,1,0:T(8,128)(2,1)S(1)}, bf16[2,72,1152]{2,1,0:T(8,128)(2,1)}, u32[]{:S(2)}) copy-start(bf16[2,72,1152]{2,1,0:T(8,128)(2,1)} %copy-done.11) | copy-start | bytes 995332
  232.9 4.3 %copy-start.2 = (bf16[2,288,960]{2,1,0:T(8,128)(2,1)S(1)}, bf16[2,288,960]{2,1,0:T(8,128)(2,1)}, u32[]{:S(2)}) copy-start(bf16[2,288,960]{2,1,0:T(8,128)(2,1)} %get-tuple-element.142.refs_1_) | copy-start | bytes 3317764
  232.9 4.3 %copy-start.3 = (bf16[1,576,960]{2,1,0:T(8,128)(2,1)S(1)}, bf16[1,576,960]{2,1,0:T(8,128)(2,1)}, u32[]{:S(2)}) copy-start(bf16[1,576,960]{2,1,0:T(8,128)(2,1)} %get-tuple-element.143.refs_2_) | copy-start | bytes 3317764
  232.9 4.3 %copy-start.8 = (bf16[8,72,384]{2,1,0:T(8,128)(2,1)S(1)}, bf16[8,72,384]{2,1,0:T(8,128)(2,1)}, u32[]{:S(2)}) copy-start(bf16[8,72,384]{2,1,0:T(8,128)(2,1)} %get-tuple-element.144.refs_3_) | copy-start | bytes 1327108
  234.5 8.9 %collective-permute-start.20 = (bf16[36,2304]{1,0:T(8,128)(2,1)S(1)}, bf16[36,2304]{1,0:T(8,128)(2,1)S(1)}, u32[]{:S(2)}, u32[]{:S(2)}) collective-permute-start(bf16[36,2304]{1,0:T(8,128)(2,1)S(1)} %get-tuple-element.164), channel_id=1, source_target_pairs={{0,4},{1,5},{2,6},{3,7},{4,0},{5,1},{6,2},{7,3},{8,12},{9,13},{10,... | collective-permute-start | bytes 497672 | tf_op jit(solution)/shard_map/ppermute | solution.py:495
  239.4 4.8 %copy-start.13 = (f32[8,128]{1,0:T(8,128)}, f32[8,128]{1,0:T(8,128)S(1)}, u32[]{:S(2)}) copy-start(f32[8,128]{1,0:T(8,128)S(1)} %get-tuple-element.154.refs_4_) | copy-start | bytes 12292
  239.4 19.6 %collective-permute-start.17 = (bf16[1,288,960]{2,1,0:T(8,128)(2,1)S(1)}, bf16[1,288,960]{2,1,0:T(8,128)(2,1)S(1)}, u32[]{:S(2)}, u32[]{:S(2)}) collective-permute-start(bf16[1,288,960]{2,1,0:T(8,128)(2,1)S(1)} %get-tuple-element.160), channel_id=1, source_target_pairs={{0,16},{8,24},{16,0},{24,8},{1,17},{9,25},{17,1},{25,9},{2,18},{10... | collective-permute-start | bytes 1658888 | tf_op jit(solution)/shard_map/ppermute | solution.py:495
  241.0 18.0 %collective-permute-start.18 = (bf16[4,72,960]{2,1,0:T(8,128)(2,1)S(1)}, bf16[4,72,960]{2,1,0:T(8,128)(2,1)S(1)}, u32[]{:S(2)}, u32[]{:S(2)}) collective-permute-start(bf16[4,72,960]{2,1,0:T(8,128)(2,1)S(1)} %get-tuple-element.161), channel_id=1, source_target_pairs={{0,2},{1,3},{2,0},{3,1},{4,6},{5,7},{6,4},{7,5},{8,10},{9,11},{10,... | collective-permute-start | bytes 1658888 | tf_op jit(solution)/shard_map/ppermute | solution.py:495
  242.4 6.5 %collective-permute-start.21 = (bf16[36,2304]{1,0:T(8,128)(2,1)S(1)}, bf16[36,2304]{1,0:T(8,128)(2,1)S(1)}, u32[]{:S(2)}, u32[]{:S(2)}) collective-permute-start(bf16[36,2304]{1,0:T(8,128)(2,1)S(1)} %get-tuple-element.165), channel_id=1, source_target_pairs={{0,1},{1,0},{2,3},{3,2},{4,5},{5,4},{6,7},{7,6},{8,9},{9,8},{10,11... | collective-permute-start | bytes 497672 | tf_op jit(solution)/shard_map/ppermute | solution.py:495
  242.4 14.5 %collective-permute-start.22 = (bf16[36,2304]{1,0:T(8,128)(2,1)S(1)}, bf16[36,2304]{1,0:T(8,128)(2,1)S(1)}, u32[]{:S(2)}, u32[]{:S(2)}) collective-permute-start(bf16[36,2304]{1,0:T(8,128)(2,1)S(1)} %get-tuple-element.166), channel_id=1, source_target_pairs={{0,5},{1,4},{2,7},{3,6},{4,1},{5,0},{6,3},{7,2},{8,13},{9,12},{10,... | collective-permute-start | bytes 497672 | tf_op jit(solution)/shard_map/ppermute | solution.py:495
  243.4 15.6 %collective-permute-start.19 = (bf16[2,144,384]{2,1,0:T(8,128)(2,1)S(1)}, bf16[2,144,384]{2,1,0:T(8,128)(2,1)S(1)}, u32[]{:S(2)}, u32[]{:S(2)}) collective-permute-start(bf16[2,144,384]{2,1,0:T(8,128)(2,1)S(1)} %get-tuple-element.162), channel_id=1, source_target_pairs={{0,8},{8,0},{16,24},{24,16},{1,9},{9,1},{17,25},{25,17},{2,10},{10... | collective-permute-start | bytes 663560 | tf_op jit(solution)/shard_map/ppermute | solution.py:495
  260.3 9.5 %collective-permute-start.23 = (bf16[2,72,960]{2,1,0:T(8,128)(2,1)S(1)}, bf16[2,72,960]{2,1,0:T(8,128)(2,1)S(1)}, u32[]{:S(2)}, u32[]{:S(2)}) collective-permute-start(bf16[2,72,960]{2,1,0:T(8,128)(2,1)S(1)} %get-tuple-element.172), channel_id=1, source_target_pairs={{0,2},{1,3},{2,0},{3,1},{4,6},{5,7},{6,4},{7,5},{8,10},{9,11},{10,... | collective-permute-start | bytes 829448 | tf_op jit(solution)/shard_map/ppermute | solution.py:495
  260.7 9.2 %collective-permute-start.24 = (bf16[1,144,960]{2,1,0:T(8,128)(2,1)S(1)}, bf16[1,144,960]{2,1,0:T(8,128)(2,1)S(1)}, u32[]{:S(2)}, u32[]{:S(2)}) collective-permute-start(bf16[1,144,960]{2,1,0:T(8,128)(2,1)S(1)} %get-tuple-element.173), channel_id=1, source_target_pairs={{0,8},{8,0},{16,24},{24,16},{1,9},{9,1},{17,25},{25,17},{2,10},{10... | collective-permute-start | bytes 829448 | tf_op jit(solution)/shard_map/ppermute | solution.py:495
  261.3 5.6 %collective-permute-start.25 = (bf16[1,144,384]{2,1,0:T(8,128)(2,1)S(1)}, bf16[1,144,384]{2,1,0:T(8,128)(2,1)S(1)}, u32[]{:S(2)}, u32[]{:S(2)}) collective-permute-start(bf16[1,144,384]{2,1,0:T(8,128)(2,1)S(1)} %get-tuple-element.174), channel_id=1, source_target_pairs={{0,16},{8,24},{16,0},{24,8},{1,17},{9,25},{17,1},{25,9},{2,18},{10... | collective-permute-start | bytes 331784 | tf_op jit(solution)/shard_map/ppermute | solution.py:495
  271.5 16.1 %collective-permute-start.26 = (bf16[36,2304]{1,0:T(8,128)(2,1)S(1)}, bf16[36,2304]{1,0:T(8,128)(2,1)S(1)}, u32[]{:S(2)}, u32[]{:S(2)}) collective-permute-start(bf16[36,2304]{1,0:T(8,128)(2,1)S(1)} %get-tuple-element.177), channel_id=1, source_target_pairs={{0,4},{1,5},{2,6},{3,7},{4,0},{5,1},{6,2},{7,3},{8,12},{9,13},{10,... | collective-permute-start | bytes 497672 | tf_op jit(solution)/shard_map/ppermute | solution.py:495
  274.2 13.4 %collective-permute-start.27 = (bf16[36,2304]{1,0:T(8,128)(2,1)S(1)}, bf16[36,2304]{1,0:T(8,128)(2,1)S(1)}, u32[]{:S(2)}, u32[]{:S(2)}) collective-permute-start(bf16[36,2304]{1,0:T(8,128)(2,1)S(1)} %get-tuple-element.178), channel_id=1, source_target_pairs={{0,1},{1,0},{2,3},{3,2},{4,5},{5,4},{6,7},{7,6},{8,9},{9,8},{10,11... | collective-permute-start | bytes 497672 | tf_op jit(solution)/shard_map/ppermute | solution.py:495
  274.2 16.8 %collective-permute-start.28 = (bf16[36,2304]{1,0:T(8,128)(2,1)S(1)}, bf16[36,2304]{1,0:T(8,128)(2,1)S(1)}, u32[]{:S(2)}, u32[]{:S(2)}) collective-permute-start(bf16[36,2304]{1,0:T(8,128)(2,1)S(1)} %get-tuple-element.179), channel_id=1, source_target_pairs={{0,5},{1,4},{2,7},{3,6},{4,1},{5,0},{6,3},{7,2},{8,13},{9,12},{10,... | collective-permute-start | bytes 497672 | tf_op jit(solution)/shard_map/ppermute | solution.py:495
  (15 other events, 16.7 us)

commit v5 on v3

--- a/solution.py
+++ b/solution.py
@@ -28,7 +28,7 @@
 
 ROOM = {
     "split": 56, "space_forward": 56, "time": 56, "weights": 56, "space_backward": 56,
-    "grad_input": 56, "stage": 24, "last_stage": 16, "assemble": 16, "join": 56,
+    "grad_input": 56, "stage": 24, "last_stage": 16, "core_stage": 16, "assemble": 16, "join": 56,
 }
 SPACES = {"v": pltpu.VMEM, "s": pltpu.SMEM, "a": pl.ANY}
 
@@ -477,6 +477,40 @@
             outs[2 * place + 1][:, start:stop] = other.astype(BF16)
 
 
+def far_stage_kernel(bit, cuts, place_ref, *refs):
+    count = len(cuts)
+    (near_out, far_out), total = refs[-3:-1], refs[-1]
+    rows = near_out.shape[0]
+    mine = bit_of(place_ref, "seq", bit) == 0
+    for part, (start, stop) in enumerate(cuts):
+        add_got(total, refs[part], refs[count + part])
+        low, high = total[:rows, : stop - start], total[rows : 2 * rows, : stop - start]
+        near_out[:, start:stop] = jnp.where(mine, low, high).astype(BF16)
+        far_out[:, start:stop] = jnp.where(mine, high, low).astype(BF16)
+
+
+def core_stage_kernel(place_ref, near_ref, got_ref, *refs):
+    kept_out, sent_out = refs[-2:]
+    rows = kept_out.shape[0]
+    core = (place_ref[1] & 1) == 0
+    total = near_ref[...].astype(F32) + got_ref[...].astype(F32)
+    low, high = total[:rows], total[rows:]
+    kept_out[...] = jnp.where(core, low, high).astype(BF16)
+    sent_out[...] = jnp.where(core, high, low).astype(BF16)
+
+
+def assemble_two_kernel(place_ref, kept_ref, got_ref, *refs):
+    qkv_ref, out_ref = refs[-2:]
+    width = out_ref.shape[1]
+    core = (place_ref[1] & 1) == 0
+    kept, got = kept_ref[...].astype(F32), got_ref[...].astype(F32)
+    low = jnp.where(core, kept, got).astype(BF16)
+    high = jnp.where(core, got, kept).astype(BF16)
+    qkv_ref[:, : 2 * width] = low
+    qkv_ref[:, 2 * width :] = high[:, :width]
+    out_ref[...] = high[:, width:]
+
+
 def assemble_kernel(place_ref, *refs):
     near, far, near_other, far_other = [ref[...].astype(F32) for ref in refs[:4]]
     qkv_ref, out_ref = refs[-2:]
@@ -561,10 +595,32 @@
         )
         return token
 
+    def far_stage(self, deps=()):
+        while self.step < len(self.bits) - 1:
+            self.stage()
+        bit = self.orders[0][-1][1]
+        rows = self.width >> len(self.bits)
+        near, far, token = call(
+            "last_stage", 1, functools.partial(far_stage_kernel, bit, self.cuts),
+            "s" + "v" * (2 * self.parts), (shaped(rows, 2 * self.width),) * 2, "vv",
+            [pltpu.VMEM((2 * rows, self.columns), F32)],
+        )(self.place, *self.kept, *self.got, deps=deps)
+        self.sums = (near, swap(far, "seq", 1 << bit))
+        return token
+
+    def core_stage(self, deps=()):
+        rows = self.width >> (len(self.bits) + 1)
+        kept, sent, token = call(
+            "core_stage", 1, core_stage_kernel, "svv", (shaped(rows, 2 * self.width),) * 2, "vv"
+        )(self.place, *self.sums, deps=deps)
+        self.sums = (kept, swap(sent, "seq", 1))
+        return token
+
     def finish(self, deps=()):
         rows = self.sums[0].shape[0]
         return call(
-            "assemble", 1, assemble_kernel, "svvvv",
+            "assemble", 1, assemble_kernel if len(self.sums) == 4 else assemble_two_kernel,
+            "s" + "v" * len(self.sums),
             (shaped(rows, 3 * self.width), shaped(rows, self.width)), "vv",
         )(self.place, *self.sums, deps=deps)
 
@@ -732,12 +788,13 @@
             v, space_units[v], d_middles[v], deps=[token, out_back] if v else [token]
         )
         grad_input.append(one_grad)
-    token = time_sum.last_stage(deps=[token])
+    token = time_sum.far_stage(deps=[token])
     token = space_sum.stage(deps=[token])
     block_out, grad_input, token = call(
         "join", 4, join_kernel, "vv" + "v" * videos, (all_rows, all_rows), "vv"
     )(out_back, from_joint, *grad_input, deps=[token])
     token = space_sum.stage(deps=[token])
+    token = time_sum.core_stage(deps=[token])
     token = space_sum.last_stage(deps=[token])
     *grad_time, token = time_sum.finish(deps=[token])
     *grad_space, _ = space_sum.finish(deps=[token])

time: 294 us -> 293 us (level)
  the two profiles are of different devices: /device:TPU:0 before, /device:TPU:1 now
where the time goes in v5:
time: 293 us; the launch traced here: 287 us
  Pallas kernels  158 us (54%)
  waiting for transfers between devices  62.4 us (21%)
  starting transfers between devices  54.4 us (19%)
  local copies, waits for them, and re-layouts  9.62 us (3%)
    pallas_call x21, Pallas kernels, run(): pl.pallas_call(with_token, out_shape=(*out_shape, TOKEN), in_specs=[pl.Bl...  158 us
    ppermute x28, waiting for transfers between devices, swap(): return lax.ppermute(x, axis, [(i, i ^ mask) for i in range(size)])  40.6 us
    all_to_all x6, starting transfers between devices, exchange(): lax.all_to_all(pieces, 'seq', split_axis=0, concat_axis=0, tiled=True)  31 us
    ppermute x28, starting transfers between devices, swap(): return lax.ppermute(x, axis, [(i, i ^ mask) for i in range(size)])  23.4 us
    all_to_all x6, waiting for transfers between devices, exchange(): lax.all_to_all(pieces, 'seq', split_axis=0, concat_axis=0, tiled=True)  21.8 us
    unnamed x51, local copies, waits for them, and re-layouts  9.62 us
  transfers between devices with their start and end apart: 34, of which 12 were waited for; matrix products, arithmetic and copies ran while one was open for 0% of the time, Pallas kernels for 53%

profile of v5, /device:TPU:1, one launch (start us, length us, event | category | flops | bytes accessed | tf_op | source)
XLA Modules:
  0.0 287.1 jit_solution(4598758734325414179)
XLA Ops:
  0.6 2.8 split.1
  3.4 6.5 %all-to-all-start = ((bf16[8,40,1152]{2,1,0:T(8,128)(2,1)}), bf16[8,40,1152]{2,1,0:T(8,128)(2,1)S(1)}, u32[]{:S(2)}, u32[]{:S(2)}) async-start(bf16[8,40,1152]{2,1,0:T(8,128)(2,1)} %get-tuple-element.99), calls=%async_computation | async-start | bytes 1474560 | tf_op jit(solution)/shard_map/all_to_all | solution.py:664
  10.5 11.8 %space_forward.2 = (bf16[8,40,1152]{2,1,0:T(8,128)(2,1)}, bf16[288,3456]{1,0:T(8,128)(2,1)}, bf16[288,2304]{1,0:T(8,128)(2,1)}, bf16[16,144,288]{2,1,0:T(8,128)(2,1)}, f32[8,128]{1,0:T(8,128)}) custom-call(bf16[2,288,1152]{2,1,0:T(8,128)(2,1)} %bitcast.9, bf16[2,288,1152]{2,1,0:T(8,128)(2,1)} %bitcast.7, f32[2,6,1152]{2,1,0:T(8,128)} %copy.25.refs_2_.refs_3_, ...), custom_call_target="tpu_custom_call" | custom-call | flops 14000000000 | bytes 14000000 | tf_op jit(solution)/shard_map/space_forward/pallas_call | solution.py:44
  23.1 5.9 %all-to-all-done.refs_8_.refs_2_.refs_12_ = bf16[8,40,1152]{2,1,0:T(8,128)(2,1)S(1)} async-done(((bf16[8,40,1152]{2,1,0:T(8,128)(2,1)}), bf16[8,40,1152]{2,1,0:T(8,128)(2,1)S(1)}, u32[]{:S(2)}, u32[]{:S(2)}) %all-to-all-start) | async-done | bytes 737312 | tf_op jit(solution)/shard_map/all_to_all | solution.py:664
  29.0 4.6 %all-to-all-start.2 = ((bf16[8,40,1152]{2,1,0:T(8,128)(2,1)}), bf16[8,40,1152]{2,1,0:T(8,128)(2,1)S(1)}, u32[]{:S(2)}, u32[]{:S(2)}) async-start(bf16[8,40,1152]{2,1,0:T(8,128)(2,1)} %get-tuple-element.101), calls=%async_computation.2 | async-start | bytes 1474560 | tf_op jit(solution)/shard_map/all_to_all | solution.py:664
  33.5 13.4 %space_forward.3 = (bf16[8,72,1152]{2,1,0:T(8,128)(2,1)}, bf16[288,3456]{1,0:T(8,128)(2,1)}, bf16[288,2304]{1,0:T(8,128)(2,1)}, bf16[16,144,288]{2,1,0:T(8,128)(2,1)}, f32[8,128]{1,0:T(8,128)}) custom-call(bf16[2,288,1152]{2,1,0:T(8,128)(2,1)} %bitcast.10, bf16[2,288,1152]{2,1,0:T(8,128)(2,1)} %bitcast.8, f32[2,6,1152]{2,1,0:T(8,128)} %copy.25.refs_2_.refs_3_, ...), custom_call_target="tpu_custom_call" | custom-call | flops 14000000000 | bytes 14000000 | tf_op jit(solution)/shard_map/space_forward/pallas_call | solution.py:44
  46.9 5.6 %all-to-all-done.2.refs_1_ = bf16[8,40,1152]{2,1,0:T(8,128)(2,1)S(1)} async-done(((bf16[8,40,1152]{2,1,0:T(8,128)(2,1)}), bf16[8,40,1152]{2,1,0:T(8,128)(2,1)S(1)}, u32[]{:S(2)}, u32[]{:S(2)}) %all-to-all-start.2) | async-done | bytes 737312 | tf_op jit(solution)/shard_map/all_to_all | solution.py:664
  53.5 4.6 %all-to-all-start.1 = ((bf16[8,72,1152]{2,1,0:T(8,128)(2,1)}), bf16[8,72,1152]{2,1,0:T(8,128)(2,1)S(1)}, u32[]{:S(2)}, u32[]{:S(2)}) async-start(bf16[8,72,1152]{2,1,0:T(8,128)(2,1)} %get-tuple-element.100), calls=%async_computation.1 | async-start | bytes 2654208 | tf_op jit(solution)/shard_map/all_to_all | solution.py:664
  58.1 20.8 %time.2 = (bf16[8,40,1152]{2,1,0:T(8,128)(2,1)}, bf16[8,72,1152]{2,1,0:T(8,128)(2,1)}, bf16[288,2304]{1,0:T(8,128)(2,1)}, bf16[288,2304]{1,0:T(8,128)(2,1)}, bf1...) custom-call(s32[2]{0:T(128)} %pad_add_fusion.refs_0_.refs_10_, bf16[8,40,1152]{2,1,0:T(8,128)(2,1)} %copy-done.22, ...), custom_call_target="tpu_custom_call" | custom-call | flops 24999999488 | bytes 25000000 | tf_op jit(solution)/shard_map/time/pallas_call | solution.py:44
  79.5 10.2 %all-to-all-done.1.refs_1_.refs_2_ = bf16[8,72,1152]{2,1,0:T(8,128)(2,1)S(1)} async-done(((bf16[8,72,1152]{2,1,0:T(8,128)(2,1)}), bf16[8,72,1152]{2,1,0:T(8,128)(2,1)S(1)}, u32[]{:S(2)}, u32[]{:S(2)}) %all-to-all-start.1) | async-done | bytes 1327136 | tf_op jit(solution)/shard_map/all_to_all | solution.py:664
  89.8 4.8 %all-to-all-start.4 = ((bf16[8,40,1152]{2,1,0:T(8,128)(2,1)}), bf16[8,40,1152]{2,1,0:T(8,128)(2,1)S(1)}, u32[]{:S(2)}, u32[]{:S(2)}) async-start(bf16[8,40,1152]{2,1,0:T(8,128)(2,1)} %get-tuple-element.106), calls=%async_computation.4 | async-start | bytes 1474560 | tf_op jit(solution)/shard_map/all_to_all | solution.py:664
  94.6 21.5 %time.3 = (bf16[8,40,1152]{2,1,0:T(8,128)(2,1)}, bf16[8,72,1152]{2,1,0:T(8,128)(2,1)}, bf16[288,2304]{1,0:T(8,128)(2,1)}, bf16[288,2304]{1,0:T(8,128)(2,1)}, bf1...) custom-call(s32[2]{0:T(128)} %pad_add_fusion.refs_0_.refs_10_, bf16[8,72,1152]{2,1,0:T(8,128)(2,1)} %copy-done.18, ...), custom_call_target="tpu_custom_call" | custom-call | flops 24999999488 | bytes 25000000 | tf_op jit(solution)/shard_map/time/pallas_call | solution.py:44
  116.7 5.3 %all-to-all-start.5 = ((bf16[8,40,1152]{2,1,0:T(8,128)(2,1)}), bf16[8,40,1152]{2,1,0:T(8,128)(2,1)S(1)}, u32[]{:S(2)}, u32[]{:S(2)}) async-start(bf16[8,40,1152]{2,1,0:T(8,128)(2,1)} %get-tuple-element.124), calls=%async_computation.5 | async-start | bytes 1474560 | tf_op jit(solution)/shard_map/all_to_all | solution.py:664
  122.0 11.4 %space_backward.2 = (bf16[288,1152]{1,0:T(8,128)(2,1)}, bf16[288,2304]{1,0:T(8,128)(2,1)}, bf16[288,4608]{1,0:T(8,128)(2,1)}, f32[8,128]{1,0:T(8,128)}) custom-call(s32[2]{0:T(128)} %pad_add_fusion.refs_0_.refs_10_, bf16[8,40,1152]{2,1,0:T(8,128)(2,1)} %copy-done.21, f32[2,6,1152]{2,1,0:T(8,128)} %copy.25.refs_2_.refs_3_, bf16[1152,1152]{1,0:T(8,128)(2,1)} %refs_3_.11, ...), custom_call_target="tpu_custom_call" | custom-call | flops 15000000512 | bytes 15000000 | tf_op jit(solution)/shard_map/space_backward/pallas_call | solution.py:44
  133.6 14.9 %weights.2 = (bf16[2,288,1152]{2,1,0:T(8,128)(2,1)}, bf16[2,288,1152]{2,1,0:T(8,128)(2,1)}, bf16[1,576,1152]{2,1,0:T(8,128)(2,1)}, bf16[1,576,1152]{2,1,0:T(8,128)(2,1)}, f32[8,128]{1,0:T(8,128)}) custom-call(s32[2]{0:T(128)} %pad_add_fusion.refs_0_.refs_10_, bf16[288,2304]{1,0:T(8,128)(2,1)} %get-tuple-element.113.refs_1_, ...), custom_call_target="tpu_custom_call" | custom-call | flops 10000000000 | bytes 10000000 | tf_op jit(solution)/shard_map/weights/pallas_call | solution.py:44
  148.5 1.3 collective-permute-start.5
  149.8 1.2 collective-permute-start.6
  151.9 11.5 %space_backward.3 = (bf16[288,1152]{1,0:T(8,128)(2,1)}, bf16[288,2304]{1,0:T(8,128)(2,1)}, bf16[288,4608]{1,0:T(8,128)(2,1)}, f32[8,128]{1,0:T(8,128)}) custom-call(s32[2]{0:T(128)} %pad_add_fusion.refs_0_.refs_10_, bf16[8,40,1152]{2,1,0:T(8,128)(2,1)} %copy-done.19, f32[2,6,1152]{2,1,0:T(8,128)} %copy.25.refs_2_.refs_3_, bf16[1152,1152]{1,0:T(8,128)(2,1)} %refs_3_.11, ...), custom_call_target="tpu_custom_call" | custom-call | flops 15000000512 | bytes 15000000 | tf_op jit(solution)/shard_map/space_backward/pallas_call | solution.py:44
  163.4 1.1 collective-permute-start.11
  164.5 5.2 %all-to-all-start.3 = ((bf16[8,72,1152]{2,1,0:T(8,128)(2,1)}), bf16[8,72,1152]{2,1,0:T(8,128)(2,1)}, u32[]{:S(2)}, u32[]{:S(2)}) async-start(bf16[8,72,1152]{2,1,0:T(8,128)(2,1)} %get-tuple-element.105), calls=%async_computation.3 | async-start | bytes 2654208 | tf_op jit(solution)/shard_map/all_to_all | solution.py:664
  169.7 9.4 %collective-permute-done.5.refs_3_ = bf16[2,288,1152]{2,1,0:T(8,128)(2,1)S(1)} collective-permute-done((bf16[2,288,1152]{2,1,0:T(8,128)(2,1)}, bf16[2,288,1152]{2,1,0:T(8,128)(2,1)S(1)}, u32[]{:S(2)}, u32[]{:S(2)}) %collective-permute-start.5) | collective-permute-done | bytes 1327136 | tf_op jit(solution)/shard_map/ppermute | solution.py:529
  180.0 1.3 copy-done.4
  181.3 1.3 copy-done.5
  182.7 1.4 stage.4
  184.1 1.3 collective-permute-start.8
  185.7 14.8 %weights.3 = (bf16[2,288,960]{2,1,0:T(8,128)(2,1)}, bf16[2,288,960]{2,1,0:T(8,128)(2,1)}, bf16[1,576,960]{2,1,0:T(8,128)(2,1)}, bf16[1,576,960]{2,1,0:T(8,128)(2...) custom-call(s32[2]{0:T(128)} %pad_add_fusion.refs_0_.refs_10_, ...), custom_call_target="tpu_custom_call" | custom-call | flops 10000000000 | bytes 10000000 | tf_op jit(solution)/shard_map/weights/pallas_call | solution.py:44
  200.5 1.2 collective-permute-start.12
  201.9 2.0 collective-permute-start.14
  204.7 1.5 stage.5
  208.2 1.5 collective-permute-start.16
  209.7 9.5 %grad_input.2 = (bf16[288,1152]{1,0:T(8,128)(2,1)}, f32[8,128]{1,0:T(8,128)}) custom-call(bf16[288,4608]{1,0:T(8,128)(2,1)} %get-tuple-element.111.refs_5_.refs_0_, bf16[288,1152]{1,0:T(8,128)(2,1)} %get-tuple-element.112.refs_1_, bf16[2,288,1152]{2,1,0:T(8,128)(2,1)} %bitcast.11, f32[2,6,1152]{2,1,0:T(8,128)} %copy.25.refs_2_.refs_3_, ...), custom_call_target="tpu_custom_call" | custom-call | flops 8000000000 | bytes 8000000 | tf_op jit(solution)/shard_map/grad_input/pallas_call | solution.py:44
  219.2 9.3 %grad_input.3 = (bf16[288,1152]{1,0:T(8,128)(2,1)}, f32[8,128]{1,0:T(8,128)}) custom-call(bf16[288,4608]{1,0:T(8,128)(2,1)} %get-tuple-element.134.refs_6_.refs_0_, bf16[288,1152]{1,0:T(8,128)(2,1)} %get-tuple-element.141.refs_1_, bf16[2,288,1152]{2,1,0:T(8,128)(2,1)} %bitcast.12, f32[2,6,1152]{2,1,0:T(8,128)} %copy.25.refs_2_.refs_3_, ...), custom_call_target="tpu_custom_call" | custom-call | flops 8000000000 | bytes 8000000 | tf_op jit(solution)/shard_map/grad_input/pallas_call | solution.py:44
  229.3 1.3 last_stage.2
  231.1 2.1 stage.6
  233.2 1.3 collective-permute-start.17
  234.5 2.3 collective-permute-start.23
  237.2 4.7 %join.1 = (bf16[2,288,1152]{2,1,0:T(8,128)(2,1)}, bf16[2,288,1152]{2,1,0:T(8,128)(2,1)}, f32[8,128]{1,0:T(8,128)}) custom-call(bf16[8,72,1152]{2,1,0:T(8,128)(2,1)} %all-to-all-done.3.refs_6_.refs_0_, bf16[576,576]{1,0:T(8,128)(2,1)} %constant.30.clone.refs_1_, bf16[288,1152]{1,0:T(8,128)(2,1)} %get-tuple-element.140.refs_2_, ...), custom_call_target="tpu_custom_call" | custom-call | flops 4000000000 | bytes 4000000 | tf_op jit(solution)/shard_map/join/pallas_call | solution.py:44
  241.9 3.0 %collective-permute-done.17.refs_4_ = bf16[1,288,960]{2,1,0:T(8,128)(2,1)S(1)} collective-permute-done((bf16[1,288,960]{2,1,0:T(8,128)(2,1)S(1)}, bf16[1,288,960]{2,1,0:T(8,128)(2,1)S(1)}, u32[]{:S(2)}, u32[]{:S(2)}) %collective-permute-start.17) | collective-permute-done | bytes 552992 | tf_op jit(solution)/shard_map/ppermute | solution.py:529
  245.0 10.9 %collective-permute-done.18.refs_5_ = bf16[4,72,960]{2,1,0:T(8,128)(2,1)S(1)} collective-permute-done((bf16[4,72,960]{2,1,0:T(8,128)(2,1)S(1)}, bf16[4,72,960]{2,1,0:T(8,128)(2,1)S(1)}, u32[]{:S(2)}, u32[]{:S(2)}) %collective-permute-start.18) | collective-permute-done | bytes 552992 | tf_op jit(solution)/shard_map/ppermute | solution.py:529
  256.5 1.3 stage.7
  259.3 2.1 collective-permute-start.27
  261.9 3.0 %collective-permute-done.20.refs_4_ = bf16[2,72,960]{2,1,0:T(8,128)(2,1)S(1)} collective-permute-done((bf16[2,72,960]{2,1,0:T(8,128)(2,1)S(1)}, bf16[2,72,960]{2,1,0:T(8,128)(2,1)S(1)}, u32[]{:S(2)}, u32[]{:S(2)}) %collective-permute-start.20) | collective-permute-done | bytes 276512 | tf_op jit(solution)/shard_map/ppermute | solution.py:529
  265.0 1.1 last_stage.3
  266.2 4.0 %collective-permute-start.25 = (bf16[36,2304]{1,0:T(8,128)(2,1)S(1)}, bf16[36,2304]{1,0:T(8,128)(2,1)S(1)}, u32[]{:S(2)}, u32[]{:S(2)}) collective-permute-start(bf16[36,2304]{1,0:T(8,128)(2,1)S(1)} %get-tuple-element.178), channel_id=1, source_target_pairs={{0,1},{1,0},{2,3},{3,2},{4,5},{5,4},{6,7},{7,6},{8,9},{9,8},{10,11... | collective-permute-start | bytes 497672 | tf_op jit(solution)/shard_map/ppermute | solution.py:529
  271.1 1.3 assemble.2
  272.4 8.2 %collective-permute-done.24.refs_2_ = bf16[36,2304]{1,0:T(8,128)(2,1)S(1)} collective-permute-done((bf16[36,2304]{1,0:T(8,128)(2,1)S(1)}, bf16[36,2304]{1,0:T(8,128)(2,1)S(1)}, u32[]{:S(2)}, u32[]{:S(2)}) %collective-permute-start.24) | collective-permute-done | bytes 165920 | tf_op jit(solution)/shard_map/ppermute | solution.py:529
  280.6 4.6 %collective-permute-done.26.refs_4_ = bf16[36,2304]{1,0:T(8,128)(2,1)S(1)} collective-permute-done((bf16[36,2304]{1,0:T(8,128)(2,1)S(1)}, bf16[36,2304]{1,0:T(8,128)(2,1)S(1)}, u32[]{:S(2)}, u32[]{:S(2)}) %collective-permute-start.26) | collective-permute-done | bytes 165920 | tf_op jit(solution)/shard_map/ppermute | solution.py:529
  285.3 1.4 assemble.3
  (93 shorter events, 13.9 us)
Async XLA Ops:
  3.4 6.5 %copy-start.23 = (f32[2,6,1152]{2,0,1:T(2,128)S(1)}, f32[2,6,1152]{2,0,1:T(2,128)}, u32[]{:S(2)}) copy-start(f32[2,6,1152]{2,0,1:T(2,128)} %param.19) | copy-start | bytes 165892
  3.4 25.6 %all-to-all-start = ((bf16[8,40,1152]{2,1,0:T(8,128)(2,1)}), bf16[8,40,1152]{2,1,0:T(8,128)(2,1)S(1)}, u32[]{:S(2)}, u32[]{:S(2)}) async-start(bf16[8,40,1152]{2,1,0:T(8,128)(2,1)} %get-tuple-element.99), calls=%async_computation | async-start | bytes 1474560 | tf_op jit(solution)/shard_map/all_to_all | solution.py:664
  22.3 93.9 %collective-permute-start = (bf16[288,2304]{1,0:T(8,128)(2,1)}, bf16[288,2304]{1,0:T(8,128)(2,1)S(1)}, u32[]{:S(2)}, u32[]{:S(2)}) collective-permute-start(bf16[288,2304]{1,0:T(8,128)(2,1)} %get-tuple-element.110.refs_1_), channel_id=1, source_target_pairs={{0,1},{1,0},{2,3},{3,2},{4,5},{5,4},{6,7},{7,6},{8,9},{9,8},{10,11... | collective-permute-start | bytes 3981320 | tf_op jit(solution)/shard_map/ppermute | solution.py:529
  29.0 4.6 %copy-start.20 = (bf16[8,40,1152]{2,1,0:T(8,128)(2,1)}, bf16[8,40,1152]{2,1,0:T(8,128)(2,1)S(1)}, u32[]{:S(2)}) copy-start(bf16[8,40,1152]{2,1,0:T(8,128)(2,1)S(1)} %all-to-all-done.refs_8_.refs_2_.refs_12_) | copy-start | bytes 2211844
  29.0 23.6 %all-to-all-start.2 = ((bf16[8,40,1152]{2,1,0:T(8,128)(2,1)}), bf16[8,40,1152]{2,1,0:T(8,128)(2,1)S(1)}, u32[]{:S(2)}, u32[]{:S(2)}) async-start(bf16[8,40,1152]{2,1,0:T(8,128)(2,1)} %get-tuple-element.101), calls=%async_computation.2 | async-start | bytes 1474560 | tf_op jit(solution)/shard_map/all_to_all | solution.py:664
  53.5 36.3 %all-to-all-start.1 = ((bf16[8,72,1152]{2,1,0:T(8,128)(2,1)}), bf16[8,72,1152]{2,1,0:T(8,128)(2,1)S(1)}, u32[]{:S(2)}, u32[]{:S(2)}) async-start(bf16[8,72,1152]{2,1,0:T(8,128)(2,1)} %get-tuple-element.100), calls=%async_computation.1 | async-start | bytes 2654208 | tf_op jit(solution)/shard_map/all_to_all | solution.py:664
  78.9 54.6 %collective-permute-start.1 = (bf16[288,2304]{1,0:T(8,128)(2,1)}, bf16[288,2304]{1,0:T(8,128)(2,1)}, u32[]{:S(2)}, u32[]{:S(2)}) collective-permute-start(bf16[288,2304]{1,0:T(8,128)(2,1)} %get-tuple-element.113.refs_1_), channel_id=1, source_target_pairs={{0,1},{1,0},{2,3},{3,2},{4,5},{5,4},{6,7},{7,6},{8,9},{9,8},{10,11... | collective-permute-start | bytes 3981320 | tf_op jit(solution)/shard_map/ppermute | solution.py:529
  79.0 54.6 %collective-permute-start.3 = (bf16[288,2304]{1,0:T(8,128)(2,1)}, bf16[288,2304]{1,0:T(8,128)(2,1)}, u32[]{:S(2)}, u32[]{:S(2)}) collective-permute-start(bf16[288,2304]{1,0:T(8,128)(2,1)} %get-tuple-element.117), channel_id=1, source_target_pairs={{0,1},{1,0},{2,3},{3,2},{4,5},{5,4},{6,7},{7,6},{8,9},{9,8},{10,11... | collective-permute-start | bytes 3981320 | tf_op jit(solution)/shard_map/ppermute | solution.py:529
  79.4 71.6 %collective-permute-start.7 = (bf16[288,2304]{1,0:T(8,128)(2,1)}, bf16[288,2304]{1,0:T(8,128)(2,1)}, u32[]{:S(2)}, u32[]{:S(2)}) collective-permute-start(bf16[288,2304]{1,0:T(8,128)(2,1)} %get-tuple-element.128.refs_2_), channel_id=1, source_target_pairs={{0,1},{1,0},{2,3},{3,2},{4,5},{5,4},{6,7},{7,6},{8,9},{9,8},{10,11... | collective-permute-start | bytes 3981320 | tf_op jit(solution)/shard_map/ppermute | solution.py:529
  89.8 4.8 %copy-start.18 = (bf16[8,72,1152]{2,1,0:T(8,128)(2,1)}, bf16[8,72,1152]{2,1,0:T(8,128)(2,1)S(1)}, u32[]{:S(2)}) copy-start(bf16[8,72,1152]{2,1,0:T(8,128)(2,1)S(1)} %all-to-all-done.1.refs_1_.refs_2_) | copy-start | bytes 3981316
  89.8 26.9 %all-to-all-start.4 = ((bf16[8,40,1152]{2,1,0:T(8,128)(2,1)}), bf16[8,40,1152]{2,1,0:T(8,128)(2,1)S(1)}, u32[]{:S(2)}, u32[]{:S(2)}) async-start(bf16[8,40,1152]{2,1,0:T(8,128)(2,1)} %get-tuple-element.106), calls=%async_computation.4 | async-start | bytes 1474560 | tf_op jit(solution)/shard_map/all_to_all | solution.py:664
  116.1 17.5 %collective-permute-start.2 = (bf16[288,2304]{1,0:T(8,128)(2,1)}, bf16[288,2304]{1,0:T(8,128)(2,1)}, u32[]{:S(2)}, u32[]{:S(2)}) collective-permute-start(bf16[288,2304]{1,0:T(8,128)(2,1)} %get-tuple-element.114.refs_2_), channel_id=1, source_target_pairs={{0,1},{1,0},{2,3},{3,2},{4,5},{5,4},{6,7},{7,6},{8,9},{9,8},{10,11... | collective-permute-start | bytes 3981320 | tf_op jit(solution)/shard_map/ppermute | solution.py:529
  116.2 5.8 %copy-start.24 = (bf16[288,2304]{1,0:T(8,128)(2,1)}, bf16[288,2304]{1,0:T(8,128)(2,1)S(1)}, u32[]{:S(2)}) copy-start(bf16[288,2304]{1,0:T(8,128)(2,1)S(1)} %collective-permute-done.refs_8_.refs_3_) | copy-start | bytes 3981316
  116.2 17.3 %collective-permute-start.4 = (bf16[288,2304]{1,0:T(8,128)(2,1)}, bf16[288,2304]{1,0:T(8,128)(2,1)}, u32[]{:S(2)}, u32[]{:S(2)}) collective-permute-start(bf16[288,2304]{1,0:T(8,128)(2,1)} %get-tuple-element.118), channel_id=1, source_target_pairs={{0,1},{1,0},{2,3},{3,2},{4,5},{5,4},{6,7},{7,6},{8,9},{9,8},{10,11... | collective-permute-start | bytes 3981320 | tf_op jit(solution)/shard_map/ppermute | solution.py:529
  116.7 5.4 %copy-start.21 = (bf16[8,40,1152]{2,1,0:T(8,128)(2,1)}, bf16[8,40,1152]{2,1,0:T(8,128)(2,1)S(1)}, u32[]{:S(2)}) copy-start(bf16[8,40,1152]{2,1,0:T(8,128)(2,1)S(1)} %all-to-all-done.4.refs_1_) | copy-start | bytes 2211844
  116.7 34.3 %all-to-all-start.5 = ((bf16[8,40,1152]{2,1,0:T(8,128)(2,1)}), bf16[8,40,1152]{2,1,0:T(8,128)(2,1)S(1)}, u32[]{:S(2)}, u32[]{:S(2)}) async-start(bf16[8,40,1152]{2,1,0:T(8,128)(2,1)} %get-tuple-element.124), calls=%async_computation.5 | async-start | bytes 1474560 | tf_op jit(solution)/shard_map/all_to_all | solution.py:664
  133.5 52.2 %collective-permute-start.10 = (bf16[288,2304]{1,0:T(8,128)(2,1)}, bf16[288,2304]{1,0:T(8,128)(2,1)}, u32[]{:S(2)}, u32[]{:S(2)}) collective-permute-start(bf16[288,2304]{1,0:T(8,128)(2,1)} %get-tuple-element.135), channel_id=1, source_target_pairs={{0,1},{1,0},{2,3},{3,2},{4,5},{5,4},{6,7},{7,6},{8,9},{9,8},{10,11... | collective-permute-start | bytes 3981320 | tf_op jit(solution)/shard_map/ppermute | solution.py:529
  148.5 30.6 %collective-permute-start.5 = (bf16[2,288,1152]{2,1,0:T(8,128)(2,1)}, bf16[2,288,1152]{2,1,0:T(8,128)(2,1)S(1)}, u32[]{:S(2)}, u32[]{:S(2)}) collective-permute-start(bf16[2,288,1152]{2,1,0:T(8,128)(2,1)} %get-tuple-element.122), channel_id=1, source_target_pairs={{0,8},{8,0},{16,24},{24,16},{1,9},{9,1},{17,25},{25,17},{2,10},{10... | collective-permute-start | bytes 3981320 | tf_op jit(solution)/shard_map/ppermute | solution.py:529
  149.8 30.2 %collective-permute-start.6 = (bf16[1,576,1152]{2,1,0:T(8,128)(2,1)}, bf16[1,576,1152]{2,1,0:T(8,128)(2,1)S(1)}, u32[]{:S(2)}, u32[]{:S(2)}) collective-permute-start(bf16[1,576,1152]{2,1,0:T(8,128)(2,1)} %get-tuple-element.123), channel_id=1, source_target_pairs={{0,16},{8,24},{16,0},{24,8},{1,17},{9,25},{17,1},{25,9},{2,18},{10... | collective-permute-start | bytes 3981320 | tf_op jit(solution)/shard_map/ppermute | solution.py:529
  163.4 22.3 %collective-permute-start.11 = (bf16[288,2304]{1,0:T(8,128)(2,1)}, bf16[288,2304]{1,0:T(8,128)(2,1)}, u32[]{:S(2)}, u32[]{:S(2)}) collective-permute-start(bf16[288,2304]{1,0:T(8,128)(2,1)} %get-tuple-element.136), channel_id=1, source_target_pairs={{0,1},{1,0},{2,3},{3,2},{4,5},{5,4},{6,7},{7,6},{8,9},{9,8},{10,11... | collective-permute-start | bytes 3981320 | tf_op jit(solution)/shard_map/ppermute | solution.py:529
  164.5 15.5 %copy-start = (s32[2]{0:T(128)S(1)}, s32[2]{0:T(128)}, u32[]{:S(2)}) copy-start(s32[2]{0:T(128)} %pad_add_fusion.refs_0_.refs_10_) | copy-start | bytes 28
  164.5 15.5 %copy-start.13 = (f32[8,128]{1,0:T(8,128)S(1)}, f32[8,128]{1,0:T(8,128)}, u32[]{:S(2)}) copy-start(f32[8,128]{1,0:T(8,128)} %get-tuple-element.129.refs_5_) | copy-start | bytes 12292
  164.5 54.6 %all-to-all-start.3 = ((bf16[8,72,1152]{2,1,0:T(8,128)(2,1)}), bf16[8,72,1152]{2,1,0:T(8,128)(2,1)}, u32[]{:S(2)}, u32[]{:S(2)}) async-start(bf16[8,72,1152]{2,1,0:T(8,128)(2,1)} %get-tuple-element.105), calls=%async_computation.3 | async-start | bytes 2654208 | tf_op jit(solution)/shard_map/all_to_all | solution.py:664
  184.1 1.7 copy-start.12
  184.1 19.9 %collective-permute-start.8 = (bf16[1,288,1152]{2,1,0:T(8,128)(2,1)S(1)}, bf16[1,288,1152]{2,1,0:T(8,128)(2,1)S(1)}, u32[]{:S(2)}, u32[]{:S(2)}) collective-permute-start(bf16[1,288,1152]{2,1,0:T(8,128)(2,1)S(1)} %get-tuple-element.132), channel_id=1, source_target_pairs={{0,16},{8,24},{16,0},{24,8},{1,17},{9,25},{17,1},{25,9},{2,18},{10... | collective-permute-start | bytes 1990664 | tf_op jit(solution)/shard_map/ppermute | solution.py:529
  185.4 18.6 %collective-permute-start.9 = (bf16[1,288,1152]{2,1,0:T(8,128)(2,1)S(1)}, bf16[1,288,1152]{2,1,0:T(8,128)(2,1)S(1)}, u32[]{:S(2)}, u32[]{:S(2)}) collective-permute-start(bf16[1,288,1152]{2,1,0:T(8,128)(2,1)S(1)} %get-tuple-element.133), channel_id=1, source_target_pairs={{0,8},{8,0},{16,24},{24,16},{1,9},{9,1},{17,25},{25,17},{2,10},{10... | collective-permute-start | bytes 1990664 | tf_op jit(solution)/shard_map/ppermute | solution.py:529
  185.7 18.3 %copy-start.1 = (s32[2]{0:T(128)S(1)}, s32[2]{0:T(128)}, u32[]{:S(2)}) copy-start(s32[2]{0:T(128)} %pad_add_fusion.refs_0_.refs_10_) | copy-start | bytes 28
  200.5 30.1 %collective-permute-start.12 = (bf16[2,288,960]{2,1,0:T(8,128)(2,1)}, bf16[2,288,960]{2,1,0:T(8,128)(2,1)S(1)}, u32[]{:S(2)}, u32[]{:S(2)}) collective-permute-start(bf16[2,288,960]{2,1,0:T(8,128)(2,1)} %get-tuple-element.147), channel_id=1, source_target_pairs={{0,8},{8,0},{16,24},{24,16},{1,9},{9,1},{17,25},{25,17},{2,10},{10... | collective-permute-start | bytes 3317768 | tf_op jit(solution)/shard_map/ppermute | solution.py:529
  201.7 28.9 %collective-permute-start.13 = (bf16[1,576,960]{2,1,0:T(8,128)(2,1)}, bf16[1,576,960]{2,1,0:T(8,128)(2,1)S(1)}, u32[]{:S(2)}, u32[]{:S(2)}) collective-permute-start(bf16[1,576,960]{2,1,0:T(8,128)(2,1)} %get-tuple-element.148), channel_id=1, source_target_pairs={{0,16},{8,24},{16,0},{24,8},{1,17},{9,25},{17,1},{25,9},{2,18},{10... | collective-permute-start | bytes 3317768 | tf_op jit(solution)/shard_map/ppermute | solution.py:529
  201.9 28.7 %collective-permute-start.14 = (bf16[8,72,384]{2,1,0:T(8,128)(2,1)}, bf16[8,72,384]{2,1,0:T(8,128)(2,1)S(1)}, u32[]{:S(2)}, u32[]{:S(2)}) collective-permute-start(bf16[8,72,384]{2,1,0:T(8,128)(2,1)} %get-tuple-element.149), channel_id=1, source_target_pairs={{0,2},{1,3},{2,0},{3,1},{4,6},{5,7},{6,4},{7,5},{8,10},{9,11},{10,... | collective-permute-start | bytes 1327112 | tf_op jit(solution)/shard_map/ppermute | solution.py:529
  208.2 20.3 %collective-permute-start.15 = (bf16[2,72,1152]{2,1,0:T(8,128)(2,1)}, bf16[2,72,1152]{2,1,0:T(8,128)(2,1)S(1)}, u32[]{:S(2)}, u32[]{:S(2)}) collective-permute-start(bf16[2,72,1152]{2,1,0:T(8,128)(2,1)} %get-tuple-element.152), channel_id=1, source_target_pairs={{0,2},{1,3},{2,0},{3,1},{4,6},{5,7},{6,4},{7,5},{8,10},{9,11},{10,... | collective-permute-start | bytes 995336 | tf_op jit(solution)/shard_map/ppermute | solution.py:529
  208.2 20.3 %collective-permute-start.16 = (bf16[2,72,1152]{2,1,0:T(8,128)(2,1)S(1)}, bf16[2,72,1152]{2,1,0:T(8,128)(2,1)}, u32[]{:S(2)}, u32[]{:S(2)}) collective-permute-start(bf16[2,72,1152]{2,1,0:T(8,128)(2,1)S(1)} %get-tuple-element.153), channel_id=1, source_target_pairs={{0,2},{1,3},{2,0},{3,1},{4,6},{5,7},{6,4},{7,5},{8,10},{9,11},{10,... | collective-permute-start | bytes 995336 | tf_op jit(solution)/shard_map/ppermute | solution.py:529
  219.2 9.4 %copy-start.8 = (bf16[2,72,1152]{2,1,0:T(8,128)(2,1)S(1)}, bf16[2,72,1152]{2,1,0:T(8,128)(2,1)}, u32[]{:S(2)}) copy-start(bf16[2,72,1152]{2,1,0:T(8,128)(2,1)} %copy-done.7) | copy-start | bytes 995332
  219.2 9.4 %copy-start.10 = (bf16[2,72,1152]{2,1,0:T(8,128)(2,1)S(1)}, bf16[2,72,1152]{2,1,0:T(8,128)(2,1)}, u32[]{:S(2)}) copy-start(bf16[2,72,1152]{2,1,0:T(8,128)(2,1)} %copy-done.9) | copy-start | bytes 995332
  229.2 1.7 copy-start.3
  229.2 1.8 copy-start.6
  233.2 4.0 %copy-start.11 = (f32[8,128]{1,0:T(8,128)}, f32[8,128]{1,0:T(8,128)S(1)}, u32[]{:S(2)}) copy-start(f32[8,128]{1,0:T(8,128)S(1)} %get-tuple-element.156.refs_4_) | copy-start | bytes 12292
  233.2 11.8 %collective-permute-start.17 = (bf16[1,288,960]{2,1,0:T(8,128)(2,1)S(1)}, bf16[1,288,960]{2,1,0:T(8,128)(2,1)S(1)}, u32[]{:S(2)}, u32[]{:S(2)}) collective-permute-start(bf16[1,288,960]{2,1,0:T(8,128)(2,1)S(1)} %get-tuple-element.162), channel_id=1, source_target_pairs={{0,16},{8,24},{16,0},{24,8},{1,17},{9,25},{17,1},{25,9},{2,18},{10... | collective-permute-start | bytes 1658888 | tf_op jit(solution)/shard_map/ppermute | solution.py:529
  234.5 21.4 %collective-permute-start.18 = (bf16[4,72,960]{2,1,0:T(8,128)(2,1)S(1)}, bf16[4,72,960]{2,1,0:T(8,128)(2,1)S(1)}, u32[]{:S(2)}, u32[]{:S(2)}) collective-permute-start(bf16[4,72,960]{2,1,0:T(8,128)(2,1)S(1)} %get-tuple-element.163), channel_id=1, source_target_pairs={{0,2},{1,3},{2,0},{3,1},{4,6},{5,7},{6,4},{7,5},{8,10},{9,11},{10,... | collective-permute-start | bytes 1658888 | tf_op jit(solution)/shard_map/ppermute | solution.py:529
  234.5 24.0 %collective-permute-start.23 = (bf16[72,2304]{1,0:T(8,128)(2,1)S(1)}, bf16[72,2304]{1,0:T(8,128)(2,1)S(1)}, u32[]{:S(2)}, u32[]{:S(2)}) collective-permute-start(bf16[72,2304]{1,0:T(8,128)(2,1)S(1)} %get-tuple-element.173), channel_id=1, source_target_pairs={{0,4},{1,5},{2,6},{3,7},{4,0},{5,1},{6,2},{7,3},{8,12},{9,13},{10,... | collective-permute-start | bytes 995336 | tf_op jit(solution)/shard_map/ppermute | solution.py:529
  236.9 5.1 %collective-permute-start.19 = (bf16[2,144,384]{2,1,0:T(8,128)(2,1)S(1)}, bf16[2,144,384]{2,1,0:T(8,128)(2,1)S(1)}, u32[]{:S(2)}, u32[]{:S(2)}) collective-permute-start(bf16[2,144,384]{2,1,0:T(8,128)(2,1)S(1)} %get-tuple-element.164), channel_id=1, source_target_pairs={{0,8},{8,0},{16,24},{24,16},{1,9},{9,1},{17,25},{25,17},{2,10},{10... | collective-permute-start | bytes 663560 | tf_op jit(solution)/shard_map/ppermute | solution.py:529
  257.9 7.1 %collective-permute-start.20 = (bf16[2,72,960]{2,1,0:T(8,128)(2,1)S(1)}, bf16[2,72,960]{2,1,0:T(8,128)(2,1)S(1)}, u32[]{:S(2)}, u32[]{:S(2)}) collective-permute-start(bf16[2,72,960]{2,1,0:T(8,128)(2,1)S(1)} %get-tuple-element.169), channel_id=1, source_target_pairs={{0,2},{1,3},{2,0},{3,1},{4,6},{5,7},{6,4},{7,5},{8,10},{9,11},{10,... | collective-permute-start | bytes 829448 | tf_op jit(solution)/shard_map/ppermute | solution.py:529
  257.9 7.1 %collective-permute-start.21 = (bf16[1,144,960]{2,1,0:T(8,128)(2,1)S(1)}, bf16[1,144,960]{2,1,0:T(8,128)(2,1)S(1)}, u32[]{:S(2)}, u32[]{:S(2)}) collective-permute-start(bf16[1,144,960]{2,1,0:T(8,128)(2,1)S(1)} %get-tuple-element.170), channel_id=1, source_target_pairs={{0,8},{8,0},{16,24},{24,16},{1,9},{9,1},{17,25},{25,17},{2,10},{10... | collective-permute-start | bytes 829448 | tf_op jit(solution)/shard_map/ppermute | solution.py:529
  258.3 3.6 %collective-permute-start.22 = (bf16[1,144,384]{2,1,0:T(8,128)(2,1)S(1)}, bf16[1,144,384]{2,1,0:T(8,128)(2,1)S(1)}, u32[]{:S(2)}, u32[]{:S(2)}) collective-permute-start(bf16[1,144,384]{2,1,0:T(8,128)(2,1)S(1)} %get-tuple-element.171), channel_id=1, source_target_pairs={{0,16},{8,24},{16,0},{24,8},{1,17},{9,25},{17,1},{25,9},{2,18},{10... | collective-permute-start | bytes 331784 | tf_op jit(solution)/shard_map/ppermute | solution.py:529
  259.3 11.8 %collective-permute-start.27 = (bf16[36,2304]{1,0:T(8,128)(2,1)S(1)}, bf16[36,2304]{1,0:T(8,128)(2,1)S(1)}, u32[]{:S(2)}, u32[]{:S(2)}) collective-permute-start(bf16[36,2304]{1,0:T(8,128)(2,1)S(1)} %get-tuple-element.181), channel_id=1, source_target_pairs={{0,1},{1,0},{2,3},{3,2},{4,5},{5,4},{6,7},{7,6},{8,9},{9,8},{10,11... | collective-permute-start | bytes 497672 | tf_op jit(solution)/shard_map/ppermute | solution.py:529
  266.1 14.5 %collective-permute-start.24 = (bf16[36,2304]{1,0:T(8,128)(2,1)S(1)}, bf16[36,2304]{1,0:T(8,128)(2,1)S(1)}, u32[]{:S(2)}, u32[]{:S(2)}) collective-permute-start(bf16[36,2304]{1,0:T(8,128)(2,1)S(1)} %get-tuple-element.177), channel_id=1, source_target_pairs={{0,4},{1,5},{2,6},{3,7},{4,0},{5,1},{6,2},{7,3},{8,12},{9,13},{10,... | collective-permute-start | bytes 497672 | tf_op jit(solution)/shard_map/ppermute | solution.py:529
  266.2 14.4 %collective-permute-start.25 = (bf16[36,2304]{1,0:T(8,128)(2,1)S(1)}, bf16[36,2304]{1,0:T(8,128)(2,1)S(1)}, u32[]{:S(2)}, u32[]{:S(2)}) collective-permute-start(bf16[36,2304]{1,0:T(8,128)(2,1)S(1)} %get-tuple-element.178), channel_id=1, source_target_pairs={{0,1},{1,0},{2,3},{3,2},{4,5},{5,4},{6,7},{7,6},{8,9},{9,8},{10,11... | collective-permute-start | bytes 497672 | tf_op jit(solution)/shard_map/ppermute | solution.py:529
  270.2 15.0 %collective-permute-start.26 = (bf16[36,2304]{1,0:T(8,128)(2,1)S(1)}, bf16[36,2304]{1,0:T(8,128)(2,1)S(1)}, u32[]{:S(2)}, u32[]{:S(2)}) collective-permute-start(bf16[36,2304]{1,0:T(8,128)(2,1)S(1)} %get-tuple-element.179), channel_id=1, source_target_pairs={{0,5},{1,4},{2,7},{3,6},{4,1},{5,0},{6,3},{7,2},{8,13},{9,12},{10,... | collective-permute-start | bytes 497672 | tf_op jit(solution)/shard_map/ppermute | solution.py:529
  (11 other events, 9.9 us)

commit v6 on v5

--- a/solution.py
+++ b/solution.py
@@ -28,7 +28,7 @@
 
 ROOM = {
     "split": 56, "space_forward": 56, "time": 56, "weights": 56, "space_backward": 56,
-    "grad_input": 56, "stage": 24, "last_stage": 16, "core_stage": 16, "assemble": 16, "join": 56,
+    "grad_input": 56, "early_stage": 60, "stage": 24, "last_stage": 16, "core_stage": 16, "assemble": 16, "join": 56,
 }
 SPACES = {"v": pltpu.VMEM, "s": pltpu.SMEM, "a": pl.ANY}
 
@@ -545,7 +545,7 @@
         ends = [0, (tiles - tiles // 6) * 64, (tiles - tiles // 6) * 128] if late else [0, width]
         self.cuts = tuple(zip(ends, ends[1:] + [2 * width]))
         self.parts = len(self.orders)
-        self.place, self.width = place, width
+        self.place, self.width, self.late = place, width, late
         self.columns = max(stop - start for start, stop in self.cuts)
         self.bits = dp_bits[::-1] + seq_bits[::-1]
         self.step = 0
@@ -572,8 +572,8 @@
     def stage(self, deps=()):
         steps, shapes = self.next_steps()
         *halves, token = call(
-            "stage", 2, functools.partial(stage_kernel, steps), "s" + "v" * (2 * self.parts),
-            shapes, "v" * len(shapes),
+            "stage" if self.late else "early_stage", 2, functools.partial(stage_kernel, steps),
+            "s" + "v" * (2 * self.parts), shapes, "v" * len(shapes),
             [pltpu.VMEM((self.width >> self.step, self.columns), F32)],
         )(self.place, *self.kept, *self.got, deps=deps)
         self.send(halves)

time: 293 us -> 294 us (level)
  Pallas kernels: 158 us -> 162 us
    pallas_call x21, Pallas kernels: 158 us -> 162 us  [run(): pl.pallas_call(with_token, out_shape=(*out_shape, TOKEN), in_specs=[pl.Bl...]
    unnamed x51 -> x41, local copies, waits for them, and re-layouts: 9.62 us -> 7.47 us
  transfers between devices with their start and end apart: 34 -> 34, of which waited for: 12 -> 12; matrix products, arithmetic and copies ran while one was open for 0% -> 0% of each run, Pallas kernels for 53% -> 54%
where the time goes in v6:
time: 294 us; the launch traced here: 288 us
  Pallas kernels  162 us (55%)
  waiting for transfers between devices  61.4 us (21%)
  starting transfers between devices  55 us (19%)
  local copies, waits for them, and re-layouts  7.47 us (3%)
    pallas_call x21, Pallas kernels, run(): pl.pallas_call(with_token, out_shape=(*out_shape, TOKEN), in_specs=[pl.Bl...  162 us
    ppermute x28, waiting for transfers between devices, swap(): return lax.ppermute(x, axis, [(i, i ^ mask) for i in range(size)])  39.5 us
    all_to_all x6, starting transfers between devices, exchange(): lax.all_to_all(pieces, 'seq', split_axis=0, concat_axis=0, tiled=True)  30.9 us
    ppermute x28, starting transfers between devices, swap(): return lax.ppermute(x, axis, [(i, i ^ mask) for i in range(size)])  24.1 us
    all_to_all x6, waiting for transfers between devices, exchange(): lax.all_to_all(pieces, 'seq', split_axis=0, concat_axis=0, tiled=True)  21.9 us
    unnamed x41, local copies, waits for them, and re-layouts  7.47 us
  transfers between devices with their start and end apart: 34, of which 12 were waited for; matrix products, arithmetic and copies ran while one was open for 0% of the time, Pallas kernels for 54%

profile of v6, /device:TPU:1, one launch (start us, length us, event | category | flops | bytes accessed | tf_op | source)
XLA Modules:
  0.0 288.4 jit_solution(5527851943463924568)
XLA Ops:
  0.6 2.8 split.1
  3.4 6.5 %all-to-all-start = ((bf16[8,40,1152]{2,1,0:T(8,128)(2,1)}), bf16[8,40,1152]{2,1,0:T(8,128)(2,1)S(1)}, u32[]{:S(2)}, u32[]{:S(2)}) async-start(bf16[8,40,1152]{2,1,0:T(8,128)(2,1)} %get-tuple-element.99), calls=%async_computation | async-start | bytes 1474560 | tf_op jit(solution)/shard_map/all_to_all | solution.py:664
  10.5 11.8 %space_forward.2 = (bf16[8,40,1152]{2,1,0:T(8,128)(2,1)}, bf16[288,3456]{1,0:T(8,128)(2,1)}, bf16[288,2304]{1,0:T(8,128)(2,1)}, bf16[16,144,288]{2,1,0:T(8,128)(2,1)}, f32[8,128]{1,0:T(8,128)}) custom-call(bf16[2,288,1152]{2,1,0:T(8,128)(2,1)} %bitcast.9, bf16[2,288,1152]{2,1,0:T(8,128)(2,1)} %bitcast.7, f32[2,6,1152]{2,1,0:T(8,128)} %copy.25.refs_2_.refs_3_, ...), custom_call_target="tpu_custom_call" | custom-call | flops 14000000000 | bytes 14000000 | tf_op jit(solution)/shard_map/space_forward/pallas_call | solution.py:44
  23.1 5.9 %all-to-all-done.refs_8_.refs_2_.refs_12_ = bf16[8,40,1152]{2,1,0:T(8,128)(2,1)S(1)} async-done(((bf16[8,40,1152]{2,1,0:T(8,128)(2,1)}), bf16[8,40,1152]{2,1,0:T(8,128)(2,1)S(1)}, u32[]{:S(2)}, u32[]{:S(2)}) %all-to-all-start) | async-done | bytes 737312 | tf_op jit(solution)/shard_map/all_to_all | solution.py:664
  29.0 4.6 %all-to-all-start.2 = ((bf16[8,40,1152]{2,1,0:T(8,128)(2,1)}), bf16[8,40,1152]{2,1,0:T(8,128)(2,1)S(1)}, u32[]{:S(2)}, u32[]{:S(2)}) async-start(bf16[8,40,1152]{2,1,0:T(8,128)(2,1)} %get-tuple-element.101), calls=%async_computation.2 | async-start | bytes 1474560 | tf_op jit(solution)/shard_map/all_to_all | solution.py:664
  33.5 13.4 %space_forward.3 = (bf16[8,72,1152]{2,1,0:T(8,128)(2,1)}, bf16[288,3456]{1,0:T(8,128)(2,1)}, bf16[288,2304]{1,0:T(8,128)(2,1)}, bf16[16,144,288]{2,1,0:T(8,128)(2,1)}, f32[8,128]{1,0:T(8,128)}) custom-call(bf16[2,288,1152]{2,1,0:T(8,128)(2,1)} %bitcast.10, bf16[2,288,1152]{2,1,0:T(8,128)(2,1)} %bitcast.8, f32[2,6,1152]{2,1,0:T(8,128)} %copy.25.refs_2_.refs_3_, ...), custom_call_target="tpu_custom_call" | custom-call | flops 14000000000 | bytes 14000000 | tf_op jit(solution)/shard_map/space_forward/pallas_call | solution.py:44
  46.9 5.6 %all-to-all-done.2.refs_1_ = bf16[8,40,1152]{2,1,0:T(8,128)(2,1)S(1)} async-done(((bf16[8,40,1152]{2,1,0:T(8,128)(2,1)}), bf16[8,40,1152]{2,1,0:T(8,128)(2,1)S(1)}, u32[]{:S(2)}, u32[]{:S(2)}) %all-to-all-start.2) | async-done | bytes 737312 | tf_op jit(solution)/shard_map/all_to_all | solution.py:664
  53.4 4.6 %all-to-all-start.1 = ((bf16[8,72,1152]{2,1,0:T(8,128)(2,1)}), bf16[8,72,1152]{2,1,0:T(8,128)(2,1)S(1)}, u32[]{:S(2)}, u32[]{:S(2)}) async-start(bf16[8,72,1152]{2,1,0:T(8,128)(2,1)} %get-tuple-element.100), calls=%async_computation.1 | async-start | bytes 2654208 | tf_op jit(solution)/shard_map/all_to_all | solution.py:664
  58.1 20.7 %time.2 = (bf16[8,40,1152]{2,1,0:T(8,128)(2,1)}, bf16[8,72,1152]{2,1,0:T(8,128)(2,1)}, bf16[288,2304]{1,0:T(8,128)(2,1)}, bf16[288,2304]{1,0:T(8,128)(2,1)}, bf1...) custom-call(s32[2]{0:T(128)} %pad_add_fusion.refs_0_.refs_10_, bf16[8,40,1152]{2,1,0:T(8,128)(2,1)} %copy-done.15, ...), custom_call_target="tpu_custom_call" | custom-call | flops 24999999488 | bytes 25000000 | tf_op jit(solution)/shard_map/time/pallas_call | solution.py:44
  79.4 10.3 %all-to-all-done.1.refs_1_.refs_2_ = bf16[8,72,1152]{2,1,0:T(8,128)(2,1)S(1)} async-done(((bf16[8,72,1152]{2,1,0:T(8,128)(2,1)}), bf16[8,72,1152]{2,1,0:T(8,128)(2,1)S(1)}, u32[]{:S(2)}, u32[]{:S(2)}) %all-to-all-start.1) | async-done | bytes 1327136 | tf_op jit(solution)/shard_map/all_to_all | solution.py:664
  89.7 4.8 %all-to-all-start.4 = ((bf16[8,40,1152]{2,1,0:T(8,128)(2,1)}), bf16[8,40,1152]{2,1,0:T(8,128)(2,1)S(1)}, u32[]{:S(2)}, u32[]{:S(2)}) async-start(bf16[8,40,1152]{2,1,0:T(8,128)(2,1)} %get-tuple-element.106), calls=%async_computation.4 | async-start | bytes 1474560 | tf_op jit(solution)/shard_map/all_to_all | solution.py:664
  94.6 21.5 %time.3 = (bf16[8,40,1152]{2,1,0:T(8,128)(2,1)}, bf16[8,72,1152]{2,1,0:T(8,128)(2,1)}, bf16[288,2304]{1,0:T(8,128)(2,1)}, bf16[288,2304]{1,0:T(8,128)(2,1)}, bf1...) custom-call(s32[2]{0:T(128)} %pad_add_fusion.refs_0_.refs_10_, bf16[8,72,1152]{2,1,0:T(8,128)(2,1)} %copy-done.11, ...), custom_call_target="tpu_custom_call" | custom-call | flops 24999999488 | bytes 25000000 | tf_op jit(solution)/shard_map/time/pallas_call | solution.py:44
  116.7 5.3 %all-to-all-start.5 = ((bf16[8,40,1152]{2,1,0:T(8,128)(2,1)}), bf16[8,40,1152]{2,1,0:T(8,128)(2,1)S(1)}, u32[]{:S(2)}, u32[]{:S(2)}) async-start(bf16[8,40,1152]{2,1,0:T(8,128)(2,1)} %get-tuple-element.124), calls=%async_computation.5 | async-start | bytes 1474560 | tf_op jit(solution)/shard_map/all_to_all | solution.py:664
  122.0 11.4 %space_backward.2 = (bf16[288,1152]{1,0:T(8,128)(2,1)}, bf16[288,2304]{1,0:T(8,128)(2,1)}, bf16[288,4608]{1,0:T(8,128)(2,1)}, f32[8,128]{1,0:T(8,128)}) custom-call(s32[2]{0:T(128)} %pad_add_fusion.refs_0_.refs_10_, bf16[8,40,1152]{2,1,0:T(8,128)(2,1)} %copy-done.14, f32[2,6,1152]{2,1,0:T(8,128)} %copy.25.refs_2_.refs_3_, bf16[1152,1152]{1,0:T(8,128)(2,1)} %refs_3_.11, ...), custom_call_target="tpu_custom_call" | custom-call | flops 15000000512 | bytes 15000000 | tf_op jit(solution)/shard_map/space_backward/pallas_call | solution.py:44
  133.6 1.0 copy-done.18
  134.6 15.0 %weights.2 = (bf16[2,288,1152]{2,1,0:T(8,128)(2,1)}, bf16[2,288,1152]{2,1,0:T(8,128)(2,1)}, bf16[1,576,1152]{2,1,0:T(8,128)(2,1)}, bf16[1,576,1152]{2,1,0:T(8,128)(2,1)}, f32[8,128]{1,0:T(8,128)}) custom-call(s32[2]{0:T(128)} %pad_add_fusion.refs_0_.refs_10_, bf16[288,2304]{1,0:T(8,128)(2,1)} %get-tuple-element.113.refs_1_, ...), custom_call_target="tpu_custom_call" | custom-call | flops 10000000000 | bytes 10000000 | tf_op jit(solution)/shard_map/weights/pallas_call | solution.py:44
  149.7 1.3 collective-permute-start.5
  150.9 1.2 collective-permute-start.6
  152.2 0.9 copy-done.12
  153.1 11.5 %space_backward.3 = (bf16[288,1152]{1,0:T(8,128)(2,1)}, bf16[288,2304]{1,0:T(8,128)(2,1)}, bf16[288,4608]{1,0:T(8,128)(2,1)}, f32[8,128]{1,0:T(8,128)}) custom-call(s32[2]{0:T(128)} %pad_add_fusion.refs_0_.refs_10_, bf16[8,40,1152]{2,1,0:T(8,128)(2,1)} %copy-done.12, f32[2,6,1152]{2,1,0:T(8,128)} %copy.25.refs_2_.refs_3_, bf16[1152,1152]{1,0:T(8,128)(2,1)} %refs_3_.11, ...), custom_call_target="tpu_custom_call" | custom-call | flops 15000000512 | bytes 15000000 | tf_op jit(solution)/shard_map/space_backward/pallas_call | solution.py:44
  164.6 1.1 collective-permute-start.11
  165.7 5.1 %all-to-all-start.3 = ((bf16[8,72,1152]{2,1,0:T(8,128)(2,1)}), bf16[8,72,1152]{2,1,0:T(8,128)(2,1)}, u32[]{:S(2)}, u32[]{:S(2)}) async-start(bf16[8,72,1152]{2,1,0:T(8,128)(2,1)} %get-tuple-element.105), calls=%async_computation.3 | async-start | bytes 2654208 | tf_op jit(solution)/shard_map/all_to_all | solution.py:664
  170.7 9.5 %collective-permute-done.5.refs_3_ = bf16[2,288,1152]{2,1,0:T(8,128)(2,1)} collective-permute-done((bf16[2,288,1152]{2,1,0:T(8,128)(2,1)}, bf16[2,288,1152]{2,1,0:T(8,128)(2,1)}, u32[]{:S(2)}, u32[]{:S(2)}) %collective-permute-start.5) | collective-permute-done | bytes 1327136 | tf_op jit(solution)/shard_map/ppermute | solution.py:529
  181.1 4.5 %early_stage.2 = (bf16[1,288,1152]{2,1,0:T(8,128)(2,1)}, bf16[1,288,1152]{2,1,0:T(8,128)(2,1)}, bf16[1,288,1152]{2,1,0:T(8,128)(2,1)}, bf16[1,288,1152]{2,1,0:T(8,128)(2,1)}, f32[8,128]{1,0:T(8,128)}) custom-call(s32[2]{0:T(128)} %pad_add_fusion.refs_0_.refs_10_, bf16[2,288,1152]{2,1,0:T(8,128)(2,1)} %get-tuple-element.120.refs_1_, ...), custom_call_target="tpu_custom_call" | custom-call | flops 2000000000 | bytes 2000000 | tf_op jit(solution)/shard_map/early_stage/pallas_call | solution.py:44
  185.7 1.2 collective-permute-start.8
  187.3 1.0 copy-done.17
  188.8 14.7 %weights.3 = (bf16[2,288,960]{2,1,0:T(8,128)(2,1)}, bf16[2,288,960]{2,1,0:T(8,128)(2,1)}, bf16[1,576,960]{2,1,0:T(8,128)(2,1)}, bf16[1,576,960]{2,1,0:T(8,128)(2...) custom-call(s32[2]{0:T(128)} %pad_add_fusion.refs_0_.refs_10_, ...), custom_call_target="tpu_custom_call" | custom-call | flops 10000000000 | bytes 10000000 | tf_op jit(solution)/shard_map/weights/pallas_call | solution.py:44
  203.5 1.2 collective-permute-start.12
  205.0 2.1 collective-permute-start.14
  207.1 3.0 %early_stage.3 = (bf16[2,72,1152]{2,1,0:T(8,128)(2,1)}, bf16[2,72,1152]{2,1,0:T(8,128)(2,1)}, bf16[2,72,1152]{2,1,0:T(8,128)(2,1)}, bf16[2,72,1152]{2,1,0:T(8,128)(2,1)}, f32[8,128]{1,0:T(8,128)}) custom-call(s32[2]{0:T(128)} %pad_add_fusion.refs_0_.refs_10_, bf16[1,288,1152]{2,1,0:T(8,128)(2,1)} %get-tuple-element.130.refs_1_, ...), custom_call_target="tpu_custom_call" | custom-call | flops 2000000000 | bytes 2000000 | tf_op jit(solution)/shard_map/early_stage/pallas_call | solution.py:44
  210.1 1.5 collective-permute-start.16
  211.5 9.5 %grad_input.2 = (bf16[288,1152]{1,0:T(8,128)(2,1)}, f32[8,128]{1,0:T(8,128)}) custom-call(bf16[288,4608]{1,0:T(8,128)(2,1)} %get-tuple-element.111.refs_5_.refs_0_, bf16[288,1152]{1,0:T(8,128)(2,1)} %get-tuple-element.112.refs_1_, bf16[2,288,1152]{2,1,0:T(8,128)(2,1)} %bitcast.11, f32[2,6,1152]{2,1,0:T(8,128)} %copy.25.refs_2_.refs_3_, ...), custom_call_target="tpu_custom_call" | custom-call | flops 8000000000 | bytes 8000000 | tf_op jit(solution)/shard_map/grad_input/pallas_call | solution.py:44
  221.1 9.3 %grad_input.3 = (bf16[288,1152]{1,0:T(8,128)(2,1)}, f32[8,128]{1,0:T(8,128)}) custom-call(bf16[288,4608]{1,0:T(8,128)(2,1)} %get-tuple-element.134.refs_6_.refs_0_, bf16[288,1152]{1,0:T(8,128)(2,1)} %get-tuple-element.141.refs_1_, bf16[2,288,1152]{2,1,0:T(8,128)(2,1)} %bitcast.12, f32[2,6,1152]{2,1,0:T(8,128)} %copy.25.refs_2_.refs_3_, ...), custom_call_target="tpu_custom_call" | custom-call | flops 8000000000 | bytes 8000000 | tf_op jit(solution)/shard_map/grad_input/pallas_call | solution.py:44
  233.0 2.1 stage.2
  235.1 1.3 collective-permute-start.17
  236.8 2.1 collective-permute-start.23
  239.2 4.7 %join.1 = (bf16[2,288,1152]{2,1,0:T(8,128)(2,1)}, bf16[2,288,1152]{2,1,0:T(8,128)(2,1)}, f32[8,128]{1,0:T(8,128)}) custom-call(bf16[8,72,1152]{2,1,0:T(8,128)(2,1)} %all-to-all-done.3.refs_6_.refs_0_, bf16[576,576]{1,0:T(8,128)(2,1)} %constant.30.clone.refs_1_, bf16[288,1152]{1,0:T(8,128)(2,1)} %get-tuple-element.140.refs_2_, ...), custom_call_target="tpu_custom_call" | custom-call | flops 4000000000 | bytes 4000000 | tf_op jit(solution)/shard_map/join/pallas_call | solution.py:44
  244.0 2.8 collective-permute-done.17.refs_4_
  246.8 10.7 %collective-permute-done.18.refs_5_ = bf16[4,72,960]{2,1,0:T(8,128)(2,1)S(1)} collective-permute-done((bf16[4,72,960]{2,1,0:T(8,128)(2,1)S(1)}, bf16[4,72,960]{2,1,0:T(8,128)(2,1)S(1)}, u32[]{:S(2)}, u32[]{:S(2)}) %collective-permute-start.18) | collective-permute-done | bytes 552992 | tf_op jit(solution)/shard_map/ppermute | solution.py:529
  258.2 1.3 stage.3
  260.8 2.5 collective-permute-start.27
  263.5 2.8 collective-permute-done.20.refs_4_
  266.3 1.1 last_stage.3
  268.2 4.0 %collective-permute-start.25 = (bf16[36,2304]{1,0:T(8,128)(2,1)S(1)}, bf16[36,2304]{1,0:T(8,128)(2,1)S(1)}, u32[]{:S(2)}, u32[]{:S(2)}) collective-permute-start(bf16[36,2304]{1,0:T(8,128)(2,1)S(1)} %get-tuple-element.178), channel_id=1, source_target_pairs={{0,1},{1,0},{2,3},{3,2},{4,5},{5,4},{6,7},{7,6},{8,9},{9,8},{10,11... | collective-permute-start | bytes 497672 | tf_op jit(solution)/shard_map/ppermute | solution.py:529
  272.7 1.3 assemble.2
  274.1 7.6 %collective-permute-done.24.refs_2_ = bf16[36,2304]{1,0:T(8,128)(2,1)S(1)} collective-permute-done((bf16[36,2304]{1,0:T(8,128)(2,1)S(1)}, bf16[36,2304]{1,0:T(8,128)(2,1)S(1)}, u32[]{:S(2)}, u32[]{:S(2)}) %collective-permute-start.24) | collective-permute-done | bytes 165920 | tf_op jit(solution)/shard_map/ppermute | solution.py:529
  281.7 4.9 %collective-permute-done.26.refs_4_ = bf16[36,2304]{1,0:T(8,128)(2,1)S(1)} collective-permute-done((bf16[36,2304]{1,0:T(8,128)(2,1)S(1)}, bf16[36,2304]{1,0:T(8,128)(2,1)S(1)}, u32[]{:S(2)}, u32[]{:S(2)}) %collective-permute-start.26) | collective-permute-done | bytes 165920 | tf_op jit(solution)/shard_map/ppermute | solution.py:529
  286.6 1.4 assemble.3
  (83 shorter events, 12.4 us)
Async XLA Ops:
  3.4 6.5 %copy-start.16 = (f32[2,6,1152]{2,0,1:T(2,128)S(1)}, f32[2,6,1152]{2,0,1:T(2,128)}, u32[]{:S(2)}) copy-start(f32[2,6,1152]{2,0,1:T(2,128)} %param.19) | copy-start | bytes 165892
  3.4 25.6 %all-to-all-start = ((bf16[8,40,1152]{2,1,0:T(8,128)(2,1)}), bf16[8,40,1152]{2,1,0:T(8,128)(2,1)S(1)}, u32[]{:S(2)}, u32[]{:S(2)}) async-start(bf16[8,40,1152]{2,1,0:T(8,128)(2,1)} %get-tuple-element.99), calls=%async_computation | async-start | bytes 1474560 | tf_op jit(solution)/shard_map/all_to_all | solution.py:664
  22.3 93.9 %collective-permute-start = (bf16[288,2304]{1,0:T(8,128)(2,1)}, bf16[288,2304]{1,0:T(8,128)(2,1)}, u32[]{:S(2)}, u32[]{:S(2)}) collective-permute-start(bf16[288,2304]{1,0:T(8,128)(2,1)} %get-tuple-element.110.refs_1_), channel_id=1, source_target_pairs={{0,1},{1,0},{2,3},{3,2},{4,5},{5,4},{6,7},{7,6},{8,9},{9,8},{10,11... | collective-permute-start | bytes 3981320 | tf_op jit(solution)/shard_map/ppermute | solution.py:529
  29.0 4.6 %copy-start.13 = (bf16[8,40,1152]{2,1,0:T(8,128)(2,1)}, bf16[8,40,1152]{2,1,0:T(8,128)(2,1)S(1)}, u32[]{:S(2)}) copy-start(bf16[8,40,1152]{2,1,0:T(8,128)(2,1)S(1)} %all-to-all-done.refs_8_.refs_2_.refs_12_) | copy-start | bytes 2211844
  29.0 23.6 %all-to-all-start.2 = ((bf16[8,40,1152]{2,1,0:T(8,128)(2,1)}), bf16[8,40,1152]{2,1,0:T(8,128)(2,1)S(1)}, u32[]{:S(2)}, u32[]{:S(2)}) async-start(bf16[8,40,1152]{2,1,0:T(8,128)(2,1)} %get-tuple-element.101), calls=%async_computation.2 | async-start | bytes 1474560 | tf_op jit(solution)/shard_map/all_to_all | solution.py:664
  53.4 36.3 %all-to-all-start.1 = ((bf16[8,72,1152]{2,1,0:T(8,128)(2,1)}), bf16[8,72,1152]{2,1,0:T(8,128)(2,1)S(1)}, u32[]{:S(2)}, u32[]{:S(2)}) async-start(bf16[8,72,1152]{2,1,0:T(8,128)(2,1)} %get-tuple-element.100), calls=%async_computation.1 | async-start | bytes 2654208 | tf_op jit(solution)/shard_map/all_to_all | solution.py:664
  78.8 54.7 %collective-permute-start.1 = (bf16[288,2304]{1,0:T(8,128)(2,1)}, bf16[288,2304]{1,0:T(8,128)(2,1)}, u32[]{:S(2)}, u32[]{:S(2)}) collective-permute-start(bf16[288,2304]{1,0:T(8,128)(2,1)} %get-tuple-element.113.refs_1_), channel_id=1, source_target_pairs={{0,1},{1,0},{2,3},{3,2},{4,5},{5,4},{6,7},{7,6},{8,9},{9,8},{10,11... | collective-permute-start | bytes 3981320 | tf_op jit(solution)/shard_map/ppermute | solution.py:529
  78.9 54.7 %collective-permute-start.3 = (bf16[288,2304]{1,0:T(8,128)(2,1)}, bf16[288,2304]{1,0:T(8,128)(2,1)}, u32[]{:S(2)}, u32[]{:S(2)}) collective-permute-start(bf16[288,2304]{1,0:T(8,128)(2,1)} %get-tuple-element.117), channel_id=1, source_target_pairs={{0,1},{1,0},{2,3},{3,2},{4,5},{5,4},{6,7},{7,6},{8,9},{9,8},{10,11... | collective-permute-start | bytes 3981320 | tf_op jit(solution)/shard_map/ppermute | solution.py:529
  79.3 72.8 %collective-permute-start.7 = (bf16[288,2304]{1,0:T(8,128)(2,1)}, bf16[288,2304]{1,0:T(8,128)(2,1)}, u32[]{:S(2)}, u32[]{:S(2)}) collective-permute-start(bf16[288,2304]{1,0:T(8,128)(2,1)} %get-tuple-element.128.refs_2_), channel_id=1, source_target_pairs={{0,1},{1,0},{2,3},{3,2},{4,5},{5,4},{6,7},{7,6},{8,9},{9,8},{10,11... | collective-permute-start | bytes 3981320 | tf_op jit(solution)/shard_map/ppermute | solution.py:529
  89.7 4.8 %copy-start.11 = (bf16[8,72,1152]{2,1,0:T(8,128)(2,1)}, bf16[8,72,1152]{2,1,0:T(8,128)(2,1)S(1)}, u32[]{:S(2)}) copy-start(bf16[8,72,1152]{2,1,0:T(8,128)(2,1)S(1)} %all-to-all-done.1.refs_1_.refs_2_) | copy-start | bytes 3981316
  89.7 27.0 %all-to-all-start.4 = ((bf16[8,40,1152]{2,1,0:T(8,128)(2,1)}), bf16[8,40,1152]{2,1,0:T(8,128)(2,1)S(1)}, u32[]{:S(2)}, u32[]{:S(2)}) async-start(bf16[8,40,1152]{2,1,0:T(8,128)(2,1)} %get-tuple-element.106), calls=%async_computation.4 | async-start | bytes 1474560 | tf_op jit(solution)/shard_map/all_to_all | solution.py:664
  116.1 17.5 %collective-permute-start.2 = (bf16[288,2304]{1,0:T(8,128)(2,1)}, bf16[288,2304]{1,0:T(8,128)(2,1)S(1)}, u32[]{:S(2)}, u32[]{:S(2)}) collective-permute-start(bf16[288,2304]{1,0:T(8,128)(2,1)} %get-tuple-element.114.refs_2_), channel_id=1, source_target_pairs={{0,1},{1,0},{2,3},{3,2},{4,5},{5,4},{6,7},{7,6},{8,9},{9,8},{10,11... | collective-permute-start | bytes 3981320 | tf_op jit(solution)/shard_map/ppermute | solution.py:529
  116.2 17.3 %collective-permute-start.4 = (bf16[288,2304]{1,0:T(8,128)(2,1)}, bf16[288,2304]{1,0:T(8,128)(2,1)}, u32[]{:S(2)}, u32[]{:S(2)}) collective-permute-start(bf16[288,2304]{1,0:T(8,128)(2,1)} %get-tuple-element.118), channel_id=1, source_target_pairs={{0,1},{1,0},{2,3},{3,2},{4,5},{5,4},{6,7},{7,6},{8,9},{9,8},{10,11... | collective-permute-start | bytes 3981320 | tf_op jit(solution)/shard_map/ppermute | solution.py:529
  116.7 5.3 %copy-start.14 = (bf16[8,40,1152]{2,1,0:T(8,128)(2,1)}, bf16[8,40,1152]{2,1,0:T(8,128)(2,1)S(1)}, u32[]{:S(2)}) copy-start(bf16[8,40,1152]{2,1,0:T(8,128)(2,1)S(1)} %all-to-all-done.4.refs_1_) | copy-start | bytes 2211844
  116.7 35.5 %all-to-all-start.5 = ((bf16[8,40,1152]{2,1,0:T(8,128)(2,1)}), bf16[8,40,1152]{2,1,0:T(8,128)(2,1)S(1)}, u32[]{:S(2)}, u32[]{:S(2)}) async-start(bf16[8,40,1152]{2,1,0:T(8,128)(2,1)} %get-tuple-element.124), calls=%async_computation.5 | async-start | bytes 1474560 | tf_op jit(solution)/shard_map/all_to_all | solution.py:664
  133.5 53.8 %collective-permute-start.10 = (bf16[288,2304]{1,0:T(8,128)(2,1)}, bf16[288,2304]{1,0:T(8,128)(2,1)S(1)}, u32[]{:S(2)}, u32[]{:S(2)}) collective-permute-start(bf16[288,2304]{1,0:T(8,128)(2,1)} %get-tuple-element.135), channel_id=1, source_target_pairs={{0,1},{1,0},{2,3},{3,2},{4,5},{5,4},{6,7},{7,6},{8,9},{9,8},{10,11... | collective-permute-start | bytes 3981320 | tf_op jit(solution)/shard_map/ppermute | solution.py:529
  149.7 30.6 %collective-permute-start.5 = (bf16[2,288,1152]{2,1,0:T(8,128)(2,1)}, bf16[2,288,1152]{2,1,0:T(8,128)(2,1)}, u32[]{:S(2)}, u32[]{:S(2)}) collective-permute-start(bf16[2,288,1152]{2,1,0:T(8,128)(2,1)} %get-tuple-element.122), channel_id=1, source_target_pairs={{0,8},{8,0},{16,24},{24,16},{1,9},{9,1},{17,25},{25,17},{2,10},{10... | collective-permute-start | bytes 3981320 | tf_op jit(solution)/shard_map/ppermute | solution.py:529
  150.9 30.2 %collective-permute-start.6 = (bf16[1,576,1152]{2,1,0:T(8,128)(2,1)}, bf16[1,576,1152]{2,1,0:T(8,128)(2,1)}, u32[]{:S(2)}, u32[]{:S(2)}) collective-permute-start(bf16[1,576,1152]{2,1,0:T(8,128)(2,1)} %get-tuple-element.123), channel_id=1, source_target_pairs={{0,16},{8,24},{16,0},{24,8},{1,17},{9,25},{17,1},{25,9},{2,18},{10... | collective-permute-start | bytes 3981320 | tf_op jit(solution)/shard_map/ppermute | solution.py:529
  164.6 22.7 %collective-permute-start.11 = (bf16[288,2304]{1,0:T(8,128)(2,1)}, bf16[288,2304]{1,0:T(8,128)(2,1)S(1)}, u32[]{:S(2)}, u32[]{:S(2)}) collective-permute-start(bf16[288,2304]{1,0:T(8,128)(2,1)} %get-tuple-element.136), channel_id=1, source_target_pairs={{0,1},{1,0},{2,3},{3,2},{4,5},{5,4},{6,7},{7,6},{8,9},{9,8},{10,11... | collective-permute-start | bytes 3981320 | tf_op jit(solution)/shard_map/ppermute | solution.py:529
  165.7 55.4 %all-to-all-start.3 = ((bf16[8,72,1152]{2,1,0:T(8,128)(2,1)}), bf16[8,72,1152]{2,1,0:T(8,128)(2,1)}, u32[]{:S(2)}, u32[]{:S(2)}) async-start(bf16[8,72,1152]{2,1,0:T(8,128)(2,1)} %get-tuple-element.105), calls=%async_computation.3 | async-start | bytes 2654208 | tf_op jit(solution)/shard_map/all_to_all | solution.py:664
  185.7 21.4 %collective-permute-start.8 = (bf16[1,288,1152]{2,1,0:T(8,128)(2,1)}, bf16[1,288,1152]{2,1,0:T(8,128)(2,1)}, u32[]{:S(2)}, u32[]{:S(2)}) collective-permute-start(bf16[1,288,1152]{2,1,0:T(8,128)(2,1)} %get-tuple-element.132), channel_id=1, source_target_pairs={{0,16},{8,24},{16,0},{24,8},{1,17},{9,25},{17,1},{25,9},{2,18},{10... | collective-permute-start | bytes 1990664 | tf_op jit(solution)/shard_map/ppermute | solution.py:529
  186.9 20.2 %collective-permute-start.9 = (bf16[1,288,1152]{2,1,0:T(8,128)(2,1)}, bf16[1,288,1152]{2,1,0:T(8,128)(2,1)}, u32[]{:S(2)}, u32[]{:S(2)}) collective-permute-start(bf16[1,288,1152]{2,1,0:T(8,128)(2,1)} %get-tuple-element.133), channel_id=1, source_target_pairs={{0,8},{8,0},{16,24},{24,16},{1,9},{9,1},{17,25},{25,17},{2,10},{10... | collective-permute-start | bytes 1990664 | tf_op jit(solution)/shard_map/ppermute | solution.py:529
  187.2 1.6 copy-start.19
  203.5 28.4 %collective-permute-start.12 = (bf16[2,288,960]{2,1,0:T(8,128)(2,1)}, bf16[2,288,960]{2,1,0:T(8,128)(2,1)S(1)}, u32[]{:S(2)}, u32[]{:S(2)}) collective-permute-start(bf16[2,288,960]{2,1,0:T(8,128)(2,1)} %get-tuple-element.147), channel_id=1, source_target_pairs={{0,8},{8,0},{16,24},{24,16},{1,9},{9,1},{17,25},{25,17},{2,10},{10... | collective-permute-start | bytes 3317768 | tf_op jit(solution)/shard_map/ppermute | solution.py:529
  204.8 27.2 %collective-permute-start.13 = (bf16[1,576,960]{2,1,0:T(8,128)(2,1)}, bf16[1,576,960]{2,1,0:T(8,128)(2,1)S(1)}, u32[]{:S(2)}, u32[]{:S(2)}) collective-permute-start(bf16[1,576,960]{2,1,0:T(8,128)(2,1)} %get-tuple-element.148), channel_id=1, source_target_pairs={{0,16},{8,24},{16,0},{24,8},{1,17},{9,25},{17,1},{25,9},{2,18},{10... | collective-permute-start | bytes 3317768 | tf_op jit(solution)/shard_map/ppermute | solution.py:529
  205.0 26.9 %collective-permute-start.14 = (bf16[8,72,384]{2,1,0:T(8,128)(2,1)}, bf16[8,72,384]{2,1,0:T(8,128)(2,1)S(1)}, u32[]{:S(2)}, u32[]{:S(2)}) collective-permute-start(bf16[8,72,384]{2,1,0:T(8,128)(2,1)} %get-tuple-element.149), channel_id=1, source_target_pairs={{0,2},{1,3},{2,0},{3,1},{4,6},{5,7},{6,4},{7,5},{8,10},{9,11},{10,... | collective-permute-start | bytes 1327112 | tf_op jit(solution)/shard_map/ppermute | solution.py:529
  210.1 20.3 %collective-permute-start.15 = (bf16[2,72,1152]{2,1,0:T(8,128)(2,1)}, bf16[2,72,1152]{2,1,0:T(8,128)(2,1)S(1)}, u32[]{:S(2)}, u32[]{:S(2)}) collective-permute-start(bf16[2,72,1152]{2,1,0:T(8,128)(2,1)} %get-tuple-element.152), channel_id=1, source_target_pairs={{0,2},{1,3},{2,0},{3,1},{4,6},{5,7},{6,4},{7,5},{8,10},{9,11},{10,... | collective-permute-start | bytes 995336 | tf_op jit(solution)/shard_map/ppermute | solution.py:529
  210.1 20.3 %collective-permute-start.16 = (bf16[2,72,1152]{2,1,0:T(8,128)(2,1)}, bf16[2,72,1152]{2,1,0:T(8,128)(2,1)S(1)}, u32[]{:S(2)}, u32[]{:S(2)}) collective-permute-start(bf16[2,72,1152]{2,1,0:T(8,128)(2,1)} %get-tuple-element.153), channel_id=1, source_target_pairs={{0,2},{1,3},{2,0},{3,1},{4,6},{5,7},{6,4},{7,5},{8,10},{9,11},{10,... | collective-permute-start | bytes 995336 | tf_op jit(solution)/shard_map/ppermute | solution.py:529
  221.1 9.3 %copy-start = (s32[2]{0:T(128)S(1)}, s32[2]{0:T(128)}, u32[]{:S(2)}) copy-start(s32[2]{0:T(128)} %pad_add_fusion.refs_0_.refs_10_) | copy-start | bytes 28
  221.1 9.3 %copy-start.6 = (bf16[2,72,1152]{2,1,0:T(8,128)(2,1)S(1)}, bf16[2,72,1152]{2,1,0:T(8,128)(2,1)}, u32[]{:S(2)}) copy-start(bf16[2,72,1152]{2,1,0:T(8,128)(2,1)} %get-tuple-element.150.refs_1_) | copy-start | bytes 995332
  221.1 9.3 %copy-start.7 = (bf16[2,72,1152]{2,1,0:T(8,128)(2,1)S(1)}, bf16[2,72,1152]{2,1,0:T(8,128)(2,1)}, u32[]{:S(2)}) copy-start(bf16[2,72,1152]{2,1,0:T(8,128)(2,1)} %get-tuple-element.151.refs_2_) | copy-start | bytes 995332
  231.1 1.3 copy-start.1
  231.1 1.6 copy-start.2
  231.1 1.8 copy-start.3
  231.9 3.2 %copy-start.4 = (bf16[72,2304]{1,0:T(8,128)(2,1)}, bf16[72,2304]{1,0:T(8,128)(2,1)S(1)}, u32[]{:S(2)}) copy-start(bf16[72,2304]{1,0:T(8,128)(2,1)S(1)} %get-tuple-element.172.refs_1_) | copy-start | bytes 995332
  235.1 4.1 %copy-start.8 = (f32[8,128]{1,0:T(8,128)}, f32[8,128]{1,0:T(8,128)S(1)}, u32[]{:S(2)}) copy-start(f32[8,128]{1,0:T(8,128)S(1)} %get-tuple-element.156.refs_4_) | copy-start | bytes 12292
  235.1 11.7 %collective-permute-start.17 = (bf16[1,288,960]{2,1,0:T(8,128)(2,1)S(1)}, bf16[1,288,960]{2,1,0:T(8,128)(2,1)S(1)}, u32[]{:S(2)}, u32[]{:S(2)}) collective-permute-start(bf16[1,288,960]{2,1,0:T(8,128)(2,1)S(1)} %get-tuple-element.162), channel_id=1, source_target_pairs={{0,16},{8,24},{16,0},{24,8},{1,17},{9,25},{17,1},{25,9},{2,18},{10... | collective-permute-start | bytes 1658888 | tf_op jit(solution)/shard_map/ppermute | solution.py:529
  236.4 21.0 %collective-permute-start.18 = (bf16[4,72,960]{2,1,0:T(8,128)(2,1)S(1)}, bf16[4,72,960]{2,1,0:T(8,128)(2,1)S(1)}, u32[]{:S(2)}, u32[]{:S(2)}) collective-permute-start(bf16[4,72,960]{2,1,0:T(8,128)(2,1)S(1)} %get-tuple-element.163), channel_id=1, source_target_pairs={{0,2},{1,3},{2,0},{3,1},{4,6},{5,7},{6,4},{7,5},{8,10},{9,11},{10,... | collective-permute-start | bytes 1658888 | tf_op jit(solution)/shard_map/ppermute | solution.py:529
  236.8 23.3 %collective-permute-start.23 = (bf16[72,2304]{1,0:T(8,128)(2,1)S(1)}, bf16[72,2304]{1,0:T(8,128)(2,1)S(1)}, u32[]{:S(2)}, u32[]{:S(2)}) collective-permute-start(bf16[72,2304]{1,0:T(8,128)(2,1)S(1)} %get-tuple-element.173), channel_id=1, source_target_pairs={{0,4},{1,5},{2,6},{3,7},{4,0},{5,1},{6,2},{7,3},{8,12},{9,13},{10,... | collective-permute-start | bytes 995336 | tf_op jit(solution)/shard_map/ppermute | solution.py:529
  238.9 5.1 %collective-permute-start.19 = (bf16[2,144,384]{2,1,0:T(8,128)(2,1)S(1)}, bf16[2,144,384]{2,1,0:T(8,128)(2,1)S(1)}, u32[]{:S(2)}, u32[]{:S(2)}) collective-permute-start(bf16[2,144,384]{2,1,0:T(8,128)(2,1)S(1)} %get-tuple-element.164), channel_id=1, source_target_pairs={{0,8},{8,0},{16,24},{24,16},{1,9},{9,1},{17,25},{25,17},{2,10},{10... | collective-permute-start | bytes 663560 | tf_op jit(solution)/shard_map/ppermute | solution.py:529
  258.2 1.9 copy-start.5
  259.5 6.8 %collective-permute-start.20 = (bf16[2,72,960]{2,1,0:T(8,128)(2,1)S(1)}, bf16[2,72,960]{2,1,0:T(8,128)(2,1)S(1)}, u32[]{:S(2)}, u32[]{:S(2)}) collective-permute-start(bf16[2,72,960]{2,1,0:T(8,128)(2,1)S(1)} %get-tuple-element.169), channel_id=1, source_target_pairs={{0,2},{1,3},{2,0},{3,1},{4,6},{5,7},{6,4},{7,5},{8,10},{9,11},{10,... | collective-permute-start | bytes 829448 | tf_op jit(solution)/shard_map/ppermute | solution.py:529
  259.6 6.8 %collective-permute-start.21 = (bf16[1,144,960]{2,1,0:T(8,128)(2,1)S(1)}, bf16[1,144,960]{2,1,0:T(8,128)(2,1)S(1)}, u32[]{:S(2)}, u32[]{:S(2)}) collective-permute-start(bf16[1,144,960]{2,1,0:T(8,128)(2,1)S(1)} %get-tuple-element.170), channel_id=1, source_target_pairs={{0,8},{8,0},{16,24},{24,16},{1,9},{9,1},{17,25},{25,17},{2,10},{10... | collective-permute-start | bytes 829448 | tf_op jit(solution)/shard_map/ppermute | solution.py:529
  259.9 3.6 %collective-permute-start.22 = (bf16[1,144,384]{2,1,0:T(8,128)(2,1)S(1)}, bf16[1,144,384]{2,1,0:T(8,128)(2,1)S(1)}, u32[]{:S(2)}, u32[]{:S(2)}) collective-permute-start(bf16[1,144,384]{2,1,0:T(8,128)(2,1)S(1)} %get-tuple-element.171), channel_id=1, source_target_pairs={{0,16},{8,24},{16,0},{24,8},{1,17},{9,25},{17,1},{25,9},{2,18},{10... | collective-permute-start | bytes 331784 | tf_op jit(solution)/shard_map/ppermute | solution.py:529
  260.8 11.9 %collective-permute-start.27 = (bf16[36,2304]{1,0:T(8,128)(2,1)S(1)}, bf16[36,2304]{1,0:T(8,128)(2,1)S(1)}, u32[]{:S(2)}, u32[]{:S(2)}) collective-permute-start(bf16[36,2304]{1,0:T(8,128)(2,1)S(1)} %get-tuple-element.181), channel_id=1, source_target_pairs={{0,1},{1,0},{2,3},{3,2},{4,5},{5,4},{6,7},{7,6},{8,9},{9,8},{10,11... | collective-permute-start | bytes 497672 | tf_op jit(solution)/shard_map/ppermute | solution.py:529
  267.4 14.2 %collective-permute-start.24 = (bf16[36,2304]{1,0:T(8,128)(2,1)S(1)}, bf16[36,2304]{1,0:T(8,128)(2,1)S(1)}, u32[]{:S(2)}, u32[]{:S(2)}) collective-permute-start(bf16[36,2304]{1,0:T(8,128)(2,1)S(1)} %get-tuple-element.177), channel_id=1, source_target_pairs={{0,4},{1,5},{2,6},{3,7},{4,0},{5,1},{6,2},{7,3},{8,12},{9,13},{10,... | collective-permute-start | bytes 497672 | tf_op jit(solution)/shard_map/ppermute | solution.py:529
  268.2 13.4 %collective-permute-start.25 = (bf16[36,2304]{1,0:T(8,128)(2,1)S(1)}, bf16[36,2304]{1,0:T(8,128)(2,1)S(1)}, u32[]{:S(2)}, u32[]{:S(2)}) collective-permute-start(bf16[36,2304]{1,0:T(8,128)(2,1)S(1)} %get-tuple-element.178), channel_id=1, source_target_pairs={{0,1},{1,0},{2,3},{3,2},{4,5},{5,4},{6,7},{7,6},{8,9},{9,8},{10,11... | collective-permute-start | bytes 497672 | tf_op jit(solution)/shard_map/ppermute | solution.py:529
  272.2 14.4 %collective-permute-start.26 = (bf16[36,2304]{1,0:T(8,128)(2,1)S(1)}, bf16[36,2304]{1,0:T(8,128)(2,1)S(1)}, u32[]{:S(2)}, u32[]{:S(2)}) collective-permute-start(bf16[36,2304]{1,0:T(8,128)(2,1)S(1)} %get-tuple-element.179), channel_id=1, source_target_pairs={{0,5},{1,4},{2,7},{3,6},{4,1},{5,0},{6,3},{7,2},{8,13},{9,12},{10,... | collective-permute-start | bytes 497672 | tf_op jit(solution)/shard_map/ppermute | solution.py:529
  (6 other events, 5.3 us)
